TPU v7x, 1024 devices: a whole 8x8x8 slice. The times are simulated.
1024 devices in a mesh: group: 64 (over y, z), local: 16 (over x, core).
Axes of the slice: x: 8, y: 8, z: 8, core: 2. Of those that a mesh axis runs over, the one named last changes fastest.
Arguments:
- tokens: bfloat16 [8192, 3584], P(('group', 'local')), may hold values from -6 to 6
- node_picks: int32 [8192, 4], P(('group', 'local')), may hold values from 0 to 63, as said below
- gates: bfloat16 [8192, 4, 2], P(('group', 'local')), may hold values from 0.099609375 to 1
- gate_up: bfloat16 [64, 3584, 4096], P('group', None, 'local'), may hold values from -0.09375 to 0.09375
- down_weight: bfloat16 [64, 2048, 3584], P('group', None, 'local'), may hold values from -0.1875 to 0.1875
Outputs:
- mixed: bfloat16 [8192, 3584], P(('group', 'local'))
Inputs may be any that keep to these rules, and one draw needn't show every extreme that they name: `node_picks`: each token names 4 different nodes. On every device, no node is named more than 1 times by that device's tokens, and some node exactly 1 times. Over the devices that share one index along local, every node is named exactly 4 * 8 times.
All inputs are finite; a program needn't handle non-finite values.
Results may differ from a plain program's by a relative error of at most 0.0058.
Values may be sent and summed in bfloat16 or wider, within the bound.
No kernel may reach another device: no remote copies, remote signals or barrier semaphores. Data moves between devices by JAX's collectives and lax.ppermute only.
A program may use at most 32 MiB of HBM per device.

v0:
```python
import jax
import jax.numpy as jnp
from jax import lax
from jax.sharding import PartitionSpec as P

EXPERTS_PER_NODE = 2


def shards(tokens, node_picks, gates, gate_up, down_weight):
    groups = lax.axis_size("group")
    members = lax.axis_size("local")
    tok_count, row_width = tokens.shape
    visits = node_picks.shape[1]
    capacity = (tok_count * visits + groups - 1) // groups
    slots_all = groups * capacity
    received = tok_count * visits
    flat_nodes = node_picks.reshape(-1)
    node_hot = (flat_nodes[:, None] == jnp.arange(groups, dtype=jnp.int32)[None, :]).astype(
        jnp.int32
    )
    before = jnp.cumsum(node_hot, axis=0) - node_hot
    rank_of = jnp.sum(before * node_hot, axis=1)
    slot_of = flat_nodes * capacity + rank_of
    placing = (slot_of[None, :] == jnp.arange(slots_all, dtype=jnp.int32)[:, None]).astype(
        jnp.bfloat16
    )
    owner_of = (
        jnp.arange(received, dtype=jnp.int32)[:, None] // visits
        == jnp.arange(tok_count, dtype=jnp.int32)[None, :]
    ).astype(jnp.bfloat16)
    place_tok = jnp.dot(placing, owner_of, preferred_element_type=jnp.float32).astype(jnp.bfloat16)
    send_rows = jnp.dot(place_tok, tokens, preferred_element_type=jnp.float32).astype(jnp.bfloat16)
    send_gates = jnp.dot(
        placing, gates.reshape(received, gates.shape[2]), preferred_element_type=jnp.float32
    ).astype(jnp.bfloat16)
    send_rows = send_rows.reshape(groups, capacity, row_width)
    send_gates = send_gates.reshape(groups, capacity, gates.shape[2])
    in_rows, in_gates = (
        lax.all_to_all(send_rows, "group", split_axis=0, concat_axis=0, tiled=True),
        lax.all_to_all(send_gates, "group", split_axis=0, concat_axis=0, tiled=True),
    )
    in_rows = in_rows.reshape(slots_all, row_width)
    in_gates = in_gates.reshape(slots_all, gates.shape[2])
    is_live = (in_gates[:, 0] > 0).astype(jnp.int32)
    position = jnp.cumsum(is_live) - 1
    gather_sel = (
        (position[None, :] == jnp.arange(received, dtype=jnp.int32)[:, None])
        & (is_live[None, :] > 0)
    ).astype(jnp.bfloat16)
    node_rows = jnp.dot(gather_sel, in_rows, preferred_element_type=jnp.float32).astype(
        jnp.bfloat16
    )
    row_gates = jnp.dot(gather_sel, in_gates, preferred_element_type=jnp.float32).astype(
        jnp.bfloat16
    )
    expert_selection = (
        jnp.arange(gates.shape[2], dtype=jnp.int32)
        == lax.axis_index("local") // (members // EXPERTS_PER_NODE)
    ).astype(jnp.float32)
    weights_local = gate_up[0]
    split_at = weights_local.shape[1] // 2
    slot_ids = jnp.dot(
        gather_sel,
        jnp.arange(slots_all, dtype=jnp.int32).astype(jnp.bfloat16)[:, None],
        preferred_element_type=jnp.float32,
    ).astype(jnp.bfloat16)[:, 0]
    portion = lax.all_gather((node_rows, row_gates, slot_ids), "local", axis=0, tiled=True)
    projected = jnp.dot(portion[0], weights_local, preferred_element_type=jnp.float32)
    weight_of = jnp.sum(portion[1].astype(jnp.float32) * expert_selection[None, :], axis=1)
    hidden = (
        jax.nn.silu(projected[:, :split_at]) * projected[:, split_at:] * weight_of[:, None]
    ).astype(jnp.bfloat16)
    owner_slots = portion[2]
    down_local = down_weight[0]
    output_rows = jnp.dot(
        lax.all_gather(hidden, "local", axis=1, tiled=True),
        down_local,
        preferred_element_type=jnp.float32,
    ).astype(jnp.bfloat16)
    output_rows = output_rows.reshape(members, received, down_local.shape[1])
    owner_slots = owner_slots.reshape(members, received)
    restore_token_order = (
        owner_slots[:, None, :]
        == jnp.arange(slots_all, dtype=jnp.int32).astype(jnp.bfloat16)[None, :, None]
    ).astype(jnp.bfloat16)
    padded = jnp.einsum(
        "qwc,qck->qwk", restore_token_order, output_rows, preferred_element_type=jnp.float32
    ).astype(jnp.bfloat16)
    padded = padded.reshape(members, groups, capacity, down_local.shape[1])
    returned = lax.all_to_all(
        lax.all_to_all(padded, "group", split_axis=1, concat_axis=1, tiled=True),
        "local",
        split_axis=0,
        concat_axis=3,
        tiled=True,
    )
    returned = returned.reshape(slots_all, row_width)
    return jnp.dot(place_tok.T, returned, preferred_element_type=jnp.float32).astype(jnp.bfloat16)


def solution(mesh):
    placed = (
        P(("group", "local"), None),
        P(("group", "local"), None),
        P(("group", "local"), None, None),
        P("group", None, "local"),
        P("group", None, "local"),
    )
    return jax.shard_map(
        shards, mesh=mesh, in_specs=placed, out_specs=P(("group", "local"), None), check_vma=False
    )
```

profile of v0, /device:TPU:1, one launch (start us, length us, event | category | flops | bytes accessed | tf_op | source)
XLA Modules:
  0.0 227.0 jit_solution(11531433808530505906)
XLA Ops:
  6.5 0.0 copy-start
  6.5 0.9 copy.38
  7.4 0.1 reshape.124
  7.5 0.1 fusion.17
  7.6 0.1 reduce_window_sum.18
  7.6 0.2 select_reduce_fusion
  7.8 0.8 copy.39
  8.6 0.1 reshape.125
  8.7 0.1 fusion.4
  8.8 0.7 copy.40
  9.6 24.0 %all-to-all-start = ((bf16[64,1,2]{2,1,0:T(2,128)(2,1)}), bf16[64,1,2]{2,1,0:T(2,128)(2,1)S(1)}, u32[]{:S(2)}, u32[]{:S(2)}) async-start(bf16[64,1,2]{2,1,0:T(2,128)(2,1)} %copy.40), calls=%async_computation | async-start | bytes 65536 | tf_op jit(solution)/shard_map/all_to_all | solution.py:40
  33.6 0.2 convolution_convert_fusion.5
  33.8 1.1 fusion
  35.0 0.6 broadcast.80
  35.6 1.0 reduce.2
  36.5 0.9 reshape.144
  37.4 6.9 %all-to-all-done = bf16[64,1,2]{2,1,0:T(2,128)(2,1)S(1)} async-done(((bf16[64,1,2]{2,1,0:T(2,128)(2,1)}), bf16[64,1,2]{2,1,0:T(2,128)(2,1)S(1)}, u32[]{:S(2)}, u32[]{:S(2)}) %all-to-all-start) | async-done | bytes 288 | tf_op jit(solution)/shard_map/all_to_all | solution.py:40
  44.3 5.2 %all-to-all-start.1 = ((bf16[64,2,1792]{2,1,0:T(2,128)(2,1)}), bf16[64,2,1792]{2,1,0:T(2,128)(2,1)S(1)}, u32[]{:S(2)}, u32[]{:S(2)}) async-start(bf16[64,2,1792]{2,1,0:T(2,128)(2,1)} %reshape.144), calls=%async_computation.1 | async-start | bytes 917504 | tf_op jit(solution)/shard_map/all_to_all | solution.py:39
  49.5 0.0 all-gather.4.cloned.1.call-start
  49.6 0.1 copy.41
  49.7 0.1 copy.42
  49.8 0.1 reduce-window.8
  49.9 0.1 add_reduce_fusion
  50.0 14.5 %all-to-all-done.1 = bf16[64,2,1792]{2,1,0:T(2,128)(2,1)S(1)} async-done(((bf16[64,2,1792]{2,1,0:T(2,128)(2,1)}), bf16[64,2,1792]{2,1,0:T(2,128)(2,1)S(1)}, u32[]{:S(2)}, u32[]{:S(2)}) %all-to-all-start.1) | async-done | bytes 458784 | tf_op jit(solution)/shard_map/all_to_all | solution.py:39
  64.5 0.4 reshape.145
  64.9 0.9 convolution_convert_fusion.1
  65.8 0.0 all-gather.4.cloned.1.call-update
  65.8 0.0 all-gather.6.cloned.1.call-start
  65.9 0.1 fusion.5
  66.0 20.8 %all-gather = bf16[16,32,2]{1,2,0:T(2,128)(2,1)S(1)} all-gather(bf16[1,32,2]{1,2,0:T(2,128)(2,1)S(1)} %fusion.5), channel_id=1, replica_groups=mesh['group'=64,'local'=16] {'local'}, dimensions={0}, use_global_device_ids=true | all-gather | bytes 2176 | tf_op jit(solution)/shard_map/all_gather | solution.py:67
  86.9 0.1 reshape.138
  86.9 0.1 multiply_reduce_fusion
  87.0 0.0 copy-start.1
  87.0 22.5 %all-gather.4.cloned.1.call-done = bf16[512,3584]{1,0:T(8,128)(2,1)} async-done(((bf16[32,3584]{1,0:T(8,128)(2,1)}), bf16[512,3584]{1,0:T(8,128)(2,1)}) %all-gather.4.cloned.1.call-update) | async-done | bytes 3670032 | tf_op jit(solution)/shard_map/all_gather | solution.py:67
  109.5 0.0 copy-done
  109.5 3.1 %fusion.1 = f32[512,256]{1,0:T(8,128)S(1)} fusion(bf16[512,3584]{1,0:T(8,128)(2,1)} %all-gather.4.cloned.1.call-done, bf16[1,3584,256]{2,1,0:T(8,128)(2,1)S(1)} %copy-done), kind=kOutput, calls=%fused_computation.4 | convolution fusion | flops 939524096 | bytes 6029312 | tf_op jit(solution)/shard_map/dot_general | solution.py:68
  112.7 0.8 fusion.11
  113.4 0.0 all-gather.6.cloned.1.call-update
  113.5 1.3 dynamic-slice
  115.4 0.1 fusion.6
  115.5 0.2 dynamic-update-slice
  115.7 23.5 %all-reduce = bf16[512]{0:T(512)(128)(2,1)S(1)} all-reduce(bf16[512]{0:T(512)(128)(2,1)S(1)} %dynamic-update-slice), channel_id=1, replica_groups=mesh['group'=64,'local'=16] {'local'}, use_global_device_ids=true, to_apply=%add | all-reduce | flops 512 | bytes 2048
  139.2 0.1 eq.89
  139.3 20.1 %all-gather.6.cloned.1.call-done = bf16[512,2048]{1,0:T(8,128)(2,1)} async-done(((bf16[512,128]{1,0:T(8,128)(2,1)}), bf16[512,2048]{1,0:T(8,128)(2,1)}) %all-gather.6.cloned.1.call-update) | async-done | bytes 2097168 | tf_op jit(solution)/shard_map/all_gather | solution.py:76
  159.4 0.0 copy-done.1
  159.4 2.4 %convolution_convert_fusion.4 = bf16[512,224]{0,1:T(8,128)(2,1)S(1)} fusion(bf16[512,2048]{1,0:T(8,128)(2,1)} %all-gather.6.cloned.1.call-done, bf16[1,2048,224]{1,2,0:T(8,128)(2,1)S(1)} %copy-done.1), kind=kOutput, calls=%fused_computation.8 | convolution fusion | flops 469876736 | bytes 3244032 | tf_op jit(solution)/shard_map/dot_general | solution.py:75
  161.8 0.1 copy.45
  162.0 0.5 fusion.3
  162.5 0.3 copy.46
  162.8 30.4 %all_to_all.30 = bf16[16,64,1,224]{3,0,2,1:T(8,128)(2,1)S(1)} all-to-all(bf16[16,64,1,224]{3,0,2,1:T(8,128)(2,1)S(1)} %copy.46), channel_id=1, replica_groups=mesh['group'=64,'local'=16] {'group'}, dimensions={1} | all-to-all | bytes 917504 | tf_op jit(solution)/shard_map/all_to_all | solution.py:91
  193.2 0.2 copy.47
  193.3 24.9 %all_to_all.31 = bf16[16,64,1,224]{3,1,2,0:T(8,128)(2,1)S(1)} all-to-all(bf16[16,64,1,224]{3,1,2,0:T(8,128)(2,1)S(1)} %copy.47), channel_id=1, replica_groups=mesh['group'=64,'local'=16] {'local'}, dimensions={0} | all-to-all | bytes 917504 | tf_op jit(solution)/shard_map/all_to_all | solution.py:90
  218.2 0.3 copy.48
  218.5 0.9 reshape.132
  219.4 0.8 convolution_convert_fusion.2
  (7 shorter events, 0.0 us)
Async XLA Ops:
  6.5 103.0 %copy-start = (bf16[1,3584,256]{2,1,0:T(8,128)(2,1)S(1)}, bf16[1,3584,256]{2,1,0:T(8,128)(2,1)}, u32[]{:S(2)}) copy-start(bf16[1,3584,256]{2,1,0:T(8,128)(2,1)} %param.8) | copy-start | bytes 5505028
  9.6 34.7 %all-to-all-start = ((bf16[64,1,2]{2,1,0:T(2,128)(2,1)}), bf16[64,1,2]{2,1,0:T(2,128)(2,1)S(1)}, u32[]{:S(2)}, u32[]{:S(2)}) async-start(bf16[64,1,2]{2,1,0:T(2,128)(2,1)} %copy.40), calls=%async_computation | async-start | bytes 65536 | tf_op jit(solution)/shard_map/all_to_all | solution.py:40
  44.3 20.2 %all-to-all-start.1 = ((bf16[64,2,1792]{2,1,0:T(2,128)(2,1)}), bf16[64,2,1792]{2,1,0:T(2,128)(2,1)S(1)}, u32[]{:S(2)}, u32[]{:S(2)}) async-start(bf16[64,2,1792]{2,1,0:T(2,128)(2,1)} %reshape.144), calls=%async_computation.1 | async-start | bytes 917504 | tf_op jit(solution)/shard_map/all_to_all | solution.py:39
  49.5 60.0 %all-gather.4.cloned.1.call-start = ((), (), s32[]{:S(2)}) async-start(), calls=%async_computation.4 | async-start | bytes 3899392 | tf_op jit(solution)/shard_map/all_gather | solution.py:67
  65.8 93.6 %all-gather.6.cloned.1.call-start = ((), (), s32[]{:S(2)}) async-start(), calls=%async_computation.5 | async-start | bytes 2228224 | tf_op jit(solution)/shard_map/all_gather | solution.py:76
  87.0 72.4 %copy-start.1 = (bf16[1,2048,224]{1,2,0:T(8,128)(2,1)S(1)}, bf16[1,2048,224]{1,2,0:T(8,128)(2,1)}, u32[]{:S(2)}) copy-start(bf16[1,2048,224]{1,2,0:T(8,128)(2,1)} %param.9) | copy-start | bytes 2752516
Sparse Core Ops, SparseCore 0:
  65.9 43.5 all-gather.3
  113.6 45.7 all-gather.5
where the time goes:
time: 228 us; the launch traced here: 227 us
  blocking collectives  99.6 us (44%)
  waiting for transfers between devices  64 us (28%)
  starting transfers between devices  29.2 us (13%)
  between operations  14.2 us (6%)
  matrix products  9.54 us (4%)
  local copies, waits for them, and re-layouts  7.99 us (4%)
  other arithmetic  2.39 us (1%)
    all_to_all x1, blocking collectives, shards(): lax.all_to_all(padded, 'group', split_axis=1, concat_axis=1, tiled=True)  30.4 us
    all_to_all x1, blocking collectives, shards(): lax.all_to_all(lax.all_to_all(padded, 'group', split_axis=1, concat_axis=...  24.9 us
    all_to_all x1, starting transfers between devices, shards(): lax.all_to_all(send_gates, 'group', split_axis=0, concat_axis=0, tiled=True)  24 us
    unnamed x1, blocking collectives  23.5 us
    all_gather x1, waiting for transfers between devices, shards(): lax.all_gather((node_rows, row_gates, slot_ids), 'local', axis=0, tiled=T...  22.5 us
    all_gather x1, blocking collectives, shards(): lax.all_gather((node_rows, row_gates, slot_ids), 'local', axis=0, tiled=T...  20.8 us
    all_gather x1, waiting for transfers between devices, shards(): lax.all_gather(hidden, 'local', axis=1, tiled=True)  20.1 us
    all_to_all x1, waiting for transfers between devices, shards(): lax.all_to_all(send_rows, 'group', split_axis=0, concat_axis=0, tiled=True)  14.5 us
  transfers between devices with their start and end apart: 4, of which 4 were waited for; matrix products, arithmetic and copies ran while one was open for 3% of the time, Pallas kernels for 0%

commit v1 on v0

v1 whole, which is shorter than its diff:
```python
import jax
import jax.numpy as jnp
from jax import lax
from jax.sharding import Mesh
from jax.sharding import PartitionSpec as P

PAD = 128
bf16, f32 = jnp.bfloat16, jnp.float32


def dot(a, b):
    return jnp.dot(a, b, preferred_element_type=f32)


def ring(block, n):
    up = [(i, (i + 1) % n) for i in range(n)]
    down = [(i, (i - 1) % n) for i in range(n)]
    rounds = [[(0, block)]]
    fwd = back = block
    for k in range(1, n // 2):
        fwd = lax.ppermute(fwd, "x", up)
        back = lax.ppermute(back, "x", down)
        rounds.append([(k, fwd), (n - k, back)])
    rounds.append([(n // 2, lax.ppermute(fwd, "x", up))])
    return rounds


def middle(rows, gu, gu_other, dn, dn_other):
    n = lax.axis_size("x")
    x, c = lax.axis_index("x"), lax.axis_index("core")
    r, width = rows.shape[0], rows.shape[1] - PAD
    expert = x // (n // 2)
    half = gu.shape[1] // 2
    hid = jnp.zeros((n, r, 2 * half), bf16)
    for blocks in ring(rows, n):
        got = jnp.concatenate([b for _, b in blocks], axis=0) if len(blocks) > 1 else blocks[0][1]
        tok = got[:, :width]
        gate = jnp.where(expert == 0, got[:, width], got[:, width + 1]).astype(f32)[:, None]
        parts = []
        for w in (gu, gu_other):
            pr = dot(tok, w)
            parts.append((jax.nn.silu(pr[:, :half]) * pr[:, half:] * gate).astype(bf16))
        a, b = parts
        h = jnp.where(c == 0, jnp.concatenate([a, b], 1), jnp.concatenate([b, a], 1))
        for j, (k, _) in enumerate(blocks):
            hid = lax.dynamic_update_slice(
                hid, h[None, j * r : (j + 1) * r], ((x - k) % n, 0, 0)
            )
    hid = hid.reshape(n * r, 2 * half)
    out = out_other = 0.0
    for blocks in ring(hid, n):
        for k, b in blocks:
            at = ((x - k) % n) * (2 * half)
            out += dot(b, lax.dynamic_slice_in_dim(dn, at, 2 * half, 0))
            out_other += dot(b, lax.dynamic_slice_in_dim(dn_other, at, 2 * half, 0))
    feats = dn.shape[1]
    both = jnp.concatenate(
        [out.reshape(n, r, feats), out_other.reshape(n, r, feats)], axis=2
    ).astype(bf16)
    back = lax.all_to_all(both, "x", split_axis=0, concat_axis=0, tiled=True)
    back = back.transpose(1, 0, 2).reshape(r, n, 2, feats)
    back = jnp.where(c == 0, back, back[:, :, ::-1])
    return back.reshape(r, width)


def shards(tokens, node_picks, gates, gate_up, down_weight):
    group = ("y", "z")
    groups = lax.axis_size(group)
    tok_count, width = tokens.shape
    visits = node_picks.shape[1]
    received = tok_count * visits
    gu, dn = gate_up[0], down_weight[0]
    swap = [(0, 1), (1, 0)]
    gu_other = lax.ppermute(gu, "core", swap)
    dn_other = lax.ppermute(dn, "core", swap)
    hot = (node_picks[None, :, :] == jnp.arange(groups, dtype=jnp.int32)[:, None, None]).astype(f32)
    place = jnp.sum(hot, axis=2).astype(bf16)
    send_gates = jnp.sum(hot[..., None] * gates.astype(f32)[None], axis=(1, 2)).astype(bf16)
    send = jnp.concatenate(
        [
            dot(place, tokens).astype(bf16),
            send_gates,
            jnp.zeros((groups, PAD - gates.shape[2]), bf16),
        ],
        axis=1,
    )
    arrived = lax.all_to_all(send[:, None], group, split_axis=0, concat_axis=0, tiled=True)[:, 0]
    live = arrived[:, width] > 0
    ids = jnp.arange(groups, dtype=jnp.int32)
    position = (
        jnp.sum(jnp.where(live[None, :] & (ids[None, :] <= ids[:, None]), 1, 0), axis=1) - 1
    )
    select = (
        (position[None, :] == jnp.arange(received, dtype=jnp.int32)[:, None]) & live[None, :]
    ).astype(bf16)
    rows = dot(select, arrived).astype(bf16)
    visit = middle(rows, gu, gu_other, dn, dn_other)
    padded = dot(select.T, visit).astype(bf16)
    returned = lax.all_to_all(padded[:, None], group, split_axis=0, concat_axis=0, tiled=True)[:, 0]
    return dot(place.T, returned).astype(bf16)


def solution(mesh):
    fine = Mesh(mesh.devices.reshape(8, 8, 8, 2), ("y", "z", "x", "core"))
    group, local = ("y", "z"), ("x", "core")
    every = group + local
    placed = (
        P(every, None),
        P(every, None),
        P(every, None, None),
        P(group, None, local),
        P(group, None, local),
    )
    return jax.shard_map(
        shards, mesh=fine, in_specs=placed, out_specs=P(every, None), check_vma=False
    )
```

time: 228 us -> 182 us (0.80)
  the two profiles are of different devices: /device:TPU:1 before, /device:TPU:32 now
where the time goes in v1:
time: 182 us; the launch traced here: 181 us
  starting transfers between devices  73.5 us (40%)
  blocking collectives  38.9 us (21%)
  waiting for transfers between devices  31.4 us (17%)
  matrix products  24.2 us (13%)
  other arithmetic  6.11 us (3%)
  local copies, waits for them, and re-layouts  5.75 us (3%)
    ppermute x6, starting transfers between devices, ring(): back = lax.ppermute(back, 'x', down)  27.4 us
    dot_general x30, matrix products, dot(): return jnp.dot(a, b, preferred_element_type=f32)  24.2 us
    all_to_all x1, starting transfers between devices, shards(): lax.all_to_all(send[:, None], group, split_axis=0, concat_axis=0, tiled=T...  23.1 us
    all_to_all x1, blocking collectives, shards(): lax.all_to_all(padded[:, None], group, split_axis=0, concat_axis=0, tiled...  19.5 us
    all_to_all x1, blocking collectives, middle(): back = lax.all_to_all(both, 'x', split_axis=0, concat_axis=0, tiled=True)  19.4 us
    ppermute x6, starting transfers between devices, ring(): fwd = lax.ppermute(fwd, 'x', up)  14.7 us
    all_to_all x1, waiting for transfers between devices, shards(): lax.all_to_all(send[:, None], group, split_axis=0, concat_axis=0, tiled=T...  14.1 us
    ppermute x6, waiting for transfers between devices, ring(): fwd = lax.ppermute(fwd, 'x', up)  8.28 us
  transfers between devices with their start and end apart: 17, of which 11 were waited for; matrix products, arithmetic and copies ran while one was open for 13% of the time, Pallas kernels for 0%

profile of v1, /device:TPU:32, one launch (start us, length us, event | category | flops | bytes accessed | tf_op | source)
XLA Modules:
  0.0 180.6 jit_solution(5498012457450183419)
XLA Ops:
  0.0 0.8 fusion.118
  0.8 0.8 fusion.90
  1.5 0.7 convert_element_type.73
  2.4 0.3 convolution_convert_fusion
  2.9 0.5 broadcast.68
  3.4 0.9 reduce.12
  4.3 1.2 reshape.167
  5.5 23.1 %all-to-all-start = ((bf16[64,2,1856]{2,1,0:T(2,128)(2,1)}), bf16[64,2,1856]{2,1,0:T(2,128)(2,1)S(1)}, u32[]{:S(2)}, u32[]{:S(2)}) async-start(bf16[64,2,1856]{2,1,0:T(2,128)(2,1)} %reshape.167), calls=%async_computation | async-start | bytes 983040 | tf_op jit(solution)/shard_map/all_to_all | solution.py:87
  28.6 1.9 %collective-permute-start = (bf16[3584,256]{1,0:T(8,128)(2,1)S(1)}, bf16[3584,256]{1,0:T(8,128)(2,1)}, u32[]{:S(2)}, u32[]{:S(2)}) collective-permute-start(bf16[3584,256]{1,0:T(8,128)(2,1)S(1)} %bitcast.109), channel_id=1, source_target_pairs={{0,1},{1,0},{2,3},{3,2},{4,5},{5,4},{6,7},{7,6},{8,9},{9,8},{10,11... | collective-permute-start | bytes 5505032 | tf_op jit(solution)/shard_map/ppermute | solution.py:74
  30.5 2.4 %collective-permute-start.15 = (bf16[2048,224]{0,1:T(8,128)(2,1)}, bf16[2048,224]{0,1:T(8,128)(2,1)}, u32[]{:S(2)}, u32[]{:S(2)}) collective-permute-start(bf16[2048,224]{0,1:T(8,128)(2,1)} %bitcast.118), channel_id=1, source_target_pairs={{0,1},{1,0},{2,3},{3,2},{4,5},{5,4},{6,7},{7,6},{8,9},{9,8},{10,11... | collective-permute-start | bytes 2752520 | tf_op jit(solution)/shard_map/ppermute | solution.py:75
  33.2 14.1 %all-to-all-done = bf16[64,2,1856]{2,1,0:T(2,128)(2,1)S(1)} async-done(((bf16[64,2,1856]{2,1,0:T(2,128)(2,1)}), bf16[64,2,1856]{2,1,0:T(2,128)(2,1)S(1)}, u32[]{:S(2)}, u32[]{:S(2)}) %all-to-all-start) | async-done | bytes 475168 | tf_op jit(solution)/shard_map/all_to_all | solution.py:87
  47.3 0.8 reshape.168
  48.6 3.4 %collective-permute-start.1 = (bf16[32,3712]{1,0:T(8,128)(2,1)S(1)}, bf16[32,3712]{1,0:T(8,128)(2,1)S(1)}, u32[]{:S(2)}, u32[]{:S(2)}) collective-permute-start(bf16[32,3712]{1,0:T(8,128)(2,1)S(1)} %convolution_convert_fusion.2), channel_id=1, source_target_pairs={{0,2},{2,4},{4,6},{6,8},{8,10},{10,12},{12,14},{14,0},{1,3},{3,5},... | collective-permute-start | bytes 712712 | tf_op jit(solution)/shard_map/ppermute | solution.py:21
  52.0 3.7 %collective-permute-start.2 = (bf16[32,3712]{1,0:T(8,128)(2,1)S(1)}, bf16[32,3712]{1,0:T(8,128)(2,1)S(1)}, u32[]{:S(2)}, u32[]{:S(2)}) collective-permute-start(bf16[32,3712]{1,0:T(8,128)(2,1)S(1)} %convolution_convert_fusion.2), channel_id=1, source_target_pairs={{0,14},{2,0},{4,2},{6,4},{8,6},{10,8},{12,10},{14,12},{1,15},{3,1}... | collective-permute-start | bytes 712712 | tf_op jit(solution)/shard_map/ppermute | solution.py:22
  55.9 0.4 fusion.28
  56.3 1.5 collective-permute-done.1
  57.9 2.2 %collective-permute-done.2 = bf16[32,3712]{1,0:T(8,128)(2,1)S(1)} collective-permute-done((bf16[32,3712]{1,0:T(8,128)(2,1)S(1)}, bf16[32,3712]{1,0:T(8,128)(2,1)S(1)}, u32[]{:S(2)}, u32[]{:S(2)}) %collective-permute-start.2) | collective-permute-done | bytes 237600 | tf_op jit(solution)/shard_map/ppermute | solution.py:22
  60.2 3.4 %collective-permute-start.3 = (bf16[32,3712]{1,0:T(8,128)(2,1)S(1)}, bf16[32,3712]{1,0:T(8,128)(2,1)S(1)}, u32[]{:S(2)}, u32[]{:S(2)}) collective-permute-start(bf16[32,3712]{1,0:T(8,128)(2,1)S(1)} %collective-permute-done.1), channel_id=1, source_target_pairs={{0,2},{2,4},{4,6},{6,8},{8,10},{10,12},{12,14},{14,0},{1,3},{3,5},... | collective-permute-start | bytes 712712 | tf_op jit(solution)/shard_map/ppermute | solution.py:21
  63.7 3.6 %collective-permute-start.4 = (bf16[32,3712]{1,0:T(8,128)(2,1)S(1)}, bf16[32,3712]{1,0:T(8,128)(2,1)S(1)}, u32[]{:S(2)}, u32[]{:S(2)}) collective-permute-start(bf16[32,3712]{1,0:T(8,128)(2,1)S(1)} %collective-permute-done.2), channel_id=1, source_target_pairs={{0,14},{2,0},{4,2},{6,4},{8,6},{10,8},{12,10},{14,12},{1,15},{3,1}... | collective-permute-start | bytes 712712 | tf_op jit(solution)/shard_map/ppermute | solution.py:22
  67.3 0.5 fusion.20
  67.8 1.7 collective-permute-done.3
  69.4 2.2 %collective-permute-start.5 = (bf16[32,3712]{1,0:T(8,128)(2,1)S(1)}, bf16[32,3712]{1,0:T(8,128)(2,1)S(1)}, u32[]{:S(2)}, u32[]{:S(2)}) collective-permute-start(bf16[32,3712]{1,0:T(8,128)(2,1)S(1)} %collective-permute-done.3), channel_id=1, source_target_pairs={{0,2},{2,4},{4,6},{6,8},{8,10},{10,12},{12,14},{14,0},{1,3},{3,5},... | collective-permute-start | bytes 712712 | tf_op jit(solution)/shard_map/ppermute | solution.py:21
  71.8 4.7 %collective-permute-start.6 = (bf16[32,3712]{1,0:T(8,128)(2,1)S(1)}, bf16[32,3712]{1,0:T(8,128)(2,1)S(1)}, u32[]{:S(2)}, u32[]{:S(2)}) collective-permute-start(bf16[32,3712]{1,0:T(8,128)(2,1)S(1)} %collective-permute-done.4), channel_id=1, source_target_pairs={{0,14},{2,0},{4,2},{6,4},{8,6},{10,8},{12,10},{14,12},{1,15},{3,1}... | collective-permute-start | bytes 712712 | tf_op jit(solution)/shard_map/ppermute | solution.py:22
  76.7 0.5 fusion.16
  77.2 1.4 collective-permute-done.5
  78.6 2.0 %collective-permute-start.7 = (bf16[32,3712]{1,0:T(8,128)(2,1)S(1)}, bf16[32,3712]{1,0:T(8,128)(2,1)S(1)}, u32[]{:S(2)}, u32[]{:S(2)}) collective-permute-start(bf16[32,3712]{1,0:T(8,128)(2,1)S(1)} %collective-permute-done.5), channel_id=1, source_target_pairs={{0,2},{2,4},{4,6},{6,8},{8,10},{10,12},{12,14},{14,0},{1,3},{3,5},... | collective-permute-start | bytes 712712 | tf_op jit(solution)/shard_map/ppermute | solution.py:24
  80.7 0.3 collective-permute-done.6
  81.2 0.5 fusion.12
  81.7 1.9 %fusion.26 = f32[32,256]{1,0:T(8,128)S(1)} fusion(bf16[3584,256]{1,0:T(8,128)(2,1)} %collective-permute-done, bf16[32,3712]{1,0:T(8,128)(2,1)S(1)} %convolution_convert_fusion.2), kind=kOutput, calls=%fused_computation.42 | convolution fusion | flops 58720256 | bytes 2097152 | tf_op jit(solution)/shard_map/dot_general | solution.py:12
  83.7 1.9 %fusion.18 = f32[64,256]{1,0:T(8,128)S(1)} fusion(bf16[3584,256]{1,0:T(8,128)(2,1)} %collective-permute-done, bf16[64,3712]{1,0:T(8,128)(2,1)S(1)} %constant_dynamic-update-slice_fusion), kind=kOutput, calls=%fused_computation.33 | convolution fusion | flops 117440512 | bytes 2359296 | tf_op jit(solution)/shard_map/dot_general | solution.py:12
  85.7 1.9 %fusion.14 = f32[64,256]{1,0:T(8,128)S(1)} fusion(bf16[3584,256]{1,0:T(8,128)(2,1)} %collective-permute-done, bf16[64,3712]{1,0:T(8,128)(2,1)S(1)} %constant_dynamic-update-slice_fusion.2), kind=kOutput, calls=%fused_computation.29 | convolution fusion | flops 117440512 | bytes 2359296 | tf_op jit(solution)/shard_map/dot_general | solution.py:12
  87.9 1.9 %fusion.10 = f32[64,256]{1,0:T(8,128)S(1)} fusion(bf16[3584,256]{1,0:T(8,128)(2,1)} %collective-permute-done, bf16[64,3712]{1,0:T(8,128)(2,1)S(1)} %constant_dynamic-update-slice_fusion.4), kind=kOutput, calls=%fused_computation.25 | convolution fusion | flops 117440512 | bytes 2359296 | tf_op jit(solution)/shard_map/dot_general | solution.py:12
  90.0 0.4 fusion.24
  90.6 1.9 %fusion.22 = f32[32,256]{1,0:T(8,128)S(1)} fusion(bf16[3584,256]{1,0:T(8,128)(2,1)} %collective-permute-done, bf16[32,3712]{1,0:T(8,128)(2,1)S(1)} %collective-permute-done.7), kind=kOutput, calls=%fused_computation.38 | convolution fusion | flops 58720256 | bytes 2097152 | tf_op jit(solution)/shard_map/dot_general | solution.py:12
  92.6 4.7 %collective-permute-start.9 = (bf16[256,256]{1,0:T(8,128)(2,1)S(1)}, bf16[256,256]{1,0:T(8,128)(2,1)S(1)}, u32[]{:S(2)}, u32[]{:S(2)}) collective-permute-start(bf16[256,256]{1,0:T(8,128)(2,1)S(1)} %bitcast.113), channel_id=1, source_target_pairs={{0,14},{2,0},{4,2},{6,4},{8,6},{10,8},{12,10},{14,12},{1,15},{3,1}... | collective-permute-start | bytes 393224 | tf_op jit(solution)/shard_map/ppermute | solution.py:22
  97.3 1.9 %collective-permute-start.8 = (bf16[256,256]{1,0:T(8,128)(2,1)S(1)}, bf16[256,256]{1,0:T(8,128)(2,1)S(1)}, u32[]{:S(2)}, u32[]{:S(2)}) collective-permute-start(bf16[256,256]{1,0:T(8,128)(2,1)S(1)} %bitcast.114), channel_id=1, source_target_pairs={{0,2},{2,4},{4,6},{6,8},{8,10},{10,12},{12,14},{14,0},{1,3},{3,5},... | collective-permute-start | bytes 393224 | tf_op jit(solution)/shard_map/ppermute | solution.py:21
  99.5 1.5 collective-permute-done.9
  101.0 5.6 %collective-permute-start.11 = (bf16[256,256]{1,0:T(8,128)(2,1)S(1)}, bf16[256,256]{1,0:T(8,128)(2,1)S(1)}, u32[]{:S(2)}, u32[]{:S(2)}) collective-permute-start(bf16[256,256]{1,0:T(8,128)(2,1)S(1)} %collective-permute-done.9), channel_id=1, source_target_pairs={{0,14},{2,0},{4,2},{6,4},{8,6},{10,8},{12,10},{14,12},{1,15},{3,1}... | collective-permute-start | bytes 393224 | tf_op jit(solution)/shard_map/ppermute | solution.py:22
  106.7 1.9 %collective-permute-start.10 = (bf16[256,256]{1,0:T(8,128)(2,1)S(1)}, bf16[256,256]{1,0:T(8,128)(2,1)S(1)}, u32[]{:S(2)}, u32[]{:S(2)}) collective-permute-start(bf16[256,256]{1,0:T(8,128)(2,1)S(1)} %collective-permute-done.8), channel_id=1, source_target_pairs={{0,2},{2,4},{4,6},{6,8},{8,10},{10,12},{12,14},{14,0},{1,3},{3,5},... | collective-permute-start | bytes 393224 | tf_op jit(solution)/shard_map/ppermute | solution.py:21
  108.7 1.1 fusion.48
  109.8 1.1 fusion.50
  110.9 0.2 convolution_add_fusion.8
  111.1 1.1 fusion.3
  112.5 5.1 %collective-permute-start.13 = (bf16[256,256]{1,0:T(8,128)(2,1)S(1)}, bf16[256,256]{1,0:T(8,128)(2,1)S(1)}, u32[]{:S(2)}, u32[]{:S(2)}) collective-permute-start(bf16[256,256]{1,0:T(8,128)(2,1)S(1)} %collective-permute-done.11), channel_id=1, source_target_pairs={{0,14},{2,0},{4,2},{6,4},{8,6},{10,8},{12,10},{14,12},{1,15},{3,1}... | collective-permute-start | bytes 393224 | tf_op jit(solution)/shard_map/ppermute | solution.py:22
  117.6 1.1 fusion.45
  119.0 1.9 %collective-permute-start.12 = (bf16[256,256]{1,0:T(8,128)(2,1)S(1)}, bf16[256,256]{1,0:T(8,128)(2,1)S(1)}, u32[]{:S(2)}, u32[]{:S(2)}) collective-permute-start(bf16[256,256]{1,0:T(8,128)(2,1)S(1)} %collective-permute-done.10), channel_id=1, source_target_pairs={{0,2},{2,4},{4,6},{6,8},{8,10},{10,12},{12,14},{14,0},{1,3},{3,5},... | collective-permute-start | bytes 393224 | tf_op jit(solution)/shard_map/ppermute | solution.py:21
  120.9 1.1 fusion.2
  122.0 0.2 fusion.5
  122.3 1.1 fusion.42
  123.6 3.4 %collective-permute-done.12 = bf16[256,256]{1,0:T(8,128)(2,1)S(1)} collective-permute-done((bf16[256,256]{1,0:T(8,128)(2,1)S(1)}, bf16[256,256]{1,0:T(8,128)(2,1)S(1)}, u32[]{:S(2)}, u32[]{:S(2)}) %collective-permute-start.12) | collective-permute-done | bytes 131104 | tf_op jit(solution)/shard_map/ppermute | solution.py:21
  127.0 1.9 %collective-permute-start.14 = (bf16[256,256]{1,0:T(8,128)(2,1)S(1)}, bf16[256,256]{1,0:T(8,128)(2,1)S(1)}, u32[]{:S(2)}, u32[]{:S(2)}) collective-permute-start(bf16[256,256]{1,0:T(8,128)(2,1)S(1)} %collective-permute-done.12), channel_id=1, source_target_pairs={{0,2},{2,4},{4,6},{6,8},{8,10},{10,12},{12,14},{14,0},{1,3},{3,5},... | collective-permute-start | bytes 393224 | tf_op jit(solution)/shard_map/ppermute | solution.py:24
  129.0 1.1 fusion.1
  130.1 0.2 fusion.4
  130.3 4.8 %collective-permute-done.14 = bf16[256,256]{1,0:T(8,128)(2,1)S(1)} collective-permute-done((bf16[256,256]{1,0:T(8,128)(2,1)S(1)}, bf16[256,256]{1,0:T(8,128)(2,1)S(1)}, u32[]{:S(2)}, u32[]{:S(2)}) %collective-permute-start.14) | collective-permute-done | bytes 131104 | tf_op jit(solution)/shard_map/ppermute | solution.py:24
  135.1 1.1 fusion.7
  136.8 19.4 %all_to_all.15 = bf16[8,32,448]{2,1,0:T(8,128)(2,1)S(1)} all-to-all(bf16[8,32,448]{2,1,0:T(8,128)(2,1)S(1)} %pad_maximum_fusion), channel_id=1, replica_groups=mesh['y'=8,'z'=8,'x'=8,'core'=2] {'x'}, dimensions={0} | all-to-all | bytes 458752 | tf_op jit(solution)/shard_map/all_to_all | solution.py:60
  156.5 1.4 rev.3
  157.9 0.3 broadcast_select_fusion
  158.2 0.3 reshape.155
  158.6 0.3 fusion
  158.9 0.9 reduce.13
  160.0 19.5 %all_to_all.16 = bf16[64,2,1792]{2,1,0:T(2,128)(2,1)S(1)} all-to-all(bf16[64,2,1792]{2,1,0:T(2,128)(2,1)S(1)} %reshape.169), channel_id=1, replica_groups=mesh['y'=8,'z'=8,'x'=8,'core'=2] {'y','z'}, dimensions={0} | all-to-all | bytes 917504 | tf_op jit(solution)/shard_map/all_to_all | solution.py:99
  179.4 0.4 reshape.170
  179.8 0.8 convolution_convert_fusion.3
  (61 shorter events, 4.5 us)
Async XLA Ops:
  0.0 2.4 %copy-start = (bf16[8,3584]{1,0:T(8,128)(2,1)S(1)}, bf16[8,3584]{1,0:T(8,128)(2,1)}, u32[]{:S(2)}) copy-start(bf16[8,3584]{1,0:T(8,128)(2,1)} %param.5) | copy-start | bytes 172036
  2.8 25.8 %copy-start.1 = (bf16[1,3584,256]{2,1,0:T(8,128)(2,1)S(1)}, bf16[1,3584,256]{2,1,0:T(8,128)(2,1)}, u32[]{:S(2)}) copy-start(bf16[1,3584,256]{2,1,0:T(8,128)(2,1)} %param.8) | copy-start | bytes 5505028
  5.5 41.8 %all-to-all-start = ((bf16[64,2,1856]{2,1,0:T(2,128)(2,1)}), bf16[64,2,1856]{2,1,0:T(2,128)(2,1)S(1)}, u32[]{:S(2)}, u32[]{:S(2)}) async-start(bf16[64,2,1856]{2,1,0:T(2,128)(2,1)} %reshape.167), calls=%async_computation | async-start | bytes 983040 | tf_op jit(solution)/shard_map/all_to_all | solution.py:87
  28.6 53.1 %collective-permute-start = (bf16[3584,256]{1,0:T(8,128)(2,1)S(1)}, bf16[3584,256]{1,0:T(8,128)(2,1)}, u32[]{:S(2)}, u32[]{:S(2)}) collective-permute-start(bf16[3584,256]{1,0:T(8,128)(2,1)S(1)} %bitcast.109), channel_id=1, source_target_pairs={{0,1},{1,0},{2,3},{3,2},{4,5},{5,4},{6,7},{7,6},{8,9},{9,8},{10,11... | collective-permute-start | bytes 5505032 | tf_op jit(solution)/shard_map/ppermute | solution.py:74
  30.5 78.1 %collective-permute-start.15 = (bf16[2048,224]{0,1:T(8,128)(2,1)}, bf16[2048,224]{0,1:T(8,128)(2,1)}, u32[]{:S(2)}, u32[]{:S(2)}) collective-permute-start(bf16[2048,224]{0,1:T(8,128)(2,1)} %bitcast.118), channel_id=1, source_target_pairs={{0,1},{1,0},{2,3},{3,2},{4,5},{5,4},{6,7},{7,6},{8,9},{9,8},{10,11... | collective-permute-start | bytes 2752520 | tf_op jit(solution)/shard_map/ppermute | solution.py:75
  48.6 9.2 %collective-permute-start.1 = (bf16[32,3712]{1,0:T(8,128)(2,1)S(1)}, bf16[32,3712]{1,0:T(8,128)(2,1)S(1)}, u32[]{:S(2)}, u32[]{:S(2)}) collective-permute-start(bf16[32,3712]{1,0:T(8,128)(2,1)S(1)} %convolution_convert_fusion.2), channel_id=1, source_target_pairs={{0,2},{2,4},{4,6},{6,8},{8,10},{10,12},{12,14},{14,0},{1,3},{3,5},... | collective-permute-start | bytes 712712 | tf_op jit(solution)/shard_map/ppermute | solution.py:21
  52.0 8.0 %collective-permute-start.2 = (bf16[32,3712]{1,0:T(8,128)(2,1)S(1)}, bf16[32,3712]{1,0:T(8,128)(2,1)S(1)}, u32[]{:S(2)}, u32[]{:S(2)}) collective-permute-start(bf16[32,3712]{1,0:T(8,128)(2,1)S(1)} %convolution_convert_fusion.2), channel_id=1, source_target_pairs={{0,14},{2,0},{4,2},{6,4},{8,6},{10,8},{12,10},{14,12},{1,15},{3,1}... | collective-permute-start | bytes 712712 | tf_op jit(solution)/shard_map/ppermute | solution.py:22
  60.2 9.2 %collective-permute-start.3 = (bf16[32,3712]{1,0:T(8,128)(2,1)S(1)}, bf16[32,3712]{1,0:T(8,128)(2,1)S(1)}, u32[]{:S(2)}, u32[]{:S(2)}) collective-permute-start(bf16[32,3712]{1,0:T(8,128)(2,1)S(1)} %collective-permute-done.1), channel_id=1, source_target_pairs={{0,2},{2,4},{4,6},{6,8},{8,10},{10,12},{12,14},{14,0},{1,3},{3,5},... | collective-permute-start | bytes 712712 | tf_op jit(solution)/shard_map/ppermute | solution.py:21
  63.7 8.2 %collective-permute-start.4 = (bf16[32,3712]{1,0:T(8,128)(2,1)S(1)}, bf16[32,3712]{1,0:T(8,128)(2,1)S(1)}, u32[]{:S(2)}, u32[]{:S(2)}) collective-permute-start(bf16[32,3712]{1,0:T(8,128)(2,1)S(1)} %collective-permute-done.2), channel_id=1, source_target_pairs={{0,14},{2,0},{4,2},{6,4},{8,6},{10,8},{12,10},{14,12},{1,15},{3,1}... | collective-permute-start | bytes 712712 | tf_op jit(solution)/shard_map/ppermute | solution.py:22
  69.4 9.2 %collective-permute-start.5 = (bf16[32,3712]{1,0:T(8,128)(2,1)S(1)}, bf16[32,3712]{1,0:T(8,128)(2,1)S(1)}, u32[]{:S(2)}, u32[]{:S(2)}) collective-permute-start(bf16[32,3712]{1,0:T(8,128)(2,1)S(1)} %collective-permute-done.3), channel_id=1, source_target_pairs={{0,2},{2,4},{4,6},{6,8},{8,10},{10,12},{12,14},{14,0},{1,3},{3,5},... | collective-permute-start | bytes 712712 | tf_op jit(solution)/shard_map/ppermute | solution.py:21
  71.8 9.2 %collective-permute-start.6 = (bf16[32,3712]{1,0:T(8,128)(2,1)S(1)}, bf16[32,3712]{1,0:T(8,128)(2,1)S(1)}, u32[]{:S(2)}, u32[]{:S(2)}) collective-permute-start(bf16[32,3712]{1,0:T(8,128)(2,1)S(1)} %collective-permute-done.4), channel_id=1, source_target_pairs={{0,14},{2,0},{4,2},{6,4},{8,6},{10,8},{12,10},{14,12},{1,15},{3,1}... | collective-permute-start | bytes 712712 | tf_op jit(solution)/shard_map/ppermute | solution.py:22
  78.6 11.3 %collective-permute-start.7 = (bf16[32,3712]{1,0:T(8,128)(2,1)S(1)}, bf16[32,3712]{1,0:T(8,128)(2,1)S(1)}, u32[]{:S(2)}, u32[]{:S(2)}) collective-permute-start(bf16[32,3712]{1,0:T(8,128)(2,1)S(1)} %collective-permute-done.5), channel_id=1, source_target_pairs={{0,2},{2,4},{4,6},{6,8},{8,10},{10,12},{12,14},{14,0},{1,3},{3,5},... | collective-permute-start | bytes 712712 | tf_op jit(solution)/shard_map/ppermute | solution.py:24
  90.0 9.3 %copy-start.2 = (bf16[1,2048,224]{1,2,0:T(8,128)(2,1)S(1)}, bf16[1,2048,224]{1,2,0:T(8,128)(2,1)}, u32[]{:S(2)}) copy-start(bf16[1,2048,224]{1,2,0:T(8,128)(2,1)} %param.9) | copy-start | bytes 2752516
  92.6 8.4 %collective-permute-start.9 = (bf16[256,256]{1,0:T(8,128)(2,1)S(1)}, bf16[256,256]{1,0:T(8,128)(2,1)S(1)}, u32[]{:S(2)}, u32[]{:S(2)}) collective-permute-start(bf16[256,256]{1,0:T(8,128)(2,1)S(1)} %bitcast.113), channel_id=1, source_target_pairs={{0,14},{2,0},{4,2},{6,4},{8,6},{10,8},{12,10},{14,12},{1,15},{3,1}... | collective-permute-start | bytes 393224 | tf_op jit(solution)/shard_map/ppermute | solution.py:22
  97.3 9.4 %collective-permute-start.8 = (bf16[256,256]{1,0:T(8,128)(2,1)S(1)}, bf16[256,256]{1,0:T(8,128)(2,1)S(1)}, u32[]{:S(2)}, u32[]{:S(2)}) collective-permute-start(bf16[256,256]{1,0:T(8,128)(2,1)S(1)} %bitcast.114), channel_id=1, source_target_pairs={{0,2},{2,4},{4,6},{6,8},{8,10},{10,12},{12,14},{14,0},{1,3},{3,5},... | collective-permute-start | bytes 393224 | tf_op jit(solution)/shard_map/ppermute | solution.py:21
  101.0 11.5 %collective-permute-start.11 = (bf16[256,256]{1,0:T(8,128)(2,1)S(1)}, bf16[256,256]{1,0:T(8,128)(2,1)S(1)}, u32[]{:S(2)}, u32[]{:S(2)}) collective-permute-start(bf16[256,256]{1,0:T(8,128)(2,1)S(1)} %collective-permute-done.9), channel_id=1, source_target_pairs={{0,14},{2,0},{4,2},{6,4},{8,6},{10,8},{12,10},{14,12},{1,15},{3,1}... | collective-permute-start | bytes 393224 | tf_op jit(solution)/shard_map/ppermute | solution.py:22
  106.7 12.2 %collective-permute-start.10 = (bf16[256,256]{1,0:T(8,128)(2,1)S(1)}, bf16[256,256]{1,0:T(8,128)(2,1)S(1)}, u32[]{:S(2)}, u32[]{:S(2)}) collective-permute-start(bf16[256,256]{1,0:T(8,128)(2,1)S(1)} %collective-permute-done.8), channel_id=1, source_target_pairs={{0,2},{2,4},{4,6},{6,8},{8,10},{10,12},{12,14},{14,0},{1,3},{3,5},... | collective-permute-start | bytes 393224 | tf_op jit(solution)/shard_map/ppermute | solution.py:21
  112.5 9.8 %collective-permute-start.13 = (bf16[256,256]{1,0:T(8,128)(2,1)S(1)}, bf16[256,256]{1,0:T(8,128)(2,1)S(1)}, u32[]{:S(2)}, u32[]{:S(2)}) collective-permute-start(bf16[256,256]{1,0:T(8,128)(2,1)S(1)} %collective-permute-done.11), channel_id=1, source_target_pairs={{0,14},{2,0},{4,2},{6,4},{8,6},{10,8},{12,10},{14,12},{1,15},{3,1}... | collective-permute-start | bytes 393224 | tf_op jit(solution)/shard_map/ppermute | solution.py:22
  119.0 8.1 %collective-permute-start.12 = (bf16[256,256]{1,0:T(8,128)(2,1)S(1)}, bf16[256,256]{1,0:T(8,128)(2,1)S(1)}, u32[]{:S(2)}, u32[]{:S(2)}) collective-permute-start(bf16[256,256]{1,0:T(8,128)(2,1)S(1)} %collective-permute-done.10), channel_id=1, source_target_pairs={{0,2},{2,4},{4,6},{6,8},{8,10},{10,12},{12,14},{14,0},{1,3},{3,5},... | collective-permute-start | bytes 393224 | tf_op jit(solution)/shard_map/ppermute | solution.py:21
  127.0 8.1 %collective-permute-start.14 = (bf16[256,256]{1,0:T(8,128)(2,1)S(1)}, bf16[256,256]{1,0:T(8,128)(2,1)S(1)}, u32[]{:S(2)}, u32[]{:S(2)}) collective-permute-start(bf16[256,256]{1,0:T(8,128)(2,1)S(1)} %collective-permute-done.12), channel_id=1, source_target_pairs={{0,2},{2,4},{4,6},{6,8},{8,10},{10,12},{12,14},{14,0},{1,3},{3,5},... | collective-permute-start | bytes 393224 | tf_op jit(solution)/shard_map/ppermute | solution.py:24

commit v2 on v1

v2 whole, which is shorter than its diff:
```python
import jax
import jax.numpy as jnp
from jax import lax
from jax.experimental import pallas as pl
from jax.experimental.pallas import tpu as pltpu
from jax.sharding import Mesh
from jax.sharding import PartitionSpec as P

LANES = 128
bf16, f32, i32 = jnp.bfloat16, jnp.float32, jnp.int32
VMEM = pl.BlockSpec(memory_space=pltpu.VMEM)
SMEM = pl.BlockSpec(memory_space=pltpu.SMEM)
HBM = pl.BlockSpec(memory_space=pltpu.HBM)
CHUNKS = 4


def dot(a, b):
    return jnp.dot(a, b, preferred_element_type=f32)


def dot_dims(a, b, da, db):
    return lax.dot_general(a, b, (((da,), (db,)), ((), ())), preferred_element_type=f32)


def call(kernel, outs, specs, name, scratch=()):
    return pl.pallas_call(
        kernel,
        out_shape=[jax.ShapeDtypeStruct(s, d) for s, d in outs],
        in_specs=specs,
        out_specs=[VMEM] * len(outs),
        scratch_shapes=list(scratch),
        compiler_params=pltpu.CompilerParams(vmem_limit_bytes=20 * 2**20),
        name=name,
    )


def ring(block, n):
    up = [(i, (i + 1) % n) for i in range(n)]
    down = [(i, (i - 1) % n) for i in range(n)]
    got = [(0, block)]
    fwd = back = block
    for k in range(1, n // 2):
        fwd = lax.ppermute(fwd, "x", up)
        back = lax.ppermute(back, "x", down)
        got += [(k, fwd), (n - k, back)]
    got.append((n // 2, lax.ppermute(fwd, "x", up)))
    return got


def pack_kernel(picks_ref, gates_ref, tok_ref, send_ref, place_ref):
    visits, toks = picks_ref.shape
    groups, _, wide = send_ref.shape
    half = wide - LANES
    node = lax.broadcasted_iota(i32, (groups, toks), 0)
    place = jnp.zeros((groups, toks), f32)
    lane = lax.broadcasted_iota(i32, (groups, LANES), 1)
    tail = jnp.zeros((groups, LANES), f32)
    for j in range(visits):
        hot = (node == picks_ref[j : j + 1, :]).astype(f32)
        place += hot
        for e in range(gates_ref.shape[1]):
            gate = jnp.sum(hot * gates_ref[j, e : e + 1, :].astype(f32), axis=1, keepdims=True)
            tail += jnp.where(lane == e, gate, 0.0)
    place = place.astype(bf16)
    place_ref[...] = place
    for h in range(2):
        send_ref[:, h, :half] = dot(place, tok_ref[:, h * half : (h + 1) * half]).astype(bf16)
        send_ref[:, h, half:] = tail.astype(bf16)


def compact_kernel(in_ref, rows_ref, select_ref):
    groups, _, wide = in_ref.shape
    half = wide - LANES
    count = rows_ref.shape[0]
    tail = in_ref[:, 0, half:]
    live = (tail.astype(f32) > 0).astype(bf16)
    low = lax.broadcasted_iota(i32, (groups, groups), 0)
    high = lax.broadcasted_iota(i32, (groups, groups), 1)
    upto = dot((high <= low).astype(bf16), live)[:, :1]
    alive = live[:, :1].astype(f32) > 0
    position = lax.broadcasted_iota(i32, (groups, count), 1).astype(f32) + 1.0
    spread = jnp.where(alive & (upto == position), 1.0, 0.0).astype(bf16)
    select_ref[...] = spread
    for h in range(2):
        rows_ref[:, h * half : (h + 1) * half] = dot_dims(
            spread, in_ref[:, h, :half], 0, 0
        ).astype(bf16)
    rows_ref[:, 2 * half :] = dot_dims(spread, tail, 0, 0).astype(bf16)


def hidden_kernel(steps, at_ref, gu_ref, other_ref, *refs):
    blocks, (out_ref, buf, sems) = refs[:-3], refs[-3:]
    depth = gu_ref.shape[0] // CHUNKS
    copies = []
    for i, w in enumerate((gu_ref, other_ref)):
        for k in range(CHUNKS):
            part = pl.ds(k * depth, depth)
            copies.append(
                pltpu.make_async_copy(w.at[part, :], buf.at[i, part, :], sems.at[i, k])
            )
            copies[-1].start()
    n = len(blocks)
    x, c = at_ref[0], at_ref[1]
    r = blocks[0].shape[0]
    width = gu_ref.shape[0]
    units = gu_ref.shape[1] // 2
    hr = r // 2
    rows = jnp.concatenate([b[:, :width] for b in blocks], axis=0)
    tail = jnp.concatenate([b[:, width:] for b in blocks], axis=0).astype(f32)
    gate = jnp.where(x < n // 2, tail[:, 0:1], tail[:, 1:2])
    parts = []
    for i in range(2):
        pr = 0.0
        for k in range(CHUNKS):
            copies[i * CHUNKS + k].wait()
            lo, hi = k * depth, (k + 1) * depth
            pr += dot(rows[:, lo:hi], buf[i, lo:hi, :])
        g, p = pr[:, :units], pr[:, units:]
        parts.append((g / (1.0 + jnp.exp(-g)) * p * gate).astype(bf16))
    mine, other = parts
    first = jnp.where(c == 0, mine, other)
    second = jnp.where(c == 0, other, mine)
    h = jnp.concatenate([first, second], axis=1)
    for j, k in enumerate(steps):
        owner = lax.rem(x + (n - k), n)
        at = pl.ds(pl.multiple_of(owner * hr, hr), hr)
        for dest in range(n):
            lo = j * r + (dest % 2) * hr
            out_ref[dest, at, :] = h[lo : lo + hr]


def down_kernel(at_ref, h_ref, own_ref, other_ref, pair_ref, both_ref, out_ref, buf, sems):
    copies = [
        pltpu.make_async_copy(w, buf.at[i], sems.at[i])
        for i, w in enumerate((own_ref, other_ref, pair_ref, both_ref))
    ]
    for copy in copies:
        copy.start()
    n, rows, units = h_ref.shape
    b, c = lax.rem(at_ref[0], 2), at_ref[1]
    h = jnp.concatenate([h_ref[k] for k in range(n)], axis=1)
    parts = []
    for i in range(4):
        copies[i].wait()
        parts.append(dot_dims(h, buf[i], 1, 1).astype(bf16))
    hr = out_ref.shape[1]
    for bb in range(2):
        for cc in range(2):

            @pl.when((b == bb) & (c == cc))
            def _():
                order = [parts[2 * (p // 2 != bb) + (p % 2 != cc)] for p in range(4)]
                whole = jnp.concatenate(order, axis=1)
                for k in range(out_ref.shape[0]):
                    out_ref[k] = whole[k * hr : (k + 1) * hr]


def spread_kernel(back_ref, select_ref, out_ref):
    n, hr, feats = back_ref.shape
    rows = [
        jnp.concatenate([back_ref[2 * a], back_ref[2 * a + 1]], axis=0) for a in range(n // 2)
    ]
    whole = jnp.concatenate(rows, axis=1)
    half = out_ref.shape[2]
    for h in range(2):
        out_ref[:, h, :] = dot(select_ref[...], whole[:, h * half : (h + 1) * half]).astype(bf16)


def mix_kernel(in_ref, place_ref, out_ref):
    half = in_ref.shape[2]
    for h in range(2):
        out_ref[:, h * half : (h + 1) * half] = dot_dims(
            place_ref[...], in_ref[:, h, :], 0, 0
        ).astype(bf16)


def shards(tokens, node_picks, gates, gate_up, down_weight):
    group = ("y", "z")
    groups, n = lax.axis_size(group), lax.axis_size("x")
    toks, width = tokens.shape
    visits = node_picks.shape[1]
    r = toks * visits
    half = width // 2
    at = jnp.stack([lax.axis_index("x"), lax.axis_index("core")]).astype(i32)
    gu, dn = gate_up[0], down_weight[0].T
    feats, units = dn.shape[0], dn.shape[1] // n
    swap = [(0, 1), (1, 0)]
    pair = [(i, i ^ 1) for i in range(n)]
    send, place = call(
        pack_kernel,
        [((groups, 2, half + LANES), bf16), ((groups, toks), bf16)],
        [VMEM] * 3,
        "pack",
    )(node_picks.T, gates.transpose(1, 2, 0), tokens)
    dn_pair = lax.ppermute(dn, "x", pair)
    gu_other = lax.ppermute(gu, "core", swap)
    dn_other = lax.ppermute(dn, "core", swap)
    arrived = lax.all_to_all(send, group, split_axis=0, concat_axis=0, tiled=True)
    arrived, dn_pair, gu_other, dn_other = lax.optimization_barrier(
        (arrived, dn_pair, gu_other, dn_other)
    )
    dn_both = lax.ppermute(dn_pair, "core", swap)
    rows, select = call(
        compact_kernel,
        [((r, width + LANES), bf16), ((groups, r), bf16)],
        [VMEM],
        "compact",
    )(arrived)
    got = ring(rows, n)
    steps = tuple(k for k, _ in got)
    (hid,) = call(
        lambda *refs: hidden_kernel(steps, *refs),
        [((n, n * r // 2, units), bf16)],
        [SMEM, HBM, HBM] + [VMEM] * n,
        "hidden",
        [pltpu.VMEM((2,) + gu.shape, bf16), pltpu.SemaphoreType.DMA((2, CHUNKS))],
    )(at, gu, gu_other, *[b for _, b in got])
    hid = lax.all_to_all(hid, "x", split_axis=0, concat_axis=0, tiled=True)
    (out,) = call(
        down_kernel,
        [((n, r // 2, 4 * feats), bf16)],
        [SMEM, VMEM] + [HBM] * 4,
        "down",
        [pltpu.VMEM((4,) + dn.shape, bf16), pltpu.SemaphoreType.DMA((4,))],
    )(at, hid, dn, dn_other, dn_pair, dn_both)
    back = lax.all_to_all(out, "x", split_axis=0, concat_axis=0, tiled=True)
    (padded,) = call(spread_kernel, [((groups, 2, half), bf16)], [VMEM] * 2, "spread")(
        back, select
    )
    returned = lax.all_to_all(padded, group, split_axis=0, concat_axis=0, tiled=True)
    (mixed,) = call(mix_kernel, [((toks, width), bf16)], [VMEM] * 2, "mix")(returned, place)
    return mixed


def solution(mesh):
    fine = Mesh(mesh.devices.reshape(8, 8, 8, 2), ("y", "z", "x", "core"))
    group, local = ("y", "z"), ("x", "core")
    every = group + local
    placed = (
        P(every, None),
        P(every, None),
        P(every, None, None),
        P(group, None, local),
        P(group, None, local),
    )
    return jax.shard_map(
        shards, mesh=fine, in_specs=placed, out_specs=P(every, None), check_vma=False
    )
```

time: 182 us -> 177 us (0.973)
  matrix products: 24.2 us -> 0 us
  Pallas kernels: 0 us -> 15.4 us
  waiting for transfers between devices: 31.4 us -> 46.1 us
  starting transfers between devices: 73.5 us -> 62 us
  local copies, waits for them, and re-layouts: 5.75 us -> 12.3 us
  other arithmetic: 6.11 us -> 0.07 us
    dot_general x30 -> x0, matrix products: 24.2 us -> none  [dot(): return jnp.dot(a, b, preferred_element_type=f32)]
    ppermute x2 -> x3, waiting for transfers between devices: 4.78 us -> 25.2 us  [the longest x1 20.6 us: shards(): dn_pair = lax.ppermute(dn, 'x', pair)]
    pallas_call x0 -> x6, Pallas kernels: none -> 15.4 us  [the longest x1 6.97 us: shards(): call(lambda *refs: hidden_kernel(steps, *refs), [((n, n * r // 2, units),...]
    ppermute x6 -> x3, starting transfers between devices: 27.4 us -> 13.6 us  [ring(): back = lax.ppermute(back, 'x', down)]
    unnamed x14 -> x30, local copies, waits for them, and re-layouts: 2.56 us -> 12.3 us
    ppermute x6 -> x3, starting transfers between devices: 14.7 us -> 7.48 us  [ring(): fwd = lax.ppermute(fwd, 'x', up)]
    all_to_all x1 -> x2, starting transfers between devices: 23.1 us -> 29.8 us  [the longest x1 23.1 us: shards(): lax.all_to_all(send, group, split_axis=0, concat_axis=0, tiled=True)]
    ppermute x6 -> x3, waiting for transfers between devices: 4.16 us -> 0.01 us  [ring(): back = lax.ppermute(back, 'x', down)]
  transfers between devices with their start and end apart: 17 -> 13, of which waited for: 11 -> 6; matrix products, arithmetic and copies ran while one was open for 13% -> 0% of each run, Pallas kernels for 0% -> 5%
where the time goes in v2:
time: 177 us; the launch traced here: 176 us
  starting transfers between devices  62 us (35%)
  waiting for transfers between devices  46.1 us (26%)
  blocking collectives  39.6 us (22%)
  Pallas kernels  15.4 us (9%)
  local copies, waits for them, and re-layouts  12.3 us (7%)
    all_to_all x1, blocking collectives, shards(): lax.all_to_all(padded, group, split_axis=0, concat_axis=0, tiled=True)  27 us
    all_to_all x1, starting transfers between devices, shards(): lax.all_to_all(send, group, split_axis=0, concat_axis=0, tiled=True)  23.1 us
    ppermute x1, waiting for transfers between devices, shards(): dn_pair = lax.ppermute(dn, 'x', pair)  20.6 us
    all_to_all x1, waiting for transfers between devices, shards(): hid = lax.all_to_all(hid, 'x', split_axis=0, concat_axis=0, tiled=True)  14.1 us
    ppermute x3, starting transfers between devices, ring(): back = lax.ppermute(back, 'x', down)  13.6 us
    all_to_all x1, blocking collectives, shards(): back = lax.all_to_all(out, 'x', split_axis=0, concat_axis=0, tiled=True)  12.5 us
    unnamed x30, local copies, waits for them, and re-layouts  12.3 us
    ppermute x3, starting transfers between devices, ring(): fwd = lax.ppermute(fwd, 'x', up)  7.48 us
  transfers between devices with their start and end apart: 13, of which 6 were waited for; matrix products, arithmetic and copies ran while one was open for 0% of the time, Pallas kernels for 5%

profile of v2, /device:TPU:32, one launch (start us, length us, event | category | flops | bytes accessed | tf_op | source)
XLA Modules:
  0.0 175.6 jit_solution(1323442904958009450)
XLA Ops:
  0.0 1.9 %collective-permute-start.1 = (bf16[3584,256]{1,0:T(8,128)(2,1)}, bf16[3584,256]{1,0:T(8,128)(2,1)S(1)}, u32[]{:S(2)}, u32[]{:S(2)}) collective-permute-start(bf16[3584,256]{1,0:T(8,128)(2,1)} %bitcast.8), channel_id=1, source_target_pairs={{0,1},{1,0},{2,3},{3,2},{4,5},{5,4},{6,7},{7,6},{8,9},{9,8},{10,11... | collective-permute-start | bytes 5505032 | tf_op jit(solution)/shard_map/ppermute | solution.py:196
  1.9 0.0 copy-start.12
  1.9 0.8 copy-done.12
  2.7 0.0 copy-start.13
  2.7 0.7 copy-done.13
  3.4 0.0 copy-start.14
  3.4 0.7 copy-done.14
  4.1 1.2 pack.1
  5.3 23.1 %all-to-all-start = ((bf16[64,2,1920]{2,1,0:T(2,128)(2,1)}), bf16[64,2,1920]{2,1,0:T(2,128)(2,1)S(1)}, u32[]{:S(2)}, u32[]{:S(2)}) async-start(bf16[64,2,1920]{2,1,0:T(2,128)(2,1)} %get-tuple-element.13), calls=%async_computation | async-start | bytes 983040 | tf_op jit(solution)/shard_map/all_to_all | solution.py:198
  28.4 1.9 %collective-permute-start.2 = (bf16[224,2048]{1,0:T(8,128)(2,1)}, bf16[224,2048]{1,0:T(8,128)(2,1)S(1)}, u32[]{:S(2)}, u32[]{:S(2)}) collective-permute-start(bf16[224,2048]{1,0:T(8,128)(2,1)} %bitcast.10), channel_id=1, source_target_pairs={{0,1},{1,0},{2,3},{3,2},{4,5},{5,4},{6,7},{7,6},{8,9},{9,8},{10,11... | collective-permute-start | bytes 2752520 | tf_op jit(solution)/shard_map/ppermute | solution.py:197
  30.3 3.4 %collective-permute-start = (bf16[224,2048]{1,0:T(8,128)(2,1)}, bf16[224,2048]{1,0:T(8,128)(2,1)}, u32[]{:S(2)}, u32[]{:S(2)}) collective-permute-start(bf16[224,2048]{1,0:T(8,128)(2,1)} %bitcast.11), channel_id=1, source_target_pairs={{0,2},{2,0},{4,6},{6,4},{8,10},{10,8},{12,14},{14,12},{1,3},{3,1},... | collective-permute-start | bytes 2752520 | tf_op jit(solution)/shard_map/ppermute | solution.py:195
  33.7 0.0 collective-permute-done.2.other_ref
  33.7 0.0 copy-start.2
  33.7 0.9 copy-done.2
  34.7 20.6 %collective-permute-done.pair_ref = bf16[224,2048]{1,0:T(8,128)(2,1)} collective-permute-done((bf16[224,2048]{1,0:T(8,128)(2,1)}, bf16[224,2048]{1,0:T(8,128)(2,1)}, u32[]{:S(2)}, u32[]{:S(2)}) %collective-permute-start) | collective-permute-done | bytes 917536 | tf_op jit(solution)/shard_map/ppermute | solution.py:195
  55.3 0.0 all-to-all-done.in_ref
  55.3 0.0 collective-permute-done.1.refs_2_
  55.3 1.4 compact.1
  56.7 3.4 %collective-permute-start.3 = (bf16[32,3712]{1,0:T(8,128)(2,1)S(1)}, bf16[32,3712]{1,0:T(8,128)(2,1)S(1)}, u32[]{:S(2)}, u32[]{:S(2)}) collective-permute-start(bf16[32,3712]{1,0:T(8,128)(2,1)S(1)} %get-tuple-element.16.refs_3_), channel_id=1, source_target_pairs={{0,2},{2,4},{4,6},{6,8},{8,10},{10,12},{12,14},{14,0},{1,3},{3,5},... | collective-permute-start | bytes 712712 | tf_op jit(solution)/shard_map/ppermute | solution.py:43
  60.1 3.7 %collective-permute-start.4 = (bf16[32,3712]{1,0:T(8,128)(2,1)S(1)}, bf16[32,3712]{1,0:T(8,128)(2,1)S(1)}, u32[]{:S(2)}, u32[]{:S(2)}) collective-permute-start(bf16[32,3712]{1,0:T(8,128)(2,1)S(1)} %get-tuple-element.16.refs_3_), channel_id=1, source_target_pairs={{0,14},{2,0},{4,2},{6,4},{8,6},{10,8},{12,10},{14,12},{1,15},{3,1}... | collective-permute-start | bytes 712712 | tf_op jit(solution)/shard_map/ppermute | solution.py:44
  63.8 3.4 %collective-permute-done.3.refs_4_ = bf16[32,3712]{1,0:T(8,128)(2,1)S(1)} collective-permute-done((bf16[32,3712]{1,0:T(8,128)(2,1)S(1)}, bf16[32,3712]{1,0:T(8,128)(2,1)S(1)}, u32[]{:S(2)}, u32[]{:S(2)}) %collective-permute-start.3) | collective-permute-done | bytes 237600 | tf_op jit(solution)/shard_map/ppermute | solution.py:43
  67.2 2.2 %collective-permute-start.5 = (bf16[32,3712]{1,0:T(8,128)(2,1)S(1)}, bf16[32,3712]{1,0:T(8,128)(2,1)S(1)}, u32[]{:S(2)}, u32[]{:S(2)}) collective-permute-start(bf16[32,3712]{1,0:T(8,128)(2,1)S(1)} %collective-permute-done.3.refs_4_), channel_id=1, source_target_pairs={{0,2},{2,4},{4,6},{6,8},{8,10},{10,12},{12,14},{14,0},{1,3},{3,5},... | collective-permute-start | bytes 712712 | tf_op jit(solution)/shard_map/ppermute | solution.py:43
  69.4 0.0 collective-permute-done.4.refs_5_
  69.4 4.9 %collective-permute-start.6 = (bf16[32,3712]{1,0:T(8,128)(2,1)S(1)}, bf16[32,3712]{1,0:T(8,128)(2,1)S(1)}, u32[]{:S(2)}, u32[]{:S(2)}) collective-permute-start(bf16[32,3712]{1,0:T(8,128)(2,1)S(1)} %collective-permute-done.4.refs_5_), channel_id=1, source_target_pairs={{0,14},{2,0},{4,2},{6,4},{8,6},{10,8},{12,10},{14,12},{1,15},{3,1}... | collective-permute-start | bytes 712712 | tf_op jit(solution)/shard_map/ppermute | solution.py:44
  74.3 2.5 %collective-permute-done.5.refs_6_ = bf16[32,3712]{1,0:T(8,128)(2,1)S(1)} collective-permute-done((bf16[32,3712]{1,0:T(8,128)(2,1)S(1)}, bf16[32,3712]{1,0:T(8,128)(2,1)S(1)}, u32[]{:S(2)}, u32[]{:S(2)}) %collective-permute-start.5) | collective-permute-done | bytes 237600 | tf_op jit(solution)/shard_map/ppermute | solution.py:43
  76.8 1.9 %collective-permute-start.7 = (bf16[32,3712]{1,0:T(8,128)(2,1)S(1)}, bf16[32,3712]{1,0:T(8,128)(2,1)S(1)}, u32[]{:S(2)}, u32[]{:S(2)}) collective-permute-start(bf16[32,3712]{1,0:T(8,128)(2,1)S(1)} %collective-permute-done.5.refs_6_), channel_id=1, source_target_pairs={{0,2},{2,4},{4,6},{6,8},{8,10},{10,12},{12,14},{14,0},{1,3},{3,5},... | collective-permute-start | bytes 712712 | tf_op jit(solution)/shard_map/ppermute | solution.py:43
  78.7 0.0 copy-start.4
  78.7 0.7 copy-done.4
  79.4 0.0 collective-permute-done.6.refs_7_
  79.4 5.1 %collective-permute-start.8 = (bf16[32,3712]{1,0:T(8,128)(2,1)S(1)}, bf16[32,3712]{1,0:T(8,128)(2,1)}, u32[]{:S(2)}, u32[]{:S(2)}) collective-permute-start(bf16[32,3712]{1,0:T(8,128)(2,1)S(1)} %collective-permute-done.6.refs_7_), channel_id=1, source_target_pairs={{0,14},{2,0},{4,2},{6,4},{8,6},{10,8},{12,10},{14,12},{1,15},{3,1}... | collective-permute-start | bytes 712712 | tf_op jit(solution)/shard_map/ppermute | solution.py:44
  84.5 0.0 copy-start.6
  84.6 0.7 copy-done.6
  85.2 0.8 collective-permute-done.7.refs_8_
  86.0 1.9 %collective-permute-start.9 = (bf16[32,3712]{1,0:T(8,128)(2,1)S(1)}, bf16[32,3712]{1,0:T(8,128)(2,1)S(1)}, u32[]{:S(2)}, u32[]{:S(2)}) collective-permute-start(bf16[32,3712]{1,0:T(8,128)(2,1)S(1)} %collective-permute-done.7.refs_8_), channel_id=1, source_target_pairs={{0,2},{2,4},{4,6},{6,8},{8,10},{10,12},{12,14},{14,0},{1,3},{3,5},... | collective-permute-start | bytes 712712 | tf_op jit(solution)/shard_map/ppermute | solution.py:46
  87.9 0.0 copy-start.8
  87.9 0.7 copy-done.8
  88.6 0.1 pad_add_fusion.refs_0_.at_ref
  88.7 1.9 %collective-permute-start.10 = (bf16[224,2048]{1,0:T(8,128)(2,1)}, bf16[224,2048]{1,0:T(8,128)(2,1)}, u32[]{:S(2)}, u32[]{:S(2)}) collective-permute-start(bf16[224,2048]{1,0:T(8,128)(2,1)} %collective-permute-done.pair_ref), channel_id=1, source_target_pairs={{0,1},{1,0},{2,3},{3,2},{4,5},{5,4},{6,7},{7,6},{8,9},{9,8},{10,11... | collective-permute-start | bytes 2752520 | tf_op jit(solution)/shard_map/ppermute | solution.py:202
  90.6 0.0 collective-permute-done.8.refs_9_
  90.6 4.6 %collective-permute-done.9.refs_10_ = bf16[32,3712]{1,0:T(8,128)(2,1)S(1)} collective-permute-done((bf16[32,3712]{1,0:T(8,128)(2,1)S(1)}, bf16[32,3712]{1,0:T(8,128)(2,1)S(1)}, u32[]{:S(2)}, u32[]{:S(2)}) %collective-permute-start.9) | collective-permute-done | bytes 237600 | tf_op jit(solution)/shard_map/ppermute | solution.py:46
  95.2 0.0 copy-start.10
  95.2 0.7 copy-done.10
  95.9 0.0 copy-start
  95.9 1.5 copy-done
  97.4 0.0 copy-start.5
  97.4 0.9 copy-done.5
  98.3 0.0 copy-start.7
  98.3 0.9 copy-done.7
  99.3 0.9 copy-done.9
  100.2 0.0 copy-start.11
  100.2 0.9 copy-done.11
  101.2 0.0 copy-start.1
  101.2 7.0 %hidden.1 = bf16[8,128,256]{2,1,0:T(8,128)(2,1)} custom-call(s32[2]{0:T(128)S(1)} %pad_add_fusion.refs_0_.at_ref, bf16[3584,256]{1,0:T(8,128)(2,1)S(1)} %bitcast.9, bf16[3584,256]{1,0:T(8,128)(2,1)S(1)} %collective-permute-done.1.refs_2_, bf16[32,3712]{1,0:T(8,128)(2,1)S(1)} %get-tuple-element.16.refs_3_, ...), custom_call_target="tpu_custom_call" | custom-call | tf_op jit(solution)/shard_map/hidden/pallas_call | solution.py:211
  108.1 6.8 %all-to-all-start.1 = ((bf16[8,128,256]{2,1,0:T(8,128)(2,1)}), bf16[8,128,256]{2,1,0:T(8,128)(2,1)S(1)}, u32[]{:S(2)}, u32[]{:S(2)}) async-start(bf16[8,128,256]{2,1,0:T(8,128)(2,1)} %hidden.1), calls=%async_computation.1 | async-start | bytes 1048576 | tf_op jit(solution)/shard_map/all_to_all | solution.py:218
  114.9 0.0 collective-permute-done.10.both_ref
  114.9 14.1 %all-to-all-done.1.h_ref = bf16[8,128,256]{2,1,0:T(8,128)(2,1)S(1)} async-done(((bf16[8,128,256]{2,1,0:T(8,128)(2,1)}), bf16[8,128,256]{2,1,0:T(8,128)(2,1)S(1)}, u32[]{:S(2)}, u32[]{:S(2)}) %all-to-all-start.1) | async-done | bytes 524320 | tf_op jit(solution)/shard_map/all_to_all | solution.py:218
  129.0 0.0 copy-done.1
  129.0 0.0 copy-start.3
  129.1 1.2 copy-done.3
  130.2 3.7 %down.1 = bf16[8,16,896]{2,1,0:T(8,128)(2,1)S(1)} custom-call(s32[2]{0:T(128)S(1)} %pad_add_fusion.refs_0_.at_ref, bf16[8,128,256]{2,1,0:T(8,128)(2,1)S(1)} %all-to-all-done.1.h_ref, bf16[224,2048]{1,0:T(8,128)(2,1)S(1)} %bitcast.12, bf16[224,2048]{1,0:T(8,128)(2,1)S(1)} %copy-done.3, bf16[224,2048]{1,0:T(8,128)(2,1)} %collective-permute-done.pair_ref, ...), custom_call_target="tpu_custom_call" | custom-call | tf_op jit(solution)/shard_map/down/pallas_call | solution.py:219
  133.9 12.5 %all_to_all.20.back_ref = bf16[8,16,896]{2,1,0:T(8,128)(2,1)S(1)} all-to-all(bf16[8,16,896]{2,1,0:T(8,128)(2,1)S(1)} %down.1), channel_id=1, replica_groups=mesh['y'=8,'z'=8,'x'=8,'core'=2] {'x'}, dimensions={0} | all-to-all | bytes 458752 | tf_op jit(solution)/shard_map/all_to_all | solution.py:226
  146.5 0.3 spread.1
  146.8 27.0 %all_to_all.21.in_ref = bf16[64,2,1792]{2,1,0:T(2,128)(2,1)S(1)} all-to-all(bf16[64,2,1792]{2,1,0:T(2,128)(2,1)S(1)} %spread.1), channel_id=1, replica_groups=mesh['y'=8,'z'=8,'x'=8,'core'=2] {'y','z'}, dimensions={0} | all-to-all | bytes 917504 | tf_op jit(solution)/shard_map/all_to_all | solution.py:230
  173.8 1.8 %mix.1 = bf16[8,3584]{1,0:T(8,128)(2,1)} custom-call(bf16[64,2,1792]{2,1,0:T(2,128)(2,1)S(1)} %all_to_all.21.in_ref, bf16[64,8]{1,0:T(8,128)(2,1)S(1)} %get-tuple-element.20.place_ref), custom_call_target="tpu_custom_call" | custom-call | tf_op jit(solution)/shard_map/mix/pallas_call | solution.py:231
  (1 shorter events, 0.0 us)
Async XLA Ops:
  0.0 55.3 %collective-permute-start.1 = (bf16[3584,256]{1,0:T(8,128)(2,1)}, bf16[3584,256]{1,0:T(8,128)(2,1)S(1)}, u32[]{:S(2)}, u32[]{:S(2)}) collective-permute-start(bf16[3584,256]{1,0:T(8,128)(2,1)} %bitcast.8), channel_id=1, source_target_pairs={{0,1},{1,0},{2,3},{3,2},{4,5},{5,4},{6,7},{7,6},{8,9},{9,8},{10,11... | collective-permute-start | bytes 5505032 | tf_op jit(solution)/shard_map/ppermute | solution.py:196
  1.9 0.8 copy-start.12
  2.7 0.7 copy-start.13
  3.4 0.7 copy-start.14
  5.3 50.0 %all-to-all-start = ((bf16[64,2,1920]{2,1,0:T(2,128)(2,1)}), bf16[64,2,1920]{2,1,0:T(2,128)(2,1)S(1)}, u32[]{:S(2)}, u32[]{:S(2)}) async-start(bf16[64,2,1920]{2,1,0:T(2,128)(2,1)} %get-tuple-element.13), calls=%async_computation | async-start | bytes 983040 | tf_op jit(solution)/shard_map/all_to_all | solution.py:198
  28.4 5.3 %collective-permute-start.2 = (bf16[224,2048]{1,0:T(8,128)(2,1)}, bf16[224,2048]{1,0:T(8,128)(2,1)S(1)}, u32[]{:S(2)}, u32[]{:S(2)}) collective-permute-start(bf16[224,2048]{1,0:T(8,128)(2,1)} %bitcast.10), channel_id=1, source_target_pairs={{0,1},{1,0},{2,3},{3,2},{4,5},{5,4},{6,7},{7,6},{8,9},{9,8},{10,11... | collective-permute-start | bytes 2752520 | tf_op jit(solution)/shard_map/ppermute | solution.py:197
  30.3 25.0 %collective-permute-start = (bf16[224,2048]{1,0:T(8,128)(2,1)}, bf16[224,2048]{1,0:T(8,128)(2,1)}, u32[]{:S(2)}, u32[]{:S(2)}) collective-permute-start(bf16[224,2048]{1,0:T(8,128)(2,1)} %bitcast.11), channel_id=1, source_target_pairs={{0,2},{2,0},{4,6},{6,4},{8,10},{10,8},{12,14},{14,12},{1,3},{3,1},... | collective-permute-start | bytes 2752520 | tf_op jit(solution)/shard_map/ppermute | solution.py:195
  33.7 0.9 copy-start.2
  56.7 10.5 %collective-permute-start.3 = (bf16[32,3712]{1,0:T(8,128)(2,1)S(1)}, bf16[32,3712]{1,0:T(8,128)(2,1)S(1)}, u32[]{:S(2)}, u32[]{:S(2)}) collective-permute-start(bf16[32,3712]{1,0:T(8,128)(2,1)S(1)} %get-tuple-element.16.refs_3_), channel_id=1, source_target_pairs={{0,2},{2,4},{4,6},{6,8},{8,10},{10,12},{12,14},{14,0},{1,3},{3,5},... | collective-permute-start | bytes 712712 | tf_op jit(solution)/shard_map/ppermute | solution.py:43
  60.1 9.3 %collective-permute-start.4 = (bf16[32,3712]{1,0:T(8,128)(2,1)S(1)}, bf16[32,3712]{1,0:T(8,128)(2,1)S(1)}, u32[]{:S(2)}, u32[]{:S(2)}) collective-permute-start(bf16[32,3712]{1,0:T(8,128)(2,1)S(1)} %get-tuple-element.16.refs_3_), channel_id=1, source_target_pairs={{0,14},{2,0},{4,2},{6,4},{8,6},{10,8},{12,10},{14,12},{1,15},{3,1}... | collective-permute-start | bytes 712712 | tf_op jit(solution)/shard_map/ppermute | solution.py:44
  67.2 9.6 %collective-permute-start.5 = (bf16[32,3712]{1,0:T(8,128)(2,1)S(1)}, bf16[32,3712]{1,0:T(8,128)(2,1)S(1)}, u32[]{:S(2)}, u32[]{:S(2)}) collective-permute-start(bf16[32,3712]{1,0:T(8,128)(2,1)S(1)} %collective-permute-done.3.refs_4_), channel_id=1, source_target_pairs={{0,2},{2,4},{4,6},{6,8},{8,10},{10,12},{12,14},{14,0},{1,3},{3,5},... | collective-permute-start | bytes 712712 | tf_op jit(solution)/shard_map/ppermute | solution.py:43
  69.4 10.0 %collective-permute-start.6 = (bf16[32,3712]{1,0:T(8,128)(2,1)S(1)}, bf16[32,3712]{1,0:T(8,128)(2,1)S(1)}, u32[]{:S(2)}, u32[]{:S(2)}) collective-permute-start(bf16[32,3712]{1,0:T(8,128)(2,1)S(1)} %collective-permute-done.4.refs_5_), channel_id=1, source_target_pairs={{0,14},{2,0},{4,2},{6,4},{8,6},{10,8},{12,10},{14,12},{1,15},{3,1}... | collective-permute-start | bytes 712712 | tf_op jit(solution)/shard_map/ppermute | solution.py:44
  76.8 9.2 %collective-permute-start.7 = (bf16[32,3712]{1,0:T(8,128)(2,1)S(1)}, bf16[32,3712]{1,0:T(8,128)(2,1)S(1)}, u32[]{:S(2)}, u32[]{:S(2)}) collective-permute-start(bf16[32,3712]{1,0:T(8,128)(2,1)S(1)} %collective-permute-done.5.refs_6_), channel_id=1, source_target_pairs={{0,2},{2,4},{4,6},{6,8},{8,10},{10,12},{12,14},{14,0},{1,3},{3,5},... | collective-permute-start | bytes 712712 | tf_op jit(solution)/shard_map/ppermute | solution.py:43
  78.7 0.7 copy-start.4
  79.4 11.2 %collective-permute-start.8 = (bf16[32,3712]{1,0:T(8,128)(2,1)S(1)}, bf16[32,3712]{1,0:T(8,128)(2,1)}, u32[]{:S(2)}, u32[]{:S(2)}) collective-permute-start(bf16[32,3712]{1,0:T(8,128)(2,1)S(1)} %collective-permute-done.6.refs_7_), channel_id=1, source_target_pairs={{0,14},{2,0},{4,2},{6,4},{8,6},{10,8},{12,10},{14,12},{1,15},{3,1}... | collective-permute-start | bytes 712712 | tf_op jit(solution)/shard_map/ppermute | solution.py:44
  84.5 0.7 copy-start.6
  86.0 9.2 %collective-permute-start.9 = (bf16[32,3712]{1,0:T(8,128)(2,1)S(1)}, bf16[32,3712]{1,0:T(8,128)(2,1)S(1)}, u32[]{:S(2)}, u32[]{:S(2)}) collective-permute-start(bf16[32,3712]{1,0:T(8,128)(2,1)S(1)} %collective-permute-done.7.refs_8_), channel_id=1, source_target_pairs={{0,2},{2,4},{4,6},{6,8},{8,10},{10,12},{12,14},{14,0},{1,3},{3,5},... | collective-permute-start | bytes 712712 | tf_op jit(solution)/shard_map/ppermute | solution.py:46
  87.9 0.7 copy-start.8
  88.7 26.2 %collective-permute-start.10 = (bf16[224,2048]{1,0:T(8,128)(2,1)}, bf16[224,2048]{1,0:T(8,128)(2,1)}, u32[]{:S(2)}, u32[]{:S(2)}) collective-permute-start(bf16[224,2048]{1,0:T(8,128)(2,1)} %collective-permute-done.pair_ref), channel_id=1, source_target_pairs={{0,1},{1,0},{2,3},{3,2},{4,5},{5,4},{6,7},{7,6},{8,9},{9,8},{10,11... | collective-permute-start | bytes 2752520 | tf_op jit(solution)/shard_map/ppermute | solution.py:202
  95.2 0.7 copy-start.10
  95.9 1.5 copy-start
  97.4 0.9 copy-start.5
  98.3 0.9 copy-start.7
  99.3 0.9 copy-start.9
  100.2 0.9 copy-start.11
  101.2 27.9 %copy-start.1 = (bf16[1,2048,224]{1,2,0:T(8,128)(2,1)S(1)}, bf16[1,2048,224]{1,2,0:T(8,128)(2,1)}, u32[]{:S(2)}) copy-start(bf16[1,2048,224]{1,2,0:T(8,128)(2,1)} %param.9) | copy-start | bytes 2752516
  108.1 20.9 %all-to-all-start.1 = ((bf16[8,128,256]{2,1,0:T(8,128)(2,1)}), bf16[8,128,256]{2,1,0:T(8,128)(2,1)S(1)}, u32[]{:S(2)}, u32[]{:S(2)}) async-start(bf16[8,128,256]{2,1,0:T(8,128)(2,1)} %hidden.1), calls=%async_computation.1 | async-start | bytes 1048576 | tf_op jit(solution)/shard_map/all_to_all | solution.py:218
  129.0 1.2 copy-start.3

commit v3 on v2

--- a/solution.py
+++ b/solution.py
@@ -12,6 +12,8 @@
 SMEM = pl.BlockSpec(memory_space=pltpu.SMEM)
 HBM = pl.BlockSpec(memory_space=pltpu.HBM)
 CHUNKS = 4
+HID = 50
+DOWN = 50
 
 
 def dot(a, b):
@@ -22,14 +24,14 @@
     return lax.dot_general(a, b, (((da,), (db,)), ((), ())), preferred_element_type=f32)
 
 
-def call(kernel, outs, specs, name, scratch=()):
+def call(kernel, outs, specs, name, scratch=(), room=8):
     return pl.pallas_call(
         kernel,
         out_shape=[jax.ShapeDtypeStruct(s, d) for s, d in outs],
         in_specs=specs,
         out_specs=[VMEM] * len(outs),
         scratch_shapes=list(scratch),
-        compiler_params=pltpu.CompilerParams(vmem_limit_bytes=20 * 2**20),
+        compiler_params=pltpu.CompilerParams(vmem_limit_bytes=room * 2**20),
         name=name,
     )
 
@@ -191,15 +193,16 @@
         [((groups, 2, half + LANES), bf16), ((groups, toks), bf16)],
         [VMEM] * 3,
         "pack",
+        room=60,
     )(node_picks.T, gates.transpose(1, 2, 0), tokens)
     dn_pair = lax.ppermute(dn, "x", pair)
     gu_other = lax.ppermute(gu, "core", swap)
     dn_other = lax.ppermute(dn, "core", swap)
     arrived = lax.all_to_all(send, group, split_axis=0, concat_axis=0, tiled=True)
-    arrived, dn_pair, gu_other, dn_other = lax.optimization_barrier(
-        (arrived, dn_pair, gu_other, dn_other)
-    )
     dn_both = lax.ppermute(dn_pair, "core", swap)
+    arrived, dn_pair, gu_other, dn_other, dn_both = lax.optimization_barrier(
+        (arrived, dn_pair, gu_other, dn_other, dn_both)
+    )
     rows, select = call(
         compact_kernel,
         [((r, width + LANES), bf16), ((groups, r), bf16)],
@@ -214,6 +217,7 @@
         [SMEM, HBM, HBM] + [VMEM] * n,
         "hidden",
         [pltpu.VMEM((2,) + gu.shape, bf16), pltpu.SemaphoreType.DMA((2, CHUNKS))],
+        HID,
     )(at, gu, gu_other, *[b for _, b in got])
     hid = lax.all_to_all(hid, "x", split_axis=0, concat_axis=0, tiled=True)
     (out,) = call(
@@ -222,6 +226,7 @@
         [SMEM, VMEM] + [HBM] * 4,
         "down",
         [pltpu.VMEM((4,) + dn.shape, bf16), pltpu.SemaphoreType.DMA((4,))],
+        DOWN,
     )(at, hid, dn, dn_other, dn_pair, dn_both)
     back = lax.all_to_all(out, "x", split_axis=0, concat_axis=0, tiled=True)
     (padded,) = call(spread_kernel, [((groups, 2, half), bf16)], [VMEM] * 2, "spread")(

time: 177 us -> 154 us (0.87)
  waiting for transfers between devices: 46.1 us -> 28.8 us
  blocking collectives: 39.6 us -> 53.1 us
  local copies, waits for them, and re-layouts: 12.3 us -> 0.94 us
  starting transfers between devices: 62 us -> 55.8 us
    ppermute x1, waiting for transfers between devices: 20.6 us -> 0.01 us  [shards(): dn_pair = lax.ppermute(dn, 'x', pair)]
    all_to_all x0 -> x1, blocking collectives: none -> 18.9 us  [shards(): hid = lax.all_to_all(hid, 'x', split_axis=0, concat_axis=0, tiled=True)]
    all_to_all x1, waiting for transfers between devices: 0.01 us -> 14.8 us  [shards(): lax.all_to_all(send, group, split_axis=0, concat_axis=0, tiled=True)]
    all_to_all x1 -> x0, waiting for transfers between devices: 14.1 us -> none  [shards(): hid = lax.all_to_all(hid, 'x', split_axis=0, concat_axis=0, tiled=True)]
    unnamed x30 -> x6, local copies, waits for them, and re-layouts: 12.3 us -> 0.94 us
    all_to_all x1 -> x0, starting transfers between devices: 6.77 us -> none  [shards(): hid = lax.all_to_all(hid, 'x', split_axis=0, concat_axis=0, tiled=True)]
    all_to_all x1, blocking collectives: 27 us -> 21.7 us  [shards(): lax.all_to_all(padded, group, split_axis=0, concat_axis=0, tiled=True)]
    ppermute x1, waiting for transfers between devices: 4.59 us -> 7.3 us  [ring(): got.append((n // 2, lax.ppermute(fwd, 'x', up)))]
  transfers between devices with their start and end apart: 13 -> 12, of which waited for: 6 -> 6; matrix products, arithmetic and copies ran while one was open for 0% -> 0% of each run, Pallas kernels for 5% -> 1%
where the time goes in v3:
time: 154 us; the launch traced here: 153 us
  starting transfers between devices  55.8 us (36%)
  blocking collectives  53.1 us (34%)
  waiting for transfers between devices  28.8 us (19%)
  Pallas kernels  14.3 us (9%)
    all_to_all x1, starting transfers between devices, shards(): lax.all_to_all(send, group, split_axis=0, concat_axis=0, tiled=True)  23.1 us
    all_to_all x1, blocking collectives, shards(): lax.all_to_all(padded, group, split_axis=0, concat_axis=0, tiled=True)  21.7 us
    all_to_all x1, blocking collectives, shards(): hid = lax.all_to_all(hid, 'x', split_axis=0, concat_axis=0, tiled=True)  18.9 us
    ppermute x3, starting transfers between devices, ring(): back = lax.ppermute(back, 'x', down)  14.9 us
    all_to_all x1, waiting for transfers between devices, shards(): lax.all_to_all(send, group, split_axis=0, concat_axis=0, tiled=True)  14.8 us
    all_to_all x1, blocking collectives, shards(): back = lax.all_to_all(out, 'x', split_axis=0, concat_axis=0, tiled=True)  12.5 us
    ppermute x1, waiting for transfers between devices, ring(): got.append((n // 2, lax.ppermute(fwd, 'x', up)))  7.3 us
    ppermute x3, waiting for transfers between devices, ring(): fwd = lax.ppermute(fwd, 'x', up)  6.41 us
  transfers between devices with their start and end apart: 12, of which 6 were waited for; matrix products, arithmetic and copies ran while one was open for 0% of the time, Pallas kernels for 1%

profile of v3, /device:TPU:32, one launch (start us, length us, event | category | flops | bytes accessed | tf_op | source)
XLA Modules:
  0.0 153.2 jit_solution(7011836177284506958)
XLA Ops:
  0.0 3.4 %collective-permute-start = (bf16[224,2048]{1,0:T(8,128)(2,1)}, bf16[224,2048]{1,0:T(8,128)(2,1)S(1)}, u32[]{:S(2)}, u32[]{:S(2)}) collective-permute-start(bf16[224,2048]{1,0:T(8,128)(2,1)} %bitcast.8), channel_id=1, source_target_pairs={{0,2},{2,0},{4,6},{6,4},{8,10},{10,8},{12,14},{14,12},{1,3},{3,1},... | collective-permute-start | bytes 2752520 | tf_op jit(solution)/shard_map/ppermute | solution.py:198
  3.4 1.9 %collective-permute-start.1 = (bf16[3584,256]{1,0:T(8,128)(2,1)}, bf16[3584,256]{1,0:T(8,128)(2,1)}, u32[]{:S(2)}, u32[]{:S(2)}) collective-permute-start(bf16[3584,256]{1,0:T(8,128)(2,1)} %bitcast.11), channel_id=1, source_target_pairs={{0,1},{1,0},{2,3},{3,2},{4,5},{5,4},{6,7},{7,6},{8,9},{9,8},{10,11... | collective-permute-start | bytes 5505032 | tf_op jit(solution)/shard_map/ppermute | solution.py:199
  5.3 2.0 %pack.1 = (bf16[64,2,1920]{2,1,0:T(2,128)(2,1)}, bf16[64,8]{1,0:T(8,128)(2,1)}) custom-call(s32[4,8]{1,0:T(4,128)} %bitcast.13, bf16[4,2,8]{2,1,0:T(2,128)(2,1)} %bitcast.14, bf16[8,3584]{1,0:T(8,128)(2,1)} %tok_ref.1), custom_call_target="tpu_custom_call" | custom-call | tf_op jit(solution)/shard_map/pack/pallas_call | solution.py:191
  7.4 23.1 %all-to-all-start = ((bf16[64,2,1920]{2,1,0:T(2,128)(2,1)}), bf16[64,2,1920]{2,1,0:T(2,128)(2,1)S(1)}, u32[]{:S(2)}, u32[]{:S(2)}) async-start(bf16[64,2,1920]{2,1,0:T(2,128)(2,1)} %get-tuple-element.14), calls=%async_computation | async-start | bytes 983040 | tf_op jit(solution)/shard_map/all_to_all | solution.py:201
  30.5 1.9 %collective-permute-start.2 = (bf16[224,2048]{1,0:T(8,128)(2,1)}, bf16[224,2048]{1,0:T(8,128)(2,1)S(1)}, u32[]{:S(2)}, u32[]{:S(2)}) collective-permute-start(bf16[224,2048]{1,0:T(8,128)(2,1)} %bitcast.9), channel_id=1, source_target_pairs={{0,1},{1,0},{2,3},{3,2},{4,5},{5,4},{6,7},{7,6},{8,9},{9,8},{10,11... | collective-permute-start | bytes 2752520 | tf_op jit(solution)/shard_map/ppermute | solution.py:200
  32.5 0.0 collective-permute-done.pair_ref
  32.5 2.4 %collective-permute-start.3 = (bf16[224,2048]{1,0:T(8,128)(2,1)S(1)}, bf16[224,2048]{1,0:T(8,128)(2,1)S(1)}, u32[]{:S(2)}, u32[]{:S(2)}) collective-permute-start(bf16[224,2048]{1,0:T(8,128)(2,1)S(1)} %collective-permute-done.pair_ref), channel_id=1, source_target_pairs={{0,1},{1,0},{2,3},{3,2},{4,5},{5,4},{6,7},{7,6},{8,9},{9,8},{10,11... | collective-permute-start | bytes 2752520 | tf_op jit(solution)/shard_map/ppermute | solution.py:202
  34.9 0.2 collective-permute-done.2.other_ref
  35.1 14.8 %all-to-all-done.in_ref = bf16[64,2,1920]{2,1,0:T(2,128)(2,1)S(1)} async-done(((bf16[64,2,1920]{2,1,0:T(2,128)(2,1)}), bf16[64,2,1920]{2,1,0:T(2,128)(2,1)S(1)}, u32[]{:S(2)}, u32[]{:S(2)}) %all-to-all-start) | async-done | bytes 491552 | tf_op jit(solution)/shard_map/all_to_all | solution.py:201
  49.9 0.0 collective-permute-done.3.both_ref
  49.9 0.0 copy-start.2
  49.9 0.9 copy-done.2
  50.8 0.0 collective-permute-done.1.refs_2_
  50.8 1.4 compact.1
  52.3 2.4 %collective-permute-start.4 = (bf16[32,3712]{1,0:T(8,128)(2,1)S(1)}, bf16[32,3712]{1,0:T(8,128)(2,1)S(1)}, u32[]{:S(2)}, u32[]{:S(2)}) collective-permute-start(bf16[32,3712]{1,0:T(8,128)(2,1)S(1)} %get-tuple-element.17.refs_3_), channel_id=1, source_target_pairs={{0,2},{2,4},{4,6},{6,8},{8,10},{10,12},{12,14},{14,0},{1,3},{3,5},... | collective-permute-start | bytes 712712 | tf_op jit(solution)/shard_map/ppermute | solution.py:45
  54.6 4.7 %collective-permute-start.5 = (bf16[32,3712]{1,0:T(8,128)(2,1)S(1)}, bf16[32,3712]{1,0:T(8,128)(2,1)S(1)}, u32[]{:S(2)}, u32[]{:S(2)}) collective-permute-start(bf16[32,3712]{1,0:T(8,128)(2,1)S(1)} %get-tuple-element.17.refs_3_), channel_id=1, source_target_pairs={{0,14},{2,0},{4,2},{6,4},{8,6},{10,8},{12,10},{14,12},{1,15},{3,1}... | collective-permute-start | bytes 712712 | tf_op jit(solution)/shard_map/ppermute | solution.py:46
  59.3 2.1 %collective-permute-done.4.refs_4_ = bf16[32,3712]{1,0:T(8,128)(2,1)S(1)} collective-permute-done((bf16[32,3712]{1,0:T(8,128)(2,1)S(1)}, bf16[32,3712]{1,0:T(8,128)(2,1)S(1)}, u32[]{:S(2)}, u32[]{:S(2)}) %collective-permute-start.4) | collective-permute-done | bytes 237600 | tf_op jit(solution)/shard_map/ppermute | solution.py:45
  61.5 1.9 %collective-permute-start.6 = (bf16[32,3712]{1,0:T(8,128)(2,1)S(1)}, bf16[32,3712]{1,0:T(8,128)(2,1)S(1)}, u32[]{:S(2)}, u32[]{:S(2)}) collective-permute-start(bf16[32,3712]{1,0:T(8,128)(2,1)S(1)} %collective-permute-done.4.refs_4_), channel_id=1, source_target_pairs={{0,2},{2,4},{4,6},{6,8},{8,10},{10,12},{12,14},{14,0},{1,3},{3,5},... | collective-permute-start | bytes 712712 | tf_op jit(solution)/shard_map/ppermute | solution.py:45
  63.4 0.0 collective-permute-done.5.refs_5_
  63.4 5.1 %collective-permute-start.7 = (bf16[32,3712]{1,0:T(8,128)(2,1)S(1)}, bf16[32,3712]{1,0:T(8,128)(2,1)S(1)}, u32[]{:S(2)}, u32[]{:S(2)}) collective-permute-start(bf16[32,3712]{1,0:T(8,128)(2,1)S(1)} %collective-permute-done.5.refs_5_), channel_id=1, source_target_pairs={{0,14},{2,0},{4,2},{6,4},{8,6},{10,8},{12,10},{14,12},{1,15},{3,1}... | collective-permute-start | bytes 712712 | tf_op jit(solution)/shard_map/ppermute | solution.py:46
  68.5 2.1 %collective-permute-done.6.refs_6_ = bf16[32,3712]{1,0:T(8,128)(2,1)S(1)} collective-permute-done((bf16[32,3712]{1,0:T(8,128)(2,1)S(1)}, bf16[32,3712]{1,0:T(8,128)(2,1)S(1)}, u32[]{:S(2)}, u32[]{:S(2)}) %collective-permute-start.6) | collective-permute-done | bytes 237600 | tf_op jit(solution)/shard_map/ppermute | solution.py:45
  70.7 1.9 %collective-permute-start.8 = (bf16[32,3712]{1,0:T(8,128)(2,1)S(1)}, bf16[32,3712]{1,0:T(8,128)(2,1)S(1)}, u32[]{:S(2)}, u32[]{:S(2)}) collective-permute-start(bf16[32,3712]{1,0:T(8,128)(2,1)S(1)} %collective-permute-done.6.refs_6_), channel_id=1, source_target_pairs={{0,2},{2,4},{4,6},{6,8},{8,10},{10,12},{12,14},{14,0},{1,3},{3,5},... | collective-permute-start | bytes 712712 | tf_op jit(solution)/shard_map/ppermute | solution.py:45
  72.6 0.0 collective-permute-done.7.refs_7_
  72.6 5.1 %collective-permute-start.9 = (bf16[32,3712]{1,0:T(8,128)(2,1)S(1)}, bf16[32,3712]{1,0:T(8,128)(2,1)S(1)}, u32[]{:S(2)}, u32[]{:S(2)}) collective-permute-start(bf16[32,3712]{1,0:T(8,128)(2,1)S(1)} %collective-permute-done.7.refs_7_), channel_id=1, source_target_pairs={{0,14},{2,0},{4,2},{6,4},{8,6},{10,8},{12,10},{14,12},{1,15},{3,1}... | collective-permute-start | bytes 712712 | tf_op jit(solution)/shard_map/ppermute | solution.py:46
  77.7 2.1 %collective-permute-done.8.refs_8_ = bf16[32,3712]{1,0:T(8,128)(2,1)S(1)} collective-permute-done((bf16[32,3712]{1,0:T(8,128)(2,1)S(1)}, bf16[32,3712]{1,0:T(8,128)(2,1)S(1)}, u32[]{:S(2)}, u32[]{:S(2)}) %collective-permute-start.8) | collective-permute-done | bytes 237600 | tf_op jit(solution)/shard_map/ppermute | solution.py:45
  79.9 1.9 %collective-permute-start.10 = (bf16[32,3712]{1,0:T(8,128)(2,1)S(1)}, bf16[32,3712]{1,0:T(8,128)(2,1)}, u32[]{:S(2)}, u32[]{:S(2)}) collective-permute-start(bf16[32,3712]{1,0:T(8,128)(2,1)S(1)} %collective-permute-done.8.refs_8_), channel_id=1, source_target_pairs={{0,2},{2,4},{4,6},{6,8},{8,10},{10,12},{12,14},{14,0},{1,3},{3,5},... | collective-permute-start | bytes 712712 | tf_op jit(solution)/shard_map/ppermute | solution.py:48
  81.8 0.1 pad_add_fusion.refs_0_.at_ref
  81.9 0.0 copy-start
  81.9 0.0 collective-permute-done.9.refs_9_
  81.9 7.3 %collective-permute-done.10.refs_10_ = bf16[32,3712]{1,0:T(8,128)(2,1)} collective-permute-done((bf16[32,3712]{1,0:T(8,128)(2,1)S(1)}, bf16[32,3712]{1,0:T(8,128)(2,1)}, u32[]{:S(2)}, u32[]{:S(2)}) %collective-permute-start.10) | collective-permute-done | bytes 237600 | tf_op jit(solution)/shard_map/ppermute | solution.py:48
  89.2 4.8 %hidden.1 = bf16[8,128,256]{2,1,0:T(8,128)(2,1)S(1)} custom-call(s32[2]{0:T(128)S(1)} %pad_add_fusion.refs_0_.at_ref, bf16[3584,256]{1,0:T(8,128)(2,1)} %bitcast.12, bf16[3584,256]{1,0:T(8,128)(2,1)} %collective-permute-done.1.refs_2_, bf16[32,3712]{1,0:T(8,128)(2,1)S(1)} %get-tuple-element.17.refs_3_, bf16[32,3712]{1,0:T(8,128)(2,1)S(1)} %collective-permute-done.4.refs_4_, ...), custom_call_target="tpu_custom_call" | custom-call | tf_op jit(solution)/shard_map/hidden/pallas_call | solution.py:214
  94.0 18.9 %all_to_all.20.h_ref = bf16[8,128,256]{2,1,0:T(8,128)(2,1)S(1)} all-to-all(bf16[8,128,256]{2,1,0:T(8,128)(2,1)S(1)} %hidden.1), channel_id=1, replica_groups=mesh['y'=8,'z'=8,'x'=8,'core'=2] {'x'}, dimensions={0} | all-to-all | bytes 1048576 | tf_op jit(solution)/shard_map/all_to_all | solution.py:222
  112.9 0.0 copy-done
  112.9 3.9 %down.1 = bf16[8,16,896]{2,1,0:T(8,128)(2,1)S(1)} custom-call(s32[2]{0:T(128)S(1)} %pad_add_fusion.refs_0_.at_ref, bf16[8,128,256]{2,1,0:T(8,128)(2,1)S(1)} %all_to_all.20.h_ref, bf16[224,2048]{1,0:T(8,128)(2,1)S(1)} %bitcast.10, bf16[224,2048]{1,0:T(8,128)(2,1)S(1)} %collective-permute-done.2.other_ref, ...), custom_call_target="tpu_custom_call" | custom-call | tf_op jit(solution)/shard_map/down/pallas_call | solution.py:223
  116.8 0.0 copy-start.1
  116.9 12.5 %all_to_all.21.back_ref = bf16[8,16,896]{2,1,0:T(8,128)(2,1)S(1)} all-to-all(bf16[8,16,896]{2,1,0:T(8,128)(2,1)S(1)} %down.1), channel_id=1, replica_groups=mesh['y'=8,'z'=8,'x'=8,'core'=2] {'x'}, dimensions={0} | all-to-all | bytes 458752 | tf_op jit(solution)/shard_map/all_to_all | solution.py:231
  129.4 0.3 spread.1
  129.7 21.7 %all_to_all.22.in_ref = bf16[64,2,1792]{2,1,0:T(2,128)(2,1)S(1)} all-to-all(bf16[64,2,1792]{2,1,0:T(2,128)(2,1)S(1)} %spread.1), channel_id=1, replica_groups=mesh['y'=8,'z'=8,'x'=8,'core'=2] {'y','z'}, dimensions={0} | all-to-all | bytes 917504 | tf_op jit(solution)/shard_map/all_to_all | solution.py:235
  151.4 0.0 copy-done.1
  151.4 1.8 %mix.1 = bf16[8,3584]{1,0:T(8,128)(2,1)} custom-call(bf16[64,2,1792]{2,1,0:T(2,128)(2,1)S(1)} %all_to_all.22.in_ref, bf16[64,8]{1,0:T(8,128)(2,1)S(1)} %copy-done.1), custom_call_target="tpu_custom_call" | custom-call | tf_op jit(solution)/shard_map/mix/pallas_call | solution.py:236
Async XLA Ops:
  0.0 32.5 %collective-permute-start = (bf16[224,2048]{1,0:T(8,128)(2,1)}, bf16[224,2048]{1,0:T(8,128)(2,1)S(1)}, u32[]{:S(2)}, u32[]{:S(2)}) collective-permute-start(bf16[224,2048]{1,0:T(8,128)(2,1)} %bitcast.8), channel_id=1, source_target_pairs={{0,2},{2,0},{4,6},{6,4},{8,10},{10,8},{12,14},{14,12},{1,3},{3,1},... | collective-permute-start | bytes 2752520 | tf_op jit(solution)/shard_map/ppermute | solution.py:198
  3.4 47.4 %collective-permute-start.1 = (bf16[3584,256]{1,0:T(8,128)(2,1)}, bf16[3584,256]{1,0:T(8,128)(2,1)}, u32[]{:S(2)}, u32[]{:S(2)}) collective-permute-start(bf16[3584,256]{1,0:T(8,128)(2,1)} %bitcast.11), channel_id=1, source_target_pairs={{0,1},{1,0},{2,3},{3,2},{4,5},{5,4},{6,7},{7,6},{8,9},{9,8},{10,11... | collective-permute-start | bytes 5505032 | tf_op jit(solution)/shard_map/ppermute | solution.py:199
  7.4 42.5 %all-to-all-start = ((bf16[64,2,1920]{2,1,0:T(2,128)(2,1)}), bf16[64,2,1920]{2,1,0:T(2,128)(2,1)S(1)}, u32[]{:S(2)}, u32[]{:S(2)}) async-start(bf16[64,2,1920]{2,1,0:T(2,128)(2,1)} %get-tuple-element.14), calls=%async_computation | async-start | bytes 983040 | tf_op jit(solution)/shard_map/all_to_all | solution.py:201
  30.5 4.6 %collective-permute-start.2 = (bf16[224,2048]{1,0:T(8,128)(2,1)}, bf16[224,2048]{1,0:T(8,128)(2,1)S(1)}, u32[]{:S(2)}, u32[]{:S(2)}) collective-permute-start(bf16[224,2048]{1,0:T(8,128)(2,1)} %bitcast.9), channel_id=1, source_target_pairs={{0,1},{1,0},{2,3},{3,2},{4,5},{5,4},{6,7},{7,6},{8,9},{9,8},{10,11... | collective-permute-start | bytes 2752520 | tf_op jit(solution)/shard_map/ppermute | solution.py:200
  32.5 17.4 %collective-permute-start.3 = (bf16[224,2048]{1,0:T(8,128)(2,1)S(1)}, bf16[224,2048]{1,0:T(8,128)(2,1)S(1)}, u32[]{:S(2)}, u32[]{:S(2)}) collective-permute-start(bf16[224,2048]{1,0:T(8,128)(2,1)S(1)} %collective-permute-done.pair_ref), channel_id=1, source_target_pairs={{0,1},{1,0},{2,3},{3,2},{4,5},{5,4},{6,7},{7,6},{8,9},{9,8},{10,11... | collective-permute-start | bytes 2752520 | tf_op jit(solution)/shard_map/ppermute | solution.py:202
  49.9 0.9 copy-start.2
  52.3 9.2 %collective-permute-start.4 = (bf16[32,3712]{1,0:T(8,128)(2,1)S(1)}, bf16[32,3712]{1,0:T(8,128)(2,1)S(1)}, u32[]{:S(2)}, u32[]{:S(2)}) collective-permute-start(bf16[32,3712]{1,0:T(8,128)(2,1)S(1)} %get-tuple-element.17.refs_3_), channel_id=1, source_target_pairs={{0,2},{2,4},{4,6},{6,8},{8,10},{10,12},{12,14},{14,0},{1,3},{3,5},... | collective-permute-start | bytes 712712 | tf_op jit(solution)/shard_map/ppermute | solution.py:45
  54.6 8.8 %collective-permute-start.5 = (bf16[32,3712]{1,0:T(8,128)(2,1)S(1)}, bf16[32,3712]{1,0:T(8,128)(2,1)S(1)}, u32[]{:S(2)}, u32[]{:S(2)}) collective-permute-start(bf16[32,3712]{1,0:T(8,128)(2,1)S(1)} %get-tuple-element.17.refs_3_), channel_id=1, source_target_pairs={{0,14},{2,0},{4,2},{6,4},{8,6},{10,8},{12,10},{14,12},{1,15},{3,1}... | collective-permute-start | bytes 712712 | tf_op jit(solution)/shard_map/ppermute | solution.py:46
  61.5 9.2 %collective-permute-start.6 = (bf16[32,3712]{1,0:T(8,128)(2,1)S(1)}, bf16[32,3712]{1,0:T(8,128)(2,1)S(1)}, u32[]{:S(2)}, u32[]{:S(2)}) collective-permute-start(bf16[32,3712]{1,0:T(8,128)(2,1)S(1)} %collective-permute-done.4.refs_4_), channel_id=1, source_target_pairs={{0,2},{2,4},{4,6},{6,8},{8,10},{10,12},{12,14},{14,0},{1,3},{3,5},... | collective-permute-start | bytes 712712 | tf_op jit(solution)/shard_map/ppermute | solution.py:45
  63.4 9.2 %collective-permute-start.7 = (bf16[32,3712]{1,0:T(8,128)(2,1)S(1)}, bf16[32,3712]{1,0:T(8,128)(2,1)S(1)}, u32[]{:S(2)}, u32[]{:S(2)}) collective-permute-start(bf16[32,3712]{1,0:T(8,128)(2,1)S(1)} %collective-permute-done.5.refs_5_), channel_id=1, source_target_pairs={{0,14},{2,0},{4,2},{6,4},{8,6},{10,8},{12,10},{14,12},{1,15},{3,1}... | collective-permute-start | bytes 712712 | tf_op jit(solution)/shard_map/ppermute | solution.py:46
  70.7 9.2 %collective-permute-start.8 = (bf16[32,3712]{1,0:T(8,128)(2,1)S(1)}, bf16[32,3712]{1,0:T(8,128)(2,1)S(1)}, u32[]{:S(2)}, u32[]{:S(2)}) collective-permute-start(bf16[32,3712]{1,0:T(8,128)(2,1)S(1)} %collective-permute-done.6.refs_6_), channel_id=1, source_target_pairs={{0,2},{2,4},{4,6},{6,8},{8,10},{10,12},{12,14},{14,0},{1,3},{3,5},... | collective-permute-start | bytes 712712 | tf_op jit(solution)/shard_map/ppermute | solution.py:45
  72.6 9.3 %collective-permute-start.9 = (bf16[32,3712]{1,0:T(8,128)(2,1)S(1)}, bf16[32,3712]{1,0:T(8,128)(2,1)S(1)}, u32[]{:S(2)}, u32[]{:S(2)}) collective-permute-start(bf16[32,3712]{1,0:T(8,128)(2,1)S(1)} %collective-permute-done.7.refs_7_), channel_id=1, source_target_pairs={{0,14},{2,0},{4,2},{6,4},{8,6},{10,8},{12,10},{14,12},{1,15},{3,1}... | collective-permute-start | bytes 712712 | tf_op jit(solution)/shard_map/ppermute | solution.py:46
  79.9 9.3 %collective-permute-start.10 = (bf16[32,3712]{1,0:T(8,128)(2,1)S(1)}, bf16[32,3712]{1,0:T(8,128)(2,1)}, u32[]{:S(2)}, u32[]{:S(2)}) collective-permute-start(bf16[32,3712]{1,0:T(8,128)(2,1)S(1)} %collective-permute-done.8.refs_8_), channel_id=1, source_target_pairs={{0,2},{2,4},{4,6},{6,8},{8,10},{10,12},{12,14},{14,0},{1,3},{3,5},... | collective-permute-start | bytes 712712 | tf_op jit(solution)/shard_map/ppermute | solution.py:48
  81.9 31.0 %copy-start = (bf16[1,2048,224]{1,2,0:T(8,128)(2,1)S(1)}, bf16[1,2048,224]{1,2,0:T(8,128)(2,1)}, u32[]{:S(2)}) copy-start(bf16[1,2048,224]{1,2,0:T(8,128)(2,1)} %param.9) | copy-start | bytes 2752516
  116.8 34.6 %copy-start.1 = (bf16[64,8]{1,0:T(8,128)(2,1)S(1)}, bf16[64,8]{1,0:T(8,128)(2,1)}, u32[]{:S(2)}) copy-start(bf16[64,8]{1,0:T(8,128)(2,1)} %get-tuple-element.22.place_ref) | copy-start | bytes 3076

commit v4 on v3

--- a/solution.py
+++ b/solution.py
@@ -1,3 +1,5 @@
+import functools
+
 import jax
 import jax.numpy as jnp
 from jax import lax
@@ -13,6 +15,7 @@
 HBM = pl.BlockSpec(memory_space=pltpu.HBM)
 CHUNKS = 4
 HID = 50
+LAST = 60
 DOWN = 50
 
 
@@ -70,6 +73,15 @@
         send_ref[:, h, half:] = tail.astype(bf16)
 
 
+def by_half(hot):
+    slots, k = hot.shape
+    twice = jnp.broadcast_to(hot[:, None, :], (slots, 2, k)).reshape(2 * slots, k)
+    parity = lax.broadcasted_iota(i32, (2 * slots, k), 0) % 2
+    return jnp.concatenate([jnp.where(parity == h, twice, 0.0) for h in range(2)], axis=1).astype(
+        bf16
+    )
+
+
 def compact_kernel(in_ref, rows_ref, select_ref):
     groups, _, wide = in_ref.shape
     half = wide - LANES
@@ -81,70 +93,71 @@
     upto = dot((high <= low).astype(bf16), live)[:, :1]
     alive = live[:, :1].astype(f32) > 0
     position = lax.broadcasted_iota(i32, (groups, count), 1).astype(f32) + 1.0
-    spread = jnp.where(alive & (upto == position), 1.0, 0.0).astype(bf16)
-    select_ref[...] = spread
-    for h in range(2):
-        rows_ref[:, h * half : (h + 1) * half] = dot_dims(
-            spread, in_ref[:, h, :half], 0, 0
-        ).astype(bf16)
-    rows_ref[:, 2 * half :] = dot_dims(spread, tail, 0, 0).astype(bf16)
+    spread = jnp.where(alive & (upto == position), 1.0, 0.0)
+    select_ref[...] = spread.astype(bf16)
+    both = dot_dims(by_half(spread), in_ref[...].reshape(2 * groups, wide), 0, 0).astype(bf16)
+    rows_ref[:, :half] = both[:count, :half]
+    rows_ref[:, half : 2 * half] = both[count:, :half]
+    rows_ref[:, 2 * half :] = both[:count, half:]
 
 
 def hidden_kernel(steps, at_ref, gu_ref, other_ref, *refs):
-    blocks, (out_ref, buf, sems) = refs[:-3], refs[-3:]
+    out_ref, buf, sems = refs[-3:]
     depth = gu_ref.shape[0] // CHUNKS
     copies = []
-    for i, w in enumerate((gu_ref, other_ref)):
-        for k in range(CHUNKS):
+    for k in range(CHUNKS):
+        for i, w in enumerate((gu_ref, other_ref)):
             part = pl.ds(k * depth, depth)
             copies.append(
                 pltpu.make_async_copy(w.at[part, :], buf.at[i, part, :], sems.at[i, k])
             )
             copies[-1].start()
-    n = len(blocks)
+    done = refs[0] if steps else None
+    blocks = refs[1:-3] if steps else refs[:-3]
     x, c = at_ref[0], at_ref[1]
     r = blocks[0].shape[0]
     width = gu_ref.shape[0]
     units = gu_ref.shape[1] // 2
-    hr = r // 2
     rows = jnp.concatenate([b[:, :width] for b in blocks], axis=0)
     tail = jnp.concatenate([b[:, width:] for b in blocks], axis=0).astype(f32)
-    gate = jnp.where(x < n // 2, tail[:, 0:1], tail[:, 1:2])
+    gate = jnp.where(at_ref[2] == 0, tail[:, 0:1], tail[:, 1:2])
+    prs = [0.0, 0.0]
+    for k in range(CHUNKS):
+        for i in range(2):
+            copies[2 * k + i].wait()
+            lo, hi = k * depth, (k + 1) * depth
+            prs[i] += dot(rows[:, lo:hi], buf[i, lo:hi, :])
     parts = []
-    for i in range(2):
-        pr = 0.0
-        for k in range(CHUNKS):
-            copies[i * CHUNKS + k].wait()
-            lo, hi = k * depth, (k + 1) * depth
-            pr += dot(rows[:, lo:hi], buf[i, lo:hi, :])
+    for pr in prs:
         g, p = pr[:, :units], pr[:, units:]
         parts.append((g / (1.0 + jnp.exp(-g)) * p * gate).astype(bf16))
     mine, other = parts
     first = jnp.where(c == 0, mine, other)
     second = jnp.where(c == 0, other, mine)
     h = jnp.concatenate([first, second], axis=1)
+    if not steps:
+        out_ref[...] = h
+        return
+    n, hr = len(steps), r // 2
     for j, k in enumerate(steps):
         owner = lax.rem(x + (n - k), n)
         at = pl.ds(pl.multiple_of(owner * hr, hr), hr)
-        for dest in range(n):
-            lo = j * r + (dest % 2) * hr
-            out_ref[dest, at, :] = h[lo : lo + hr]
-
-
-def down_kernel(at_ref, h_ref, own_ref, other_ref, pair_ref, both_ref, out_ref, buf, sems):
-    copies = [
-        pltpu.make_async_copy(w, buf.at[i], sems.at[i])
-        for i, w in enumerate((own_ref, other_ref, pair_ref, both_ref))
-    ]
-    for copy in copies:
-        copy.start()
+        for b in range(2):
+            if j < n - 1:
+                part = done[j * r + b * hr : j * r + (b + 1) * hr, :]
+            else:
+                part = h[b * hr : (b + 1) * hr]
+            for dest in range(b, n, 2):
+                out_ref[dest, at, :] = part
+
+
+def down_kernel(at_ref, h_ref, own_ref, other_ref, pair_ref, both_ref, out_ref):
     n, rows, units = h_ref.shape
     b, c = lax.rem(at_ref[0], 2), at_ref[1]
     h = jnp.concatenate([h_ref[k] for k in range(n)], axis=1)
-    parts = []
-    for i in range(4):
-        copies[i].wait()
-        parts.append(dot_dims(h, buf[i], 1, 1).astype(bf16))
+    parts = [
+        dot_dims(h, w[...], 1, 1).astype(bf16) for w in (own_ref, other_ref, pair_ref, both_ref)
+    ]
     hr = out_ref.shape[1]
     for bb in range(2):
         for cc in range(2):
@@ -169,11 +182,12 @@
 
 
 def mix_kernel(in_ref, place_ref, out_ref):
-    half = in_ref.shape[2]
-    for h in range(2):
-        out_ref[:, h * half : (h + 1) * half] = dot_dims(
-            place_ref[...], in_ref[:, h, :], 0, 0
-        ).astype(bf16)
+    slots, _, half = in_ref.shape
+    toks = out_ref.shape[0]
+    lhs = by_half(place_ref[...].astype(f32))
+    both = dot_dims(lhs, in_ref[...].reshape(2 * slots, half), 0, 0).astype(bf16)
+    out_ref[:, :half] = both[:toks]
+    out_ref[:, half:] = both[toks:]
 
 
 def shards(tokens, node_picks, gates, gate_up, down_weight):
@@ -183,7 +197,8 @@
     visits = node_picks.shape[1]
     r = toks * visits
     half = width // 2
-    at = jnp.stack([lax.axis_index("x"), lax.axis_index("core")]).astype(i32)
+    x = lax.axis_index("x")
+    at = jnp.stack([x, lax.axis_index("core"), x // (n // 2)]).astype(i32)
     gu, dn = gate_up[0], down_weight[0].T
     feats, units = dn.shape[0], dn.shape[1] // n
     swap = [(0, 1), (1, 0)]
@@ -200,8 +215,8 @@
     dn_other = lax.ppermute(dn, "core", swap)
     arrived = lax.all_to_all(send, group, split_axis=0, concat_axis=0, tiled=True)
     dn_both = lax.ppermute(dn_pair, "core", swap)
-    arrived, dn_pair, gu_other, dn_other, dn_both = lax.optimization_barrier(
-        (arrived, dn_pair, gu_other, dn_other, dn_both)
+    arrived, dn_pair, dn_other, dn_both = lax.optimization_barrier(
+        (arrived, dn_pair, dn_other, dn_both)
     )
     rows, select = call(
         compact_kernel,
@@ -211,22 +226,31 @@
     )(arrived)
     got = ring(rows, n)
     steps = tuple(k for k, _ in got)
+    *early, last = [b for _, b in got]
+    scratch = [pltpu.VMEM((2,) + gu.shape, bf16), pltpu.SemaphoreType.DMA((2, CHUNKS))]
+    (done,) = call(
+        functools.partial(hidden_kernel, ()),
+        [((len(early) * r, units), bf16)],
+        [SMEM, HBM, HBM] + [VMEM] * len(early),
+        "hidden_early",
+        scratch,
+        HID,
+    )(at, gu, gu_other, *early)
     (hid,) = call(
-        lambda *refs: hidden_kernel(steps, *refs),
+        functools.partial(hidden_kernel, steps),
         [((n, n * r // 2, units), bf16)],
-        [SMEM, HBM, HBM] + [VMEM] * n,
-        "hidden",
-        [pltpu.VMEM((2,) + gu.shape, bf16), pltpu.SemaphoreType.DMA((2, CHUNKS))],
-        HID,
-    )(at, gu, gu_other, *[b for _, b in got])
+        [SMEM, HBM, HBM] + [VMEM] * 2,
+        "hidden_last",
+        scratch,
+        LAST,
+    )(at, gu, gu_other, done, last)
     hid = lax.all_to_all(hid, "x", split_axis=0, concat_axis=0, tiled=True)
     (out,) = call(
         down_kernel,
         [((n, r // 2, 4 * feats), bf16)],
-        [SMEM, VMEM] + [HBM] * 4,
+        [SMEM] + [VMEM] * 5,
         "down",
-        [pltpu.VMEM((4,) + dn.shape, bf16), pltpu.SemaphoreType.DMA((4,))],
-        DOWN,
+        room=DOWN,
     )(at, hid, dn, dn_other, dn_pair, dn_both)
     back = lax.all_to_all(out, "x", split_axis=0, concat_axis=0, tiled=True)
     (padded,) = call(spread_kernel, [((groups, 2, half), bf16)], [VMEM] * 2, "spread")(

time: 154 us -> 149 us (0.968)
  waiting for transfers between devices: 28.8 us -> 19.7 us
  blocking collectives: 53.1 us -> 54.9 us
    ppermute x1, waiting for transfers between devices: 7.3 us -> 0.83 us  [ring(): got.append((n // 2, lax.ppermute(fwd, 'x', up)))]
    all_to_all x1, waiting for transfers between devices: 14.8 us -> 12.1 us  [shards(): lax.all_to_all(send, group, split_axis=0, concat_axis=0, tiled=True)]
    pallas_call x2 -> x3, Pallas kernels: 8.76 us -> 11.3 us  [the longest x1 4.39 us: shards(): call(functools.partial(hidden_kernel, steps), [((n, n * r // 2, units), b...]
    all_to_all x1, blocking collectives: 21.7 us -> 23.3 us  [shards(): lax.all_to_all(padded, group, split_axis=0, concat_axis=0, tiled=True)]
  transfers between devices with their start and end apart: 12 -> 12, of which waited for: 6 -> 5; matrix products, arithmetic and copies ran while one was open for 0% -> 0% of each run, Pallas kernels for 1% -> 5%
where the time goes in v4:
time: 149 us; the launch traced here: 148 us
  starting transfers between devices  55.8 us (37%)
  blocking collectives  54.9 us (37%)
  waiting for transfers between devices  19.7 us (13%)
  Pallas kernels  15.3 us (10%)
  local copies, waits for them, and re-layouts  2.15 us (1%)
    all_to_all x1, blocking collectives, shards(): lax.all_to_all(padded, group, split_axis=0, concat_axis=0, tiled=True)  23.3 us
    all_to_all x1, starting transfers between devices, shards(): lax.all_to_all(send, group, split_axis=0, concat_axis=0, tiled=True)  23.1 us
    all_to_all x1, blocking collectives, shards(): hid = lax.all_to_all(hid, 'x', split_axis=0, concat_axis=0, tiled=True)  19.1 us
    ppermute x3, starting transfers between devices, ring(): back = lax.ppermute(back, 'x', down)  14.9 us
    all_to_all x1, blocking collectives, shards(): back = lax.all_to_all(out, 'x', split_axis=0, concat_axis=0, tiled=True)  12.5 us
    all_to_all x1, waiting for transfers between devices, shards(): lax.all_to_all(send, group, split_axis=0, concat_axis=0, tiled=True)  12.1 us
    ppermute x3, waiting for transfers between devices, ring(): fwd = lax.ppermute(fwd, 'x', up)  6.71 us
    ppermute x3, starting transfers between devices, ring(): fwd = lax.ppermute(fwd, 'x', up)  6.2 us
  transfers between devices with their start and end apart: 12, of which 5 were waited for; matrix products, arithmetic and copies ran while one was open for 0% of the time, Pallas kernels for 5%

profile of v4, /device:TPU:32, one launch (start us, length us, event | category | flops | bytes accessed | tf_op | source)
XLA Modules:
  0.0 148.2 jit_solution(11388476179657570417)
XLA Ops:
  0.0 3.4 %collective-permute-start.1 = (bf16[224,2048]{1,0:T(8,128)(2,1)}, bf16[224,2048]{1,0:T(8,128)(2,1)S(1)}, u32[]{:S(2)}, u32[]{:S(2)}) collective-permute-start(bf16[224,2048]{1,0:T(8,128)(2,1)} %bitcast.12), channel_id=1, source_target_pairs={{0,2},{2,0},{4,6},{6,4},{8,10},{10,8},{12,14},{14,12},{1,3},{3,1},... | collective-permute-start | bytes 2752520 | tf_op jit(solution)/shard_map/ppermute | solution.py:213
  3.4 2.1 %pack.1 = (bf16[64,2,1920]{2,1,0:T(2,128)(2,1)}, bf16[64,8]{1,0:T(8,128)(2,1)}) custom-call(s32[4,8]{1,0:T(4,128)} %bitcast.15, bf16[4,2,8]{2,1,0:T(2,128)(2,1)} %bitcast.16, bf16[8,3584]{1,0:T(8,128)(2,1)} %tok_ref.1), custom_call_target="tpu_custom_call" | custom-call | tf_op jit(solution)/shard_map/pack/pallas_call | solution.py:206
  5.5 23.1 %all-to-all-start = ((bf16[64,2,1920]{2,1,0:T(2,128)(2,1)}), bf16[64,2,1920]{2,1,0:T(2,128)(2,1)S(1)}, u32[]{:S(2)}, u32[]{:S(2)}) async-start(bf16[64,2,1920]{2,1,0:T(2,128)(2,1)} %get-tuple-element.13), calls=%async_computation | async-start | bytes 983040 | tf_op jit(solution)/shard_map/all_to_all | solution.py:216
  28.6 1.9 %collective-permute-start.2 = (bf16[224,2048]{1,0:T(8,128)(2,1)}, bf16[224,2048]{1,0:T(8,128)(2,1)S(1)}, u32[]{:S(2)}, u32[]{:S(2)}) collective-permute-start(bf16[224,2048]{1,0:T(8,128)(2,1)} %bitcast.13), channel_id=1, source_target_pairs={{0,1},{1,0},{2,3},{3,2},{4,5},{5,4},{6,7},{7,6},{8,9},{9,8},{10,11... | collective-permute-start | bytes 2752520 | tf_op jit(solution)/shard_map/ppermute | solution.py:215
  30.5 0.0 collective-permute-done.1.pair_ref
  30.5 2.4 %collective-permute-start.3 = (bf16[224,2048]{1,0:T(8,128)(2,1)S(1)}, bf16[224,2048]{1,0:T(8,128)(2,1)S(1)}, u32[]{:S(2)}, u32[]{:S(2)}) collective-permute-start(bf16[224,2048]{1,0:T(8,128)(2,1)S(1)} %collective-permute-done.1.pair_ref), channel_id=1, source_target_pairs={{0,1},{1,0},{2,3},{3,2},{4,5},{5,4},{6,7},{7,6},{8,9},{9,8},{10,11... | collective-permute-start | bytes 2752520 | tf_op jit(solution)/shard_map/ppermute | solution.py:217
  32.9 1.9 %collective-permute-start = (bf16[3584,256]{1,0:T(8,128)(2,1)}, bf16[3584,256]{1,0:T(8,128)(2,1)}, u32[]{:S(2)}, u32[]{:S(2)}) collective-permute-start(bf16[3584,256]{1,0:T(8,128)(2,1)} %bitcast.9), channel_id=1, source_target_pairs={{0,1},{1,0},{2,3},{3,2},{4,5},{5,4},{6,7},{7,6},{8,9},{9,8},{10,11... | collective-permute-start | bytes 5505032 | tf_op jit(solution)/shard_map/ppermute | solution.py:214
  34.9 0.0 collective-permute-done.2.other_ref
  34.9 12.1 %all-to-all-done.in_ref = bf16[64,2,1920]{2,1,0:T(2,128)(2,1)S(1)} async-done(((bf16[64,2,1920]{2,1,0:T(2,128)(2,1)}), bf16[64,2,1920]{2,1,0:T(2,128)(2,1)S(1)}, u32[]{:S(2)}, u32[]{:S(2)}) %all-to-all-start) | async-done | bytes 491552 | tf_op jit(solution)/shard_map/all_to_all | solution.py:216
  47.0 0.0 collective-permute-done.3.both_ref
  47.0 0.0 copy-start.6
  47.0 0.6 compact.1
  47.7 2.4 %collective-permute-start.4 = (bf16[32,3712]{1,0:T(8,128)(2,1)S(1)}, bf16[32,3712]{1,0:T(8,128)(2,1)S(1)}, u32[]{:S(2)}, u32[]{:S(2)}) collective-permute-start(bf16[32,3712]{1,0:T(8,128)(2,1)S(1)} %get-tuple-element.15.refs_0_), channel_id=1, source_target_pairs={{0,2},{2,4},{4,6},{6,8},{8,10},{10,12},{12,14},{14,0},{1,3},{3,5},... | collective-permute-start | bytes 712712 | tf_op jit(solution)/shard_map/ppermute | solution.py:48
  50.0 4.7 %collective-permute-start.5 = (bf16[32,3712]{1,0:T(8,128)(2,1)S(1)}, bf16[32,3712]{1,0:T(8,128)(2,1)S(1)}, u32[]{:S(2)}, u32[]{:S(2)}) collective-permute-start(bf16[32,3712]{1,0:T(8,128)(2,1)S(1)} %get-tuple-element.15.refs_0_), channel_id=1, source_target_pairs={{0,14},{2,0},{4,2},{6,4},{8,6},{10,8},{12,10},{14,12},{1,15},{3,1}... | collective-permute-start | bytes 712712 | tf_op jit(solution)/shard_map/ppermute | solution.py:49
  54.7 0.0 copy-done.6
  54.7 2.1 %collective-permute-done.4.refs_1_ = bf16[32,3712]{1,0:T(8,128)(2,1)S(1)} collective-permute-done((bf16[32,3712]{1,0:T(8,128)(2,1)S(1)}, bf16[32,3712]{1,0:T(8,128)(2,1)S(1)}, u32[]{:S(2)}, u32[]{:S(2)}) %collective-permute-start.4) | collective-permute-done | bytes 237600 | tf_op jit(solution)/shard_map/ppermute | solution.py:48
  56.9 1.9 %collective-permute-start.6 = (bf16[32,3712]{1,0:T(8,128)(2,1)S(1)}, bf16[32,3712]{1,0:T(8,128)(2,1)S(1)}, u32[]{:S(2)}, u32[]{:S(2)}) collective-permute-start(bf16[32,3712]{1,0:T(8,128)(2,1)S(1)} %collective-permute-done.4.refs_1_), channel_id=1, source_target_pairs={{0,2},{2,4},{4,6},{6,8},{8,10},{10,12},{12,14},{14,0},{1,3},{3,5},... | collective-permute-start | bytes 712712 | tf_op jit(solution)/shard_map/ppermute | solution.py:48
  58.8 0.0 collective-permute-done.5.refs_2_
  58.8 5.1 %collective-permute-start.7 = (bf16[32,3712]{1,0:T(8,128)(2,1)S(1)}, bf16[32,3712]{1,0:T(8,128)(2,1)S(1)}, u32[]{:S(2)}, u32[]{:S(2)}) collective-permute-start(bf16[32,3712]{1,0:T(8,128)(2,1)S(1)} %collective-permute-done.5.refs_2_), channel_id=1, source_target_pairs={{0,14},{2,0},{4,2},{6,4},{8,6},{10,8},{12,10},{14,12},{1,15},{3,1}... | collective-permute-start | bytes 712712 | tf_op jit(solution)/shard_map/ppermute | solution.py:49
  63.9 2.1 %collective-permute-done.6.refs_3_ = bf16[32,3712]{1,0:T(8,128)(2,1)S(1)} collective-permute-done((bf16[32,3712]{1,0:T(8,128)(2,1)S(1)}, bf16[32,3712]{1,0:T(8,128)(2,1)S(1)}, u32[]{:S(2)}, u32[]{:S(2)}) %collective-permute-start.6) | collective-permute-done | bytes 237600 | tf_op jit(solution)/shard_map/ppermute | solution.py:48
  66.1 1.9 %collective-permute-start.8 = (bf16[32,3712]{1,0:T(8,128)(2,1)S(1)}, bf16[32,3712]{1,0:T(8,128)(2,1)S(1)}, u32[]{:S(2)}, u32[]{:S(2)}) collective-permute-start(bf16[32,3712]{1,0:T(8,128)(2,1)S(1)} %collective-permute-done.6.refs_3_), channel_id=1, source_target_pairs={{0,2},{2,4},{4,6},{6,8},{8,10},{10,12},{12,14},{14,0},{1,3},{3,5},... | collective-permute-start | bytes 712712 | tf_op jit(solution)/shard_map/ppermute | solution.py:48
  68.0 0.0 collective-permute-done.7.refs_4_
  68.0 5.1 %collective-permute-start.9 = (bf16[32,3712]{1,0:T(8,128)(2,1)S(1)}, bf16[32,3712]{1,0:T(8,128)(2,1)S(1)}, u32[]{:S(2)}, u32[]{:S(2)}) collective-permute-start(bf16[32,3712]{1,0:T(8,128)(2,1)S(1)} %collective-permute-done.7.refs_4_), channel_id=1, source_target_pairs={{0,14},{2,0},{4,2},{6,4},{8,6},{10,8},{12,10},{14,12},{1,15},{3,1}... | collective-permute-start | bytes 712712 | tf_op jit(solution)/shard_map/ppermute | solution.py:49
  73.1 2.4 %collective-permute-done.8.refs_5_ = bf16[32,3712]{1,0:T(8,128)(2,1)S(1)} collective-permute-done((bf16[32,3712]{1,0:T(8,128)(2,1)S(1)}, bf16[32,3712]{1,0:T(8,128)(2,1)S(1)}, u32[]{:S(2)}, u32[]{:S(2)}) %collective-permute-start.8) | collective-permute-done | bytes 237600 | tf_op jit(solution)/shard_map/ppermute | solution.py:48
  75.6 1.9 %collective-permute-start.10 = (bf16[32,3712]{1,0:T(8,128)(2,1)S(1)}, bf16[32,3712]{1,0:T(8,128)(2,1)}, u32[]{:S(2)}, u32[]{:S(2)}) collective-permute-start(bf16[32,3712]{1,0:T(8,128)(2,1)S(1)} %collective-permute-done.8.refs_5_), channel_id=1, source_target_pairs={{0,2},{2,4},{4,6},{6,8},{8,10},{10,12},{12,14},{14,0},{1,3},{3,5},... | collective-permute-start | bytes 712712 | tf_op jit(solution)/shard_map/ppermute | solution.py:51
  77.5 0.1 pad_add_fusion.at_ref
  77.6 0.0 copy-start.4
  77.6 0.0 collective-permute-done.other_ref
  77.6 0.0 collective-permute-done.9.refs_6_
  77.6 0.0 copy-start
  77.6 1.5 %copy-done = bf16[1,3584,256]{2,1,0:T(8,128)(2,1)S(1)} copy-done((bf16[1,3584,256]{2,1,0:T(8,128)(2,1)S(1)}, bf16[1,3584,256]{2,1,0:T(8,128)(2,1)}, u32[]{:S(2)}) %copy-start) | copy-done | bytes 1835032
  79.1 4.3 %hidden_early.1.refs_0_ = bf16[224,256]{1,0:T(8,128)(2,1)S(1)} custom-call(s32[3]{0:T(128)S(1)} %pad_add_fusion.at_ref, bf16[3584,256]{1,0:T(8,128)(2,1)S(1)} %bitcast.11, bf16[3584,256]{1,0:T(8,128)(2,1)} %collective-permute-done.other_ref, bf16[32,3712]{1,0:T(8,128)(2,1)S(1)} %get-tuple-element.15.refs_0_, ...), custom_call_target="tpu_custom_call" | custom-call | tf_op jit(solution)/shard_map/hidden_early/pallas_call | solution.py:231
  83.4 0.0 copy-done.4
  83.4 0.0 copy-start.2
  83.4 0.6 copy-done.2
  84.0 0.0 copy-start.1
  84.1 0.8 collective-permute-done.10.refs_1_
  84.9 0.0 copy-start.5
  84.9 4.4 %hidden_last.1 = bf16[8,128,256]{2,1,0:T(8,128)(2,1)} custom-call(s32[3]{0:T(128)} %copy-done.4, bf16[3584,256]{1,0:T(8,128)(2,1)} %bitcast.10, bf16[3584,256]{1,0:T(8,128)(2,1)} %collective-permute-done.other_ref, bf16[224,256]{1,0:T(8,128)(2,1)} %copy-done.2, bf16[32,3712]{1,0:T(8,128)(2,1)} %collective-permute-done.10.refs_1_), custom_call_target="tpu_custom_call" | custom-call | tf_op jit(solution)/shard_map/hidden_last/pallas_call | solution.py:239
  89.3 19.1 %all_to_all.20.h_ref = bf16[8,128,256]{2,1,0:T(8,128)(2,1)S(1)} all-to-all(bf16[8,128,256]{2,1,0:T(8,128)(2,1)} %hidden_last.1), channel_id=1, replica_groups=mesh['y'=8,'z'=8,'x'=8,'core'=2] {'x'}, dimensions={0} | all-to-all | bytes 1048576 | tf_op jit(solution)/shard_map/all_to_all | solution.py:247
  108.4 0.0 copy-done.1
  108.4 0.0 copy-done.5
  108.4 2.7 %down.1 = bf16[8,16,896]{2,1,0:T(8,128)(2,1)S(1)} custom-call(s32[3]{0:T(128)S(1)} %copy-done.5, bf16[8,128,256]{2,1,0:T(8,128)(2,1)S(1)} %all_to_all.20.h_ref, bf16[224,2048]{1,0:T(8,128)(2,1)S(1)} %bitcast.14, bf16[224,2048]{1,0:T(8,128)(2,1)S(1)} %collective-permute-done.2.other_ref, bf16[224,2048]{1,0:T(8,128)(2,1)S(1)} %collective-permute-done.1.pair_ref, ...), custom_call_target="tpu_custom_call" | custom-call | tf_op jit(solution)/shard_map/down/pallas_call | solution.py:248
  111.1 0.0 copy-start.3
  111.1 12.5 %all_to_all.21.back_ref = bf16[8,16,896]{2,1,0:T(8,128)(2,1)S(1)} all-to-all(bf16[8,16,896]{2,1,0:T(8,128)(2,1)S(1)} %down.1), channel_id=1, replica_groups=mesh['y'=8,'z'=8,'x'=8,'core'=2] {'x'}, dimensions={0} | all-to-all | bytes 458752 | tf_op jit(solution)/shard_map/all_to_all | solution.py:255
  123.6 0.3 spread.1
  123.9 23.3 %all_to_all.22.in_ref = bf16[64,2,1792]{2,1,0:T(2,128)(2,1)S(1)} all-to-all(bf16[64,2,1792]{2,1,0:T(2,128)(2,1)S(1)} %spread.1), channel_id=1, replica_groups=mesh['y'=8,'z'=8,'x'=8,'core'=2] {'y','z'}, dimensions={0} | all-to-all | bytes 917504 | tf_op jit(solution)/shard_map/all_to_all | solution.py:259
  147.2 0.0 copy-done.3
  147.2 0.9 mix.1
Async XLA Ops:
  0.0 30.5 %collective-permute-start.1 = (bf16[224,2048]{1,0:T(8,128)(2,1)}, bf16[224,2048]{1,0:T(8,128)(2,1)S(1)}, u32[]{:S(2)}, u32[]{:S(2)}) collective-permute-start(bf16[224,2048]{1,0:T(8,128)(2,1)} %bitcast.12), channel_id=1, source_target_pairs={{0,2},{2,0},{4,6},{6,4},{8,10},{10,8},{12,14},{14,12},{1,3},{3,1},... | collective-permute-start | bytes 2752520 | tf_op jit(solution)/shard_map/ppermute | solution.py:213
  5.5 41.6 %all-to-all-start = ((bf16[64,2,1920]{2,1,0:T(2,128)(2,1)}), bf16[64,2,1920]{2,1,0:T(2,128)(2,1)S(1)}, u32[]{:S(2)}, u32[]{:S(2)}) async-start(bf16[64,2,1920]{2,1,0:T(2,128)(2,1)} %get-tuple-element.13), calls=%async_computation | async-start | bytes 983040 | tf_op jit(solution)/shard_map/all_to_all | solution.py:216
  28.6 6.3 %collective-permute-start.2 = (bf16[224,2048]{1,0:T(8,128)(2,1)}, bf16[224,2048]{1,0:T(8,128)(2,1)S(1)}, u32[]{:S(2)}, u32[]{:S(2)}) collective-permute-start(bf16[224,2048]{1,0:T(8,128)(2,1)} %bitcast.13), channel_id=1, source_target_pairs={{0,1},{1,0},{2,3},{3,2},{4,5},{5,4},{6,7},{7,6},{8,9},{9,8},{10,11... | collective-permute-start | bytes 2752520 | tf_op jit(solution)/shard_map/ppermute | solution.py:215
  30.5 16.5 %collective-permute-start.3 = (bf16[224,2048]{1,0:T(8,128)(2,1)S(1)}, bf16[224,2048]{1,0:T(8,128)(2,1)S(1)}, u32[]{:S(2)}, u32[]{:S(2)}) collective-permute-start(bf16[224,2048]{1,0:T(8,128)(2,1)S(1)} %collective-permute-done.1.pair_ref), channel_id=1, source_target_pairs={{0,1},{1,0},{2,3},{3,2},{4,5},{5,4},{6,7},{7,6},{8,9},{9,8},{10,11... | collective-permute-start | bytes 2752520 | tf_op jit(solution)/shard_map/ppermute | solution.py:217
  32.9 44.6 %collective-permute-start = (bf16[3584,256]{1,0:T(8,128)(2,1)}, bf16[3584,256]{1,0:T(8,128)(2,1)}, u32[]{:S(2)}, u32[]{:S(2)}) collective-permute-start(bf16[3584,256]{1,0:T(8,128)(2,1)} %bitcast.9), channel_id=1, source_target_pairs={{0,1},{1,0},{2,3},{3,2},{4,5},{5,4},{6,7},{7,6},{8,9},{9,8},{10,11... | collective-permute-start | bytes 5505032 | tf_op jit(solution)/shard_map/ppermute | solution.py:214
  47.0 7.7 %copy-start.6 = (bf16[224,2048]{1,0:T(8,128)(2,1)}, bf16[224,2048]{1,0:T(8,128)(2,1)S(1)}, u32[]{:S(2)}) copy-start(bf16[224,2048]{1,0:T(8,128)(2,1)S(1)} %collective-permute-done.3.both_ref) | copy-start | bytes 2752516
  47.7 9.2 %collective-permute-start.4 = (bf16[32,3712]{1,0:T(8,128)(2,1)S(1)}, bf16[32,3712]{1,0:T(8,128)(2,1)S(1)}, u32[]{:S(2)}, u32[]{:S(2)}) collective-permute-start(bf16[32,3712]{1,0:T(8,128)(2,1)S(1)} %get-tuple-element.15.refs_0_), channel_id=1, source_target_pairs={{0,2},{2,4},{4,6},{6,8},{8,10},{10,12},{12,14},{14,0},{1,3},{3,5},... | collective-permute-start | bytes 712712 | tf_op jit(solution)/shard_map/ppermute | solution.py:48
  50.0 8.7 %collective-permute-start.5 = (bf16[32,3712]{1,0:T(8,128)(2,1)S(1)}, bf16[32,3712]{1,0:T(8,128)(2,1)S(1)}, u32[]{:S(2)}, u32[]{:S(2)}) collective-permute-start(bf16[32,3712]{1,0:T(8,128)(2,1)S(1)} %get-tuple-element.15.refs_0_), channel_id=1, source_target_pairs={{0,14},{2,0},{4,2},{6,4},{8,6},{10,8},{12,10},{14,12},{1,15},{3,1}... | collective-permute-start | bytes 712712 | tf_op jit(solution)/shard_map/ppermute | solution.py:49
  56.9 9.2 %collective-permute-start.6 = (bf16[32,3712]{1,0:T(8,128)(2,1)S(1)}, bf16[32,3712]{1,0:T(8,128)(2,1)S(1)}, u32[]{:S(2)}, u32[]{:S(2)}) collective-permute-start(bf16[32,3712]{1,0:T(8,128)(2,1)S(1)} %collective-permute-done.4.refs_1_), channel_id=1, source_target_pairs={{0,2},{2,4},{4,6},{6,8},{8,10},{10,12},{12,14},{14,0},{1,3},{3,5},... | collective-permute-start | bytes 712712 | tf_op jit(solution)/shard_map/ppermute | solution.py:48
  58.8 9.2 %collective-permute-start.7 = (bf16[32,3712]{1,0:T(8,128)(2,1)S(1)}, bf16[32,3712]{1,0:T(8,128)(2,1)S(1)}, u32[]{:S(2)}, u32[]{:S(2)}) collective-permute-start(bf16[32,3712]{1,0:T(8,128)(2,1)S(1)} %collective-permute-done.5.refs_2_), channel_id=1, source_target_pairs={{0,14},{2,0},{4,2},{6,4},{8,6},{10,8},{12,10},{14,12},{1,15},{3,1}... | collective-permute-start | bytes 712712 | tf_op jit(solution)/shard_map/ppermute | solution.py:49
  66.1 9.5 %collective-permute-start.8 = (bf16[32,3712]{1,0:T(8,128)(2,1)S(1)}, bf16[32,3712]{1,0:T(8,128)(2,1)S(1)}, u32[]{:S(2)}, u32[]{:S(2)}) collective-permute-start(bf16[32,3712]{1,0:T(8,128)(2,1)S(1)} %collective-permute-done.6.refs_3_), channel_id=1, source_target_pairs={{0,2},{2,4},{4,6},{6,8},{8,10},{10,12},{12,14},{14,0},{1,3},{3,5},... | collective-permute-start | bytes 712712 | tf_op jit(solution)/shard_map/ppermute | solution.py:48
  68.0 9.6 %collective-permute-start.9 = (bf16[32,3712]{1,0:T(8,128)(2,1)S(1)}, bf16[32,3712]{1,0:T(8,128)(2,1)S(1)}, u32[]{:S(2)}, u32[]{:S(2)}) collective-permute-start(bf16[32,3712]{1,0:T(8,128)(2,1)S(1)} %collective-permute-done.7.refs_4_), channel_id=1, source_target_pairs={{0,14},{2,0},{4,2},{6,4},{8,6},{10,8},{12,10},{14,12},{1,15},{3,1}... | collective-permute-start | bytes 712712 | tf_op jit(solution)/shard_map/ppermute | solution.py:49
  75.6 9.3 %collective-permute-start.10 = (bf16[32,3712]{1,0:T(8,128)(2,1)S(1)}, bf16[32,3712]{1,0:T(8,128)(2,1)}, u32[]{:S(2)}, u32[]{:S(2)}) collective-permute-start(bf16[32,3712]{1,0:T(8,128)(2,1)S(1)} %collective-permute-done.8.refs_5_), channel_id=1, source_target_pairs={{0,2},{2,4},{4,6},{6,8},{8,10},{10,12},{12,14},{14,0},{1,3},{3,5},... | collective-permute-start | bytes 712712 | tf_op jit(solution)/shard_map/ppermute | solution.py:51
  77.6 5.8 %copy-start.4 = (s32[3]{0:T(128)}, s32[3]{0:T(128)S(1)}, u32[]{:S(2)}) copy-start(s32[3]{0:T(128)S(1)} %pad_add_fusion.at_ref) | copy-start | bytes 40
  77.6 1.5 %copy-start = (bf16[1,3584,256]{2,1,0:T(8,128)(2,1)S(1)}, bf16[1,3584,256]{2,1,0:T(8,128)(2,1)}, u32[]{:S(2)}) copy-start(bf16[1,3584,256]{2,1,0:T(8,128)(2,1)} %param.8) | copy-start | bytes 5505028
  83.4 0.6 copy-start.2
  84.0 24.3 %copy-start.1 = (bf16[1,2048,224]{1,2,0:T(8,128)(2,1)S(1)}, bf16[1,2048,224]{1,2,0:T(8,128)(2,1)}, u32[]{:S(2)}) copy-start(bf16[1,2048,224]{1,2,0:T(8,128)(2,1)} %param.9) | copy-start | bytes 2752516
  84.9 23.5 %copy-start.5 = (s32[3]{0:T(128)S(1)}, s32[3]{0:T(128)}, u32[]{:S(2)}) copy-start(s32[3]{0:T(128)} %copy-done.4) | copy-start | bytes 40
  111.1 36.2 %copy-start.3 = (bf16[64,8]{1,0:T(8,128)(2,1)S(1)}, bf16[64,8]{1,0:T(8,128)(2,1)}, u32[]{:S(2)}) copy-start(bf16[64,8]{1,0:T(8,128)(2,1)} %get-tuple-element.20.place_ref) | copy-start | bytes 3076

commit v5 on v4

--- a/solution.py
+++ b/solution.py
@@ -13,10 +13,9 @@
 VMEM = pl.BlockSpec(memory_space=pltpu.VMEM)
 SMEM = pl.BlockSpec(memory_space=pltpu.SMEM)
 HBM = pl.BlockSpec(memory_space=pltpu.HBM)
-CHUNKS = 4
 HID = 50
-LAST = 60
 DOWN = 50
+BESIDE = 2
 
 
 def dot(a, b):
@@ -39,7 +38,7 @@
     )
 
 
-def ring(block, n):
+def ring(block, n, beside):
     up = [(i, (i + 1) % n) for i in range(n)]
     down = [(i, (i - 1) % n) for i in range(n)]
     got = [(0, block)]
@@ -47,9 +46,11 @@
     for k in range(1, n // 2):
         fwd = lax.ppermute(fwd, "x", up)
         back = lax.ppermute(back, "x", down)
+        if k == BESIDE:
+            fwd, back, beside = lax.optimization_barrier((fwd, back, beside))
         got += [(k, fwd), (n - k, back)]
     got.append((n // 2, lax.ppermute(fwd, "x", up)))
-    return got
+    return got, beside
 
 
 def pack_kernel(picks_ref, gates_ref, tok_ref, send_ref, place_ref):
@@ -102,53 +103,36 @@
 
 
 def hidden_kernel(steps, at_ref, gu_ref, other_ref, *refs):
-    out_ref, buf, sems = refs[-3:]
-    depth = gu_ref.shape[0] // CHUNKS
+    blocks, (out_ref, buf, sems) = refs[:-3], refs[-3:]
     copies = []
-    for k in range(CHUNKS):
-        for i, w in enumerate((gu_ref, other_ref)):
-            part = pl.ds(k * depth, depth)
-            copies.append(
-                pltpu.make_async_copy(w.at[part, :], buf.at[i, part, :], sems.at[i, k])
-            )
-            copies[-1].start()
-    done = refs[0] if steps else None
-    blocks = refs[1:-3] if steps else refs[:-3]
+    for i, w in enumerate((gu_ref, other_ref)):
+        copies.append(pltpu.make_async_copy(w, buf.at[i], sems.at[i]))
+        copies[-1].start()
+    n = len(blocks)
     x, c = at_ref[0], at_ref[1]
     r = blocks[0].shape[0]
     width = gu_ref.shape[0]
     units = gu_ref.shape[1] // 2
+    hr = r // 2
     rows = jnp.concatenate([b[:, :width] for b in blocks], axis=0)
     tail = jnp.concatenate([b[:, width:] for b in blocks], axis=0).astype(f32)
     gate = jnp.where(at_ref[2] == 0, tail[:, 0:1], tail[:, 1:2])
-    prs = [0.0, 0.0]
-    for k in range(CHUNKS):
-        for i in range(2):
-            copies[2 * k + i].wait()
-            lo, hi = k * depth, (k + 1) * depth
-            prs[i] += dot(rows[:, lo:hi], buf[i, lo:hi, :])
     parts = []
-    for pr in prs:
+    for i in range(2):
+        copies[i].wait()
+        pr = dot(rows, buf[i])
         g, p = pr[:, :units], pr[:, units:]
         parts.append((g / (1.0 + jnp.exp(-g)) * p * gate).astype(bf16))
     mine, other = parts
     first = jnp.where(c == 0, mine, other)
     second = jnp.where(c == 0, other, mine)
     h = jnp.concatenate([first, second], axis=1)
-    if not steps:
-        out_ref[...] = h
-        return
-    n, hr = len(steps), r // 2
     for j, k in enumerate(steps):
         owner = lax.rem(x + (n - k), n)
         at = pl.ds(pl.multiple_of(owner * hr, hr), hr)
-        for b in range(2):
-            if j < n - 1:
-                part = done[j * r + b * hr : j * r + (b + 1) * hr, :]
-            else:
-                part = h[b * hr : (b + 1) * hr]
-            for dest in range(b, n, 2):
-                out_ref[dest, at, :] = part
+        for dest in range(n):
+            lo = j * r + (dest % 2) * hr
+            out_ref[dest, at, :] = h[lo : lo + hr]
 
 
 def down_kernel(at_ref, h_ref, own_ref, other_ref, pair_ref, both_ref, out_ref):
@@ -212,38 +196,26 @@
     )(node_picks.T, gates.transpose(1, 2, 0), tokens)
     dn_pair = lax.ppermute(dn, "x", pair)
     gu_other = lax.ppermute(gu, "core", swap)
-    dn_other = lax.ppermute(dn, "core", swap)
     arrived = lax.all_to_all(send, group, split_axis=0, concat_axis=0, tiled=True)
-    dn_both = lax.ppermute(dn_pair, "core", swap)
-    arrived, dn_pair, dn_other, dn_both = lax.optimization_barrier(
-        (arrived, dn_pair, dn_other, dn_both)
-    )
     rows, select = call(
         compact_kernel,
         [((r, width + LANES), bf16), ((groups, r), bf16)],
         [VMEM],
         "compact",
     )(arrived)
-    got = ring(rows, n)
+    got, dn_pair = ring(rows, n, dn_pair)
     steps = tuple(k for k, _ in got)
-    *early, last = [b for _, b in got]
-    scratch = [pltpu.VMEM((2,) + gu.shape, bf16), pltpu.SemaphoreType.DMA((2, CHUNKS))]
-    (done,) = call(
-        functools.partial(hidden_kernel, ()),
-        [((len(early) * r, units), bf16)],
-        [SMEM, HBM, HBM] + [VMEM] * len(early),
-        "hidden_early",
-        scratch,
-        HID,
-    )(at, gu, gu_other, *early)
     (hid,) = call(
         functools.partial(hidden_kernel, steps),
         [((n, n * r // 2, units), bf16)],
-        [SMEM, HBM, HBM] + [VMEM] * 2,
-        "hidden_last",
-        scratch,
-        LAST,
-    )(at, gu, gu_other, done, last)
+        [SMEM, HBM, HBM] + [VMEM] * n,
+        "hidden",
+        [pltpu.VMEM((2,) + gu.shape, bf16), pltpu.SemaphoreType.DMA((2,))],
+        HID,
+    )(at, gu, gu_other, *[b for _, b in got])
+    hid, mine, dn_pair = lax.optimization_barrier((hid, dn, dn_pair))
+    dn_other = lax.ppermute(mine, "core", swap)
+    dn_both = lax.ppermute(dn_pair, "core", swap)
     hid = lax.all_to_all(hid, "x", split_axis=0, concat_axis=0, tiled=True)
     (out,) = call(
         down_kernel,

time: 149 us -> 159 us (1.067)
  waiting for transfers between devices: 19.7 us -> 46.9 us
  blocking collectives: 54.9 us -> 39.6 us
  starting transfers between devices: 55.8 us -> 59.8 us
  Pallas kernels: 15.3 us -> 12 us
  local copies, waits for them, and re-layouts: 2.15 us -> 0.02 us
    all_to_all x1 -> x0, blocking collectives: 19.1 us -> none  [shards(): hid = lax.all_to_all(hid, 'x', split_axis=0, concat_axis=0, tiled=True)]
    all_to_all x0 -> x1, waiting for transfers between devices: none -> 10.1 us  [shards(): hid = lax.all_to_all(hid, 'x', split_axis=0, concat_axis=0, tiled=True)]
    ppermute x3, waiting for transfers between devices: 0.01 us -> 9.24 us  [ring(): back = lax.ppermute(back, 'x', down)]
    ppermute x1, waiting for transfers between devices: 0.83 us -> 7.29 us  [ring(): got.append((n // 2, lax.ppermute(fwd, 'x', up)))]
    all_to_all x0 -> x1, starting transfers between devices: none -> 5.55 us  [shards(): hid = lax.all_to_all(hid, 'x', split_axis=0, concat_axis=0, tiled=True)]
    pallas_call x1 -> x0, Pallas kernels: 4.29 us -> none  [shards(): call(functools.partial(hidden_kernel, ()), [((len(early) * r, units), bf1...]
    all_to_all x1, blocking collectives: 23.3 us -> 27 us  [shards(): lax.all_to_all(padded, group, split_axis=0, concat_axis=0, tiled=True)]
    unnamed x14 -> x8, local copies, waits for them, and re-layouts: 2.15 us -> 0.02 us
  transfers between devices with their start and end apart: 12 -> 13, of which waited for: 5 -> 7; matrix products, arithmetic and copies ran while one was open for 0% -> 0% of each run, Pallas kernels for 5% -> 0%
where the time goes in v5:
time: 159 us
  starting transfers between devices  59.8 us (38%)
  waiting for transfers between devices  46.9 us (29%)
  blocking collectives  39.6 us (25%)
  Pallas kernels  12 us (8%)
    all_to_all x1, blocking collectives, shards(): lax.all_to_all(padded, group, split_axis=0, concat_axis=0, tiled=True)  27 us
    all_to_all x1, starting transfers between devices, shards(): lax.all_to_all(send, group, split_axis=0, concat_axis=0, tiled=True)  23.1 us
    ppermute x3, starting transfers between devices, ring(): back = lax.ppermute(back, 'x', down)  13.6 us
    all_to_all x1, waiting for transfers between devices, shards(): lax.all_to_all(send, group, split_axis=0, concat_axis=0, tiled=True)  13.4 us
    all_to_all x1, blocking collectives, shards(): back = lax.all_to_all(out, 'x', split_axis=0, concat_axis=0, tiled=True)  12.5 us
    all_to_all x1, waiting for transfers between devices, shards(): hid = lax.all_to_all(hid, 'x', split_axis=0, concat_axis=0, tiled=True)  10.1 us
    ppermute x3, waiting for transfers between devices, ring(): back = lax.ppermute(back, 'x', down)  9.24 us
    ppermute x1, waiting for transfers between devices, ring(): got.append((n // 2, lax.ppermute(fwd, 'x', up)))  7.29 us
  transfers between devices with their start and end apart: 13, of which 7 were waited for; matrix products, arithmetic and copies ran while one was open for 0% of the time, Pallas kernels for 0%

profile of v5, /device:TPU:32, one launch (start us, length us, event | category | flops | bytes accessed | tf_op | source)
XLA Modules:
  0.0 158.6 jit_solution(13004661283915908171)
XLA Ops:
  0.0 2.0 %pack.1 = (bf16[64,2,1920]{2,1,0:T(2,128)(2,1)}, bf16[64,8]{1,0:T(8,128)(2,1)}) custom-call(s32[4,8]{1,0:T(4,128)} %bitcast.14, bf16[4,2,8]{2,1,0:T(2,128)(2,1)} %bitcast.15, bf16[8,3584]{1,0:T(8,128)(2,1)} %tok_ref.1), custom_call_target="tpu_custom_call" | custom-call | tf_op jit(solution)/shard_map/pack/pallas_call | solution.py:190
  2.0 23.1 %all-to-all-start = ((bf16[64,2,1920]{2,1,0:T(2,128)(2,1)}), bf16[64,2,1920]{2,1,0:T(2,128)(2,1)S(1)}, u32[]{:S(2)}, u32[]{:S(2)}) async-start(bf16[64,2,1920]{2,1,0:T(2,128)(2,1)} %get-tuple-element.15), calls=%async_computation | async-start | bytes 983040 | tf_op jit(solution)/shard_map/all_to_all | solution.py:199
  25.1 1.9 %collective-permute-start = (bf16[3584,256]{1,0:T(8,128)(2,1)}, bf16[3584,256]{1,0:T(8,128)(2,1)}, u32[]{:S(2)}, u32[]{:S(2)}) collective-permute-start(bf16[3584,256]{1,0:T(8,128)(2,1)} %bitcast.12), channel_id=1, source_target_pairs={{0,1},{1,0},{2,3},{3,2},{4,5},{5,4},{6,7},{7,6},{8,9},{9,8},{10,11... | collective-permute-start | bytes 5505032 | tf_op jit(solution)/shard_map/ppermute | solution.py:198
  27.1 3.4 %collective-permute-start.5 = (bf16[224,2048]{1,0:T(8,128)(2,1)}, bf16[224,2048]{1,0:T(8,128)(2,1)S(1)}, u32[]{:S(2)}, u32[]{:S(2)}) collective-permute-start(bf16[224,2048]{1,0:T(8,128)(2,1)} %bitcast.9), channel_id=1, source_target_pairs={{0,2},{2,0},{4,6},{6,4},{8,10},{10,8},{12,14},{14,12},{1,3},{3,1},... | collective-permute-start | bytes 2752520 | tf_op jit(solution)/shard_map/ppermute | solution.py:197
  30.5 13.4 %all-to-all-done.in_ref = bf16[64,2,1920]{2,1,0:T(2,128)(2,1)S(1)} async-done(((bf16[64,2,1920]{2,1,0:T(2,128)(2,1)}), bf16[64,2,1920]{2,1,0:T(2,128)(2,1)S(1)}, u32[]{:S(2)}, u32[]{:S(2)}) %all-to-all-start) | async-done | bytes 491552 | tf_op jit(solution)/shard_map/all_to_all | solution.py:199
  43.8 0.6 compact.1
  44.5 0.0 copy-start.2
  44.5 4.8 %collective-permute-start.2 = (bf16[32,3712]{1,0:T(8,128)(2,1)S(1)}, bf16[32,3712]{1,0:T(8,128)(2,1)S(1)}, u32[]{:S(2)}, u32[]{:S(2)}) collective-permute-start(bf16[32,3712]{1,0:T(8,128)(2,1)S(1)} %get-tuple-element.16.refs_0_), channel_id=1, source_target_pairs={{0,14},{2,0},{4,2},{6,4},{8,6},{10,8},{12,10},{14,12},{1,15},{3,1}... | collective-permute-start | bytes 712712 | tf_op jit(solution)/shard_map/ppermute | solution.py:48
  49.2 1.9 %collective-permute-start.1 = (bf16[32,3712]{1,0:T(8,128)(2,1)S(1)}, bf16[32,3712]{1,0:T(8,128)(2,1)S(1)}, u32[]{:S(2)}, u32[]{:S(2)}) collective-permute-start(bf16[32,3712]{1,0:T(8,128)(2,1)S(1)} %get-tuple-element.16.refs_0_), channel_id=1, source_target_pairs={{0,2},{2,4},{4,6},{6,8},{8,10},{10,12},{12,14},{14,0},{1,3},{3,5},... | collective-permute-start | bytes 712712 | tf_op jit(solution)/shard_map/ppermute | solution.py:47
  51.2 5.8 %collective-permute-done.2.refs_2_ = bf16[32,3712]{1,0:T(8,128)(2,1)S(1)} collective-permute-done((bf16[32,3712]{1,0:T(8,128)(2,1)S(1)}, bf16[32,3712]{1,0:T(8,128)(2,1)S(1)}, u32[]{:S(2)}, u32[]{:S(2)}) %collective-permute-start.2) | collective-permute-done | bytes 237600 | tf_op jit(solution)/shard_map/ppermute | solution.py:48
  57.0 3.7 %collective-permute-start.4 = (bf16[32,3712]{1,0:T(8,128)(2,1)S(1)}, bf16[32,3712]{1,0:T(8,128)(2,1)S(1)}, u32[]{:S(2)}, u32[]{:S(2)}) collective-permute-start(bf16[32,3712]{1,0:T(8,128)(2,1)S(1)} %collective-permute-done.2.refs_2_), channel_id=1, source_target_pairs={{0,14},{2,0},{4,2},{6,4},{8,6},{10,8},{12,10},{14,12},{1,15},{3,1}... | collective-permute-start | bytes 712712 | tf_op jit(solution)/shard_map/ppermute | solution.py:48
  60.7 0.0 collective-permute-done.1.refs_1_
  60.7 2.1 %collective-permute-start.3 = (bf16[32,3712]{1,0:T(8,128)(2,1)S(1)}, bf16[32,3712]{1,0:T(8,128)(2,1)S(1)}, u32[]{:S(2)}, u32[]{:S(2)}) collective-permute-start(bf16[32,3712]{1,0:T(8,128)(2,1)S(1)} %collective-permute-done.1.refs_1_), channel_id=1, source_target_pairs={{0,2},{2,4},{4,6},{6,8},{8,10},{10,12},{12,14},{14,0},{1,3},{3,5},... | collective-permute-start | bytes 712712 | tf_op jit(solution)/shard_map/ppermute | solution.py:47
  62.9 0.0 collective-permute-done.5.pair_ref
  62.9 3.4 %collective-permute-done.4.refs_4_ = bf16[32,3712]{1,0:T(8,128)(2,1)S(1)} collective-permute-done((bf16[32,3712]{1,0:T(8,128)(2,1)S(1)}, bf16[32,3712]{1,0:T(8,128)(2,1)S(1)}, u32[]{:S(2)}, u32[]{:S(2)}) %collective-permute-start.4) | collective-permute-done | bytes 237600 | tf_op jit(solution)/shard_map/ppermute | solution.py:48
  66.3 4.7 %collective-permute-done.3.refs_3_ = bf16[32,3712]{1,0:T(8,128)(2,1)S(1)} collective-permute-done((bf16[32,3712]{1,0:T(8,128)(2,1)S(1)}, bf16[32,3712]{1,0:T(8,128)(2,1)S(1)}, u32[]{:S(2)}, u32[]{:S(2)}) %collective-permute-start.3) | collective-permute-done | bytes 237600 | tf_op jit(solution)/shard_map/ppermute | solution.py:47
  71.0 1.9 %collective-permute-start.6 = (bf16[32,3712]{1,0:T(8,128)(2,1)S(1)}, bf16[32,3712]{1,0:T(8,128)(2,1)S(1)}, u32[]{:S(2)}, u32[]{:S(2)}) collective-permute-start(bf16[32,3712]{1,0:T(8,128)(2,1)S(1)} %collective-permute-done.3.refs_3_), channel_id=1, source_target_pairs={{0,2},{2,4},{4,6},{6,8},{8,10},{10,12},{12,14},{14,0},{1,3},{3,5},... | collective-permute-start | bytes 712712 | tf_op jit(solution)/shard_map/ppermute | solution.py:47
  72.9 5.1 %collective-permute-start.7 = (bf16[32,3712]{1,0:T(8,128)(2,1)S(1)}, bf16[32,3712]{1,0:T(8,128)(2,1)S(1)}, u32[]{:S(2)}, u32[]{:S(2)}) collective-permute-start(bf16[32,3712]{1,0:T(8,128)(2,1)S(1)} %collective-permute-done.4.refs_4_), channel_id=1, source_target_pairs={{0,14},{2,0},{4,2},{6,4},{8,6},{10,8},{12,10},{14,12},{1,15},{3,1}... | collective-permute-start | bytes 712712 | tf_op jit(solution)/shard_map/ppermute | solution.py:48
  78.0 2.2 %collective-permute-done.6.refs_5_ = bf16[32,3712]{1,0:T(8,128)(2,1)S(1)} collective-permute-done((bf16[32,3712]{1,0:T(8,128)(2,1)S(1)}, bf16[32,3712]{1,0:T(8,128)(2,1)S(1)}, u32[]{:S(2)}, u32[]{:S(2)}) %collective-permute-start.6) | collective-permute-done | bytes 237600 | tf_op jit(solution)/shard_map/ppermute | solution.py:47
  80.3 1.9 %collective-permute-start.8 = (bf16[32,3712]{1,0:T(8,128)(2,1)S(1)}, bf16[32,3712]{1,0:T(8,128)(2,1)}, u32[]{:S(2)}, u32[]{:S(2)}) collective-permute-start(bf16[32,3712]{1,0:T(8,128)(2,1)S(1)} %collective-permute-done.6.refs_5_), channel_id=1, source_target_pairs={{0,2},{2,4},{4,6},{6,8},{8,10},{10,12},{12,14},{14,0},{1,3},{3,5},... | collective-permute-start | bytes 712712 | tf_op jit(solution)/shard_map/ppermute | solution.py:52
  82.2 0.1 pad_add_fusion.at_ref
  82.3 0.0 copy-start
  82.3 0.0 collective-permute-done.7.refs_6_
  82.3 0.0 collective-permute-done.other_ref
  82.3 7.3 %collective-permute-done.8.refs_7_ = bf16[32,3712]{1,0:T(8,128)(2,1)} collective-permute-done((bf16[32,3712]{1,0:T(8,128)(2,1)S(1)}, bf16[32,3712]{1,0:T(8,128)(2,1)}, u32[]{:S(2)}, u32[]{:S(2)}) %collective-permute-start.8) | collective-permute-done | bytes 237600 | tf_op jit(solution)/shard_map/ppermute | solution.py:52
  89.6 5.5 %hidden.1 = bf16[8,128,256]{2,1,0:T(8,128)(2,1)} custom-call(s32[3]{0:T(128)S(1)} %pad_add_fusion.at_ref, bf16[3584,256]{1,0:T(8,128)(2,1)} %bitcast.13, bf16[3584,256]{1,0:T(8,128)(2,1)} %collective-permute-done.other_ref, bf16[32,3712]{1,0:T(8,128)(2,1)S(1)} %get-tuple-element.16.refs_0_, bf16[32,3712]{1,0:T(8,128)(2,1)S(1)} %collective-permute-done.1.refs_1_, ...), custom_call_target="tpu_custom_call" | custom-call | tf_op jit(solution)/shard_map/hidden/pallas_call | solution.py:208
  95.1 0.0 copy-done.2
  95.1 5.6 %all-to-all-start.1 = ((bf16[8,128,256]{2,1,0:T(8,128)(2,1)}), bf16[8,128,256]{2,1,0:T(8,128)(2,1)S(1)}, u32[]{:S(2)}, u32[]{:S(2)}) async-start(bf16[8,128,256]{2,1,0:T(8,128)(2,1)} %hidden.1), calls=%async_computation.1 | async-start | bytes 1048576 | tf_op jit(solution)/shard_map/all_to_all | solution.py:219
  100.6 0.0 copy-done
  100.6 0.0 copy-start.3
  100.6 1.9 %collective-permute-start.9 = (bf16[224,2048]{1,0:T(8,128)(2,1)S(1)}, bf16[224,2048]{1,0:T(8,128)(2,1)S(1)}, u32[]{:S(2)}, u32[]{:S(2)}) collective-permute-start(bf16[224,2048]{1,0:T(8,128)(2,1)S(1)} %bitcast.10), channel_id=1, source_target_pairs={{0,1},{1,0},{2,3},{3,2},{4,5},{5,4},{6,7},{7,6},{8,9},{9,8},{10,11... | collective-permute-start | bytes 2752520 | tf_op jit(solution)/shard_map/ppermute | solution.py:217
  102.6 2.4 %collective-permute-start.10 = (bf16[224,2048]{1,0:T(8,128)(2,1)S(1)}, bf16[224,2048]{1,0:T(8,128)(2,1)}, u32[]{:S(2)}, u32[]{:S(2)}) collective-permute-start(bf16[224,2048]{1,0:T(8,128)(2,1)S(1)} %collective-permute-done.5.pair_ref), channel_id=1, source_target_pairs={{0,1},{1,0},{2,3},{3,2},{4,5},{5,4},{6,7},{7,6},{8,9},{9,8},{10,11... | collective-permute-start | bytes 2752520 | tf_op jit(solution)/shard_map/ppermute | solution.py:218
  105.0 10.1 %all-to-all-done.1.h_ref = bf16[8,128,256]{2,1,0:T(8,128)(2,1)S(1)} async-done(((bf16[8,128,256]{2,1,0:T(8,128)(2,1)}), bf16[8,128,256]{2,1,0:T(8,128)(2,1)S(1)}, u32[]{:S(2)}, u32[]{:S(2)}) %all-to-all-start.1) | async-done | bytes 524320 | tf_op jit(solution)/shard_map/all_to_all | solution.py:219
  115.0 0.0 collective-permute-done.9.other_ref
  115.0 0.0 collective-permute-done.10.both_ref
  115.0 2.7 %down.1 = bf16[8,16,896]{2,1,0:T(8,128)(2,1)S(1)} custom-call(s32[3]{0:T(128)S(1)} %pad_add_fusion.at_ref, bf16[8,128,256]{2,1,0:T(8,128)(2,1)S(1)} %all-to-all-done.1.h_ref, bf16[224,2048]{1,0:T(8,128)(2,1)S(1)} %bitcast.11, bf16[224,2048]{1,0:T(8,128)(2,1)S(1)} %collective-permute-done.9.other_ref, bf16[224,2048]{1,0:T(8,128)(2,1)S(1)} %collective-permute-done.5.pair_ref, ...), custom_call_target="tpu_custom_call" | custom-call | tf_op jit(solution)/shard_map/down/pallas_call | solution.py:220
  117.7 0.0 copy-start.1
  117.7 12.5 %all_to_all.20.back_ref = bf16[8,16,896]{2,1,0:T(8,128)(2,1)S(1)} all-to-all(bf16[8,16,896]{2,1,0:T(8,128)(2,1)S(1)} %down.1), channel_id=1, replica_groups=mesh['y'=8,'z'=8,'x'=8,'core'=2] {'x'}, dimensions={0} | all-to-all | bytes 458752 | tf_op jit(solution)/shard_map/all_to_all | solution.py:227
  130.2 0.0 copy-done.3
  130.2 0.3 spread.1
  130.6 27.0 %all_to_all.21.in_ref = bf16[64,2,1792]{2,1,0:T(2,128)(2,1)S(1)} all-to-all(bf16[64,2,1792]{2,1,0:T(2,128)(2,1)S(1)} %spread.1), channel_id=1, replica_groups=mesh['y'=8,'z'=8,'x'=8,'core'=2] {'y','z'}, dimensions={0} | all-to-all | bytes 917504 | tf_op jit(solution)/shard_map/all_to_all | solution.py:231
  157.6 0.0 copy-done.1
  157.6 0.9 mix.1
Async XLA Ops:
  2.0 41.8 %all-to-all-start = ((bf16[64,2,1920]{2,1,0:T(2,128)(2,1)}), bf16[64,2,1920]{2,1,0:T(2,128)(2,1)S(1)}, u32[]{:S(2)}, u32[]{:S(2)}) async-start(bf16[64,2,1920]{2,1,0:T(2,128)(2,1)} %get-tuple-element.15), calls=%async_computation | async-start | bytes 983040 | tf_op jit(solution)/shard_map/all_to_all | solution.py:199
  25.1 57.2 %collective-permute-start = (bf16[3584,256]{1,0:T(8,128)(2,1)}, bf16[3584,256]{1,0:T(8,128)(2,1)}, u32[]{:S(2)}, u32[]{:S(2)}) collective-permute-start(bf16[3584,256]{1,0:T(8,128)(2,1)} %bitcast.12), channel_id=1, source_target_pairs={{0,1},{1,0},{2,3},{3,2},{4,5},{5,4},{6,7},{7,6},{8,9},{9,8},{10,11... | collective-permute-start | bytes 5505032 | tf_op jit(solution)/shard_map/ppermute | solution.py:198
  27.1 35.8 %collective-permute-start.5 = (bf16[224,2048]{1,0:T(8,128)(2,1)}, bf16[224,2048]{1,0:T(8,128)(2,1)S(1)}, u32[]{:S(2)}, u32[]{:S(2)}) collective-permute-start(bf16[224,2048]{1,0:T(8,128)(2,1)} %bitcast.9), channel_id=1, source_target_pairs={{0,2},{2,0},{4,6},{6,4},{8,10},{10,8},{12,14},{14,12},{1,3},{3,1},... | collective-permute-start | bytes 2752520 | tf_op jit(solution)/shard_map/ppermute | solution.py:197
  44.5 50.6 %copy-start.2 = (bf16[64,32]{1,0:T(8,128)(2,1)}, bf16[64,32]{1,0:T(8,128)(2,1)S(1)}, u32[]{:S(2)}) copy-start(bf16[64,32]{1,0:T(8,128)(2,1)S(1)} %get-tuple-element.23.select_ref) | copy-start | bytes 12292
  44.5 12.5 %collective-permute-start.2 = (bf16[32,3712]{1,0:T(8,128)(2,1)S(1)}, bf16[32,3712]{1,0:T(8,128)(2,1)S(1)}, u32[]{:S(2)}, u32[]{:S(2)}) collective-permute-start(bf16[32,3712]{1,0:T(8,128)(2,1)S(1)} %get-tuple-element.16.refs_0_), channel_id=1, source_target_pairs={{0,14},{2,0},{4,2},{6,4},{8,6},{10,8},{12,10},{14,12},{1,15},{3,1}... | collective-permute-start | bytes 712712 | tf_op jit(solution)/shard_map/ppermute | solution.py:48
  49.2 11.5 %collective-permute-start.1 = (bf16[32,3712]{1,0:T(8,128)(2,1)S(1)}, bf16[32,3712]{1,0:T(8,128)(2,1)S(1)}, u32[]{:S(2)}, u32[]{:S(2)}) collective-permute-start(bf16[32,3712]{1,0:T(8,128)(2,1)S(1)} %get-tuple-element.16.refs_0_), channel_id=1, source_target_pairs={{0,2},{2,4},{4,6},{6,8},{8,10},{10,12},{12,14},{14,0},{1,3},{3,5},... | collective-permute-start | bytes 712712 | tf_op jit(solution)/shard_map/ppermute | solution.py:47
  57.0 9.3 %collective-permute-start.4 = (bf16[32,3712]{1,0:T(8,128)(2,1)S(1)}, bf16[32,3712]{1,0:T(8,128)(2,1)S(1)}, u32[]{:S(2)}, u32[]{:S(2)}) collective-permute-start(bf16[32,3712]{1,0:T(8,128)(2,1)S(1)} %collective-permute-done.2.refs_2_), channel_id=1, source_target_pairs={{0,14},{2,0},{4,2},{6,4},{8,6},{10,8},{12,10},{14,12},{1,15},{3,1}... | collective-permute-start | bytes 712712 | tf_op jit(solution)/shard_map/ppermute | solution.py:48
  60.7 10.2 %collective-permute-start.3 = (bf16[32,3712]{1,0:T(8,128)(2,1)S(1)}, bf16[32,3712]{1,0:T(8,128)(2,1)S(1)}, u32[]{:S(2)}, u32[]{:S(2)}) collective-permute-start(bf16[32,3712]{1,0:T(8,128)(2,1)S(1)} %collective-permute-done.1.refs_1_), channel_id=1, source_target_pairs={{0,2},{2,4},{4,6},{6,8},{8,10},{10,12},{12,14},{14,0},{1,3},{3,5},... | collective-permute-start | bytes 712712 | tf_op jit(solution)/shard_map/ppermute | solution.py:47
  71.0 9.3 %collective-permute-start.6 = (bf16[32,3712]{1,0:T(8,128)(2,1)S(1)}, bf16[32,3712]{1,0:T(8,128)(2,1)S(1)}, u32[]{:S(2)}, u32[]{:S(2)}) collective-permute-start(bf16[32,3712]{1,0:T(8,128)(2,1)S(1)} %collective-permute-done.3.refs_3_), channel_id=1, source_target_pairs={{0,2},{2,4},{4,6},{6,8},{8,10},{10,12},{12,14},{14,0},{1,3},{3,5},... | collective-permute-start | bytes 712712 | tf_op jit(solution)/shard_map/ppermute | solution.py:47
  72.9 9.4 %collective-permute-start.7 = (bf16[32,3712]{1,0:T(8,128)(2,1)S(1)}, bf16[32,3712]{1,0:T(8,128)(2,1)S(1)}, u32[]{:S(2)}, u32[]{:S(2)}) collective-permute-start(bf16[32,3712]{1,0:T(8,128)(2,1)S(1)} %collective-permute-done.4.refs_4_), channel_id=1, source_target_pairs={{0,14},{2,0},{4,2},{6,4},{8,6},{10,8},{12,10},{14,12},{1,15},{3,1}... | collective-permute-start | bytes 712712 | tf_op jit(solution)/shard_map/ppermute | solution.py:48
  80.3 9.3 %collective-permute-start.8 = (bf16[32,3712]{1,0:T(8,128)(2,1)S(1)}, bf16[32,3712]{1,0:T(8,128)(2,1)}, u32[]{:S(2)}, u32[]{:S(2)}) collective-permute-start(bf16[32,3712]{1,0:T(8,128)(2,1)S(1)} %collective-permute-done.6.refs_5_), channel_id=1, source_target_pairs={{0,2},{2,4},{4,6},{6,8},{8,10},{10,12},{12,14},{14,0},{1,3},{3,5},... | collective-permute-start | bytes 712712 | tf_op jit(solution)/shard_map/ppermute | solution.py:52
  82.3 18.4 %copy-start = (bf16[1,2048,224]{1,2,0:T(8,128)(2,1)S(1)}, bf16[1,2048,224]{1,2,0:T(8,128)(2,1)}, u32[]{:S(2)}) copy-start(bf16[1,2048,224]{1,2,0:T(8,128)(2,1)} %param.9) | copy-start | bytes 2752516
  95.1 20.0 %all-to-all-start.1 = ((bf16[8,128,256]{2,1,0:T(8,128)(2,1)}), bf16[8,128,256]{2,1,0:T(8,128)(2,1)S(1)}, u32[]{:S(2)}, u32[]{:S(2)}) async-start(bf16[8,128,256]{2,1,0:T(8,128)(2,1)} %hidden.1), calls=%async_computation.1 | async-start | bytes 1048576 | tf_op jit(solution)/shard_map/all_to_all | solution.py:219
  100.6 29.6 %copy-start.3 = (bf16[64,32]{1,0:T(8,128)(2,1)S(1)}, bf16[64,32]{1,0:T(8,128)(2,1)}, u32[]{:S(2)}) copy-start(bf16[64,32]{1,0:T(8,128)(2,1)} %copy-done.2) | copy-start | bytes 12292
  100.6 14.4 %collective-permute-start.9 = (bf16[224,2048]{1,0:T(8,128)(2,1)S(1)}, bf16[224,2048]{1,0:T(8,128)(2,1)S(1)}, u32[]{:S(2)}, u32[]{:S(2)}) collective-permute-start(bf16[224,2048]{1,0:T(8,128)(2,1)S(1)} %bitcast.10), channel_id=1, source_target_pairs={{0,1},{1,0},{2,3},{3,2},{4,5},{5,4},{6,7},{7,6},{8,9},{9,8},{10,11... | collective-permute-start | bytes 2752520 | tf_op jit(solution)/shard_map/ppermute | solution.py:217
  102.6 12.5 %collective-permute-start.10 = (bf16[224,2048]{1,0:T(8,128)(2,1)S(1)}, bf16[224,2048]{1,0:T(8,128)(2,1)}, u32[]{:S(2)}, u32[]{:S(2)}) collective-permute-start(bf16[224,2048]{1,0:T(8,128)(2,1)S(1)} %collective-permute-done.5.pair_ref), channel_id=1, source_target_pairs={{0,1},{1,0},{2,3},{3,2},{4,5},{5,4},{6,7},{7,6},{8,9},{9,8},{10,11... | collective-permute-start | bytes 2752520 | tf_op jit(solution)/shard_map/ppermute | solution.py:218
  117.7 39.9 %copy-start.1 = (bf16[64,8]{1,0:T(8,128)(2,1)S(1)}, bf16[64,8]{1,0:T(8,128)(2,1)}, u32[]{:S(2)}) copy-start(bf16[64,8]{1,0:T(8,128)(2,1)} %get-tuple-element.24.place_ref) | copy-start | bytes 3076

commit v6 on v5

--- a/solution.py
+++ b/solution.py
@@ -14,8 +14,8 @@
 SMEM = pl.BlockSpec(memory_space=pltpu.SMEM)
 HBM = pl.BlockSpec(memory_space=pltpu.HBM)
 HID = 50
-DOWN = 50
-BESIDE = 2
+DOWN = 52
+CHUNKS = 4
 
 
 def dot(a, b):
@@ -38,7 +38,7 @@
     )
 
 
-def ring(block, n, beside):
+def ring(block, n):
     up = [(i, (i + 1) % n) for i in range(n)]
     down = [(i, (i - 1) % n) for i in range(n)]
     got = [(0, block)]
@@ -46,11 +46,9 @@
     for k in range(1, n // 2):
         fwd = lax.ppermute(fwd, "x", up)
         back = lax.ppermute(back, "x", down)
-        if k == BESIDE:
-            fwd, back, beside = lax.optimization_barrier((fwd, back, beside))
         got += [(k, fwd), (n - k, back)]
     got.append((n // 2, lax.ppermute(fwd, "x", up)))
-    return got, beside
+    return got
 
 
 def pack_kernel(picks_ref, gates_ref, tok_ref, send_ref, place_ref):
@@ -104,10 +102,15 @@
 
 def hidden_kernel(steps, at_ref, gu_ref, other_ref, *refs):
     blocks, (out_ref, buf, sems) = refs[:-3], refs[-3:]
+    depth = gu_ref.shape[0] // CHUNKS
     copies = []
     for i, w in enumerate((gu_ref, other_ref)):
-        copies.append(pltpu.make_async_copy(w, buf.at[i], sems.at[i]))
-        copies[-1].start()
+        for k in range(CHUNKS):
+            part = pl.ds(k * depth, depth)
+            copies.append(
+                pltpu.make_async_copy(w.at[part, :], buf.at[i, part, :], sems.at[i, k])
+            )
+            copies[-1].start()
     n = len(blocks)
     x, c = at_ref[0], at_ref[1]
     r = blocks[0].shape[0]
@@ -119,8 +122,11 @@
     gate = jnp.where(at_ref[2] == 0, tail[:, 0:1], tail[:, 1:2])
     parts = []
     for i in range(2):
-        copies[i].wait()
-        pr = dot(rows, buf[i])
+        pr = 0.0
+        for k in range(CHUNKS):
+            copies[i * CHUNKS + k].wait()
+            lo, hi = k * depth, (k + 1) * depth
+            pr += dot(rows[:, lo:hi], buf[i, lo:hi, :])
         g, p = pr[:, :units], pr[:, units:]
         parts.append((g / (1.0 + jnp.exp(-g)) * p * gate).astype(bf16))
     mine, other = parts
@@ -195,26 +201,28 @@
         room=60,
     )(node_picks.T, gates.transpose(1, 2, 0), tokens)
     dn_pair = lax.ppermute(dn, "x", pair)
-    gu_other = lax.ppermute(gu, "core", swap)
+    dn_pair, mine = lax.optimization_barrier((dn_pair, gu))
+    gu_other = lax.ppermute(mine, "core", swap)
+    dn_other = lax.ppermute(dn, "core", swap)
     arrived = lax.all_to_all(send, group, split_axis=0, concat_axis=0, tiled=True)
+    arrived, dn_other = lax.optimization_barrier((arrived, dn_other))
     rows, select = call(
         compact_kernel,
         [((r, width + LANES), bf16), ((groups, r), bf16)],
         [VMEM],
         "compact",
     )(arrived)
-    got, dn_pair = ring(rows, n, dn_pair)
+    got = ring(rows, n)
     steps = tuple(k for k, _ in got)
     (hid,) = call(
         functools.partial(hidden_kernel, steps),
         [((n, n * r // 2, units), bf16)],
         [SMEM, HBM, HBM] + [VMEM] * n,
         "hidden",
-        [pltpu.VMEM((2,) + gu.shape, bf16), pltpu.SemaphoreType.DMA((2,))],
+        [pltpu.VMEM((2,) + gu.shape, bf16), pltpu.SemaphoreType.DMA((2, CHUNKS))],
         HID,
     )(at, gu, gu_other, *[b for _, b in got])
-    hid, mine, dn_pair = lax.optimization_barrier((hid, dn, dn_pair))
-    dn_other = lax.ppermute(mine, "core", swap)
+    hid, dn_pair = lax.optimization_barrier((hid, dn_pair))
     dn_both = lax.ppermute(dn_pair, "core", swap)
     hid = lax.all_to_all(hid, "x", split_axis=0, concat_axis=0, tiled=True)
     (out,) = call(

time: 159 us -> 148 us (0.931)
  waiting for transfers between devices: 46.9 us -> 39.4 us
  blocking collectives: 39.6 us -> 32.5 us
  starting transfers between devices: 59.8 us -> 61.6 us
    ppermute x3, waiting for transfers between devices: 9.24 us -> 0.01 us  [ring(): back = lax.ppermute(back, 'x', down)]
    all_to_all x1, blocking collectives: 27 us -> 19.9 us  [shards(): lax.all_to_all(padded, group, split_axis=0, concat_axis=0, tiled=True)]
  transfers between devices with their start and end apart: 13 -> 13, of which waited for: 7 -> 7; matrix products, arithmetic and copies ran while one was open for 0% -> 0% of each run, Pallas kernels for 0% -> 2%
where the time goes in v6:
time: 148 us; the launch traced here: 147 us
  starting transfers between devices  61.6 us (42%)
  waiting for transfers between devices  39.4 us (27%)
  blocking collectives  32.5 us (22%)
  Pallas kernels  12.4 us (8%)
    all_to_all x1, starting transfers between devices, shards(): lax.all_to_all(send, group, split_axis=0, concat_axis=0, tiled=True)  23.1 us
    all_to_all x1, blocking collectives, shards(): lax.all_to_all(padded, group, split_axis=0, concat_axis=0, tiled=True)  19.9 us
    ppermute x3, starting transfers between devices, ring(): back = lax.ppermute(back, 'x', down)  14.9 us
    all_to_all x1, waiting for transfers between devices, shards(): lax.all_to_all(send, group, split_axis=0, concat_axis=0, tiled=True)  13.7 us
    all_to_all x1, blocking collectives, shards(): back = lax.all_to_all(out, 'x', split_axis=0, concat_axis=0, tiled=True)  12.5 us
    all_to_all x1, waiting for transfers between devices, shards(): hid = lax.all_to_all(hid, 'x', split_axis=0, concat_axis=0, tiled=True)  11.4 us
    ppermute x1, waiting for transfers between devices, ring(): got.append((n // 2, lax.ppermute(fwd, 'x', up)))  7.19 us
    ppermute x3, waiting for transfers between devices, ring(): fwd = lax.ppermute(fwd, 'x', up)  6.71 us
  transfers between devices with their start and end apart: 13, of which 7 were waited for; matrix products, arithmetic and copies ran while one was open for 0% of the time, Pallas kernels for 2%

profile of v6, /device:TPU:32, one launch (start us, length us, event | category | flops | bytes accessed | tf_op | source)
XLA Modules:
  0.0 147.0 jit_solution(15499726301037136191)
XLA Ops:
  0.0 3.4 %collective-permute-start = (bf16[224,2048]{1,0:T(8,128)(2,1)}, bf16[224,2048]{1,0:T(8,128)(2,1)S(1)}, u32[]{:S(2)}, u32[]{:S(2)}) collective-permute-start(bf16[224,2048]{1,0:T(8,128)(2,1)} %bitcast.9), channel_id=1, source_target_pairs={{0,2},{2,0},{4,6},{6,4},{8,10},{10,8},{12,14},{14,12},{1,3},{3,1},... | collective-permute-start | bytes 2752520 | tf_op jit(solution)/shard_map/ppermute | solution.py:203
  3.4 2.0 %pack.1 = (bf16[64,2,1920]{2,1,0:T(2,128)(2,1)}, bf16[64,8]{1,0:T(8,128)(2,1)}) custom-call(s32[4,8]{1,0:T(4,128)} %bitcast.14, bf16[4,2,8]{2,1,0:T(2,128)(2,1)} %bitcast.15, bf16[8,3584]{1,0:T(8,128)(2,1)} %tok_ref.1), custom_call_target="tpu_custom_call" | custom-call | tf_op jit(solution)/shard_map/pack/pallas_call | solution.py:196
  5.4 23.1 %all-to-all-start = ((bf16[64,2,1920]{2,1,0:T(2,128)(2,1)}), bf16[64,2,1920]{2,1,0:T(2,128)(2,1)S(1)}, u32[]{:S(2)}, u32[]{:S(2)}) async-start(bf16[64,2,1920]{2,1,0:T(2,128)(2,1)} %get-tuple-element.16), calls=%async_computation | async-start | bytes 983040 | tf_op jit(solution)/shard_map/all_to_all | solution.py:207
  28.6 1.9 %collective-permute-start.2 = (bf16[224,2048]{1,0:T(8,128)(2,1)}, bf16[224,2048]{1,0:T(8,128)(2,1)}, u32[]{:S(2)}, u32[]{:S(2)}) collective-permute-start(bf16[224,2048]{1,0:T(8,128)(2,1)} %bitcast.10), channel_id=1, source_target_pairs={{0,1},{1,0},{2,3},{3,2},{4,5},{5,4},{6,7},{7,6},{8,9},{9,8},{10,11... | collective-permute-start | bytes 2752520 | tf_op jit(solution)/shard_map/ppermute | solution.py:206
  30.5 0.0 collective-permute-done.pair_ref
  30.5 0.0 copy-start.2
  30.5 2.4 %collective-permute-start.1 = (bf16[3584,256]{1,0:T(8,128)(2,1)}, bf16[3584,256]{1,0:T(8,128)(2,1)}, u32[]{:S(2)}, u32[]{:S(2)}) collective-permute-start(bf16[3584,256]{1,0:T(8,128)(2,1)} %bitcast.12), channel_id=1, source_target_pairs={{0,1},{1,0},{2,3},{3,2},{4,5},{5,4},{6,7},{7,6},{8,9},{9,8},{10,11... | collective-permute-start | bytes 5505032 | tf_op jit(solution)/shard_map/ppermute | solution.py:205
  33.0 0.3 collective-permute-done.2.other_ref
  33.3 13.7 %all-to-all-done.in_ref = bf16[64,2,1920]{2,1,0:T(2,128)(2,1)S(1)} async-done(((bf16[64,2,1920]{2,1,0:T(2,128)(2,1)}), bf16[64,2,1920]{2,1,0:T(2,128)(2,1)S(1)}, u32[]{:S(2)}, u32[]{:S(2)}) %all-to-all-start) | async-done | bytes 491552 | tf_op jit(solution)/shard_map/all_to_all | solution.py:207
  47.0 0.6 compact.1
  47.6 2.4 %collective-permute-start.3 = (bf16[32,3712]{1,0:T(8,128)(2,1)S(1)}, bf16[32,3712]{1,0:T(8,128)(2,1)S(1)}, u32[]{:S(2)}, u32[]{:S(2)}) collective-permute-start(bf16[32,3712]{1,0:T(8,128)(2,1)S(1)} %get-tuple-element.18.refs_0_), channel_id=1, source_target_pairs={{0,2},{2,4},{4,6},{6,8},{8,10},{10,12},{12,14},{14,0},{1,3},{3,5},... | collective-permute-start | bytes 712712 | tf_op jit(solution)/shard_map/ppermute | solution.py:47
  50.0 4.7 %collective-permute-start.4 = (bf16[32,3712]{1,0:T(8,128)(2,1)S(1)}, bf16[32,3712]{1,0:T(8,128)(2,1)S(1)}, u32[]{:S(2)}, u32[]{:S(2)}) collective-permute-start(bf16[32,3712]{1,0:T(8,128)(2,1)S(1)} %get-tuple-element.18.refs_0_), channel_id=1, source_target_pairs={{0,14},{2,0},{4,2},{6,4},{8,6},{10,8},{12,10},{14,12},{1,15},{3,1}... | collective-permute-start | bytes 712712 | tf_op jit(solution)/shard_map/ppermute | solution.py:48
  54.7 0.0 copy-done.2
  54.7 2.1 %collective-permute-done.3.refs_1_ = bf16[32,3712]{1,0:T(8,128)(2,1)S(1)} collective-permute-done((bf16[32,3712]{1,0:T(8,128)(2,1)S(1)}, bf16[32,3712]{1,0:T(8,128)(2,1)S(1)}, u32[]{:S(2)}, u32[]{:S(2)}) %collective-permute-start.3) | collective-permute-done | bytes 237600 | tf_op jit(solution)/shard_map/ppermute | solution.py:47
  56.9 1.9 %collective-permute-start.5 = (bf16[32,3712]{1,0:T(8,128)(2,1)S(1)}, bf16[32,3712]{1,0:T(8,128)(2,1)S(1)}, u32[]{:S(2)}, u32[]{:S(2)}) collective-permute-start(bf16[32,3712]{1,0:T(8,128)(2,1)S(1)} %collective-permute-done.3.refs_1_), channel_id=1, source_target_pairs={{0,2},{2,4},{4,6},{6,8},{8,10},{10,12},{12,14},{14,0},{1,3},{3,5},... | collective-permute-start | bytes 712712 | tf_op jit(solution)/shard_map/ppermute | solution.py:47
  58.8 0.0 collective-permute-done.4.refs_2_
  58.8 5.1 %collective-permute-start.6 = (bf16[32,3712]{1,0:T(8,128)(2,1)S(1)}, bf16[32,3712]{1,0:T(8,128)(2,1)S(1)}, u32[]{:S(2)}, u32[]{:S(2)}) collective-permute-start(bf16[32,3712]{1,0:T(8,128)(2,1)S(1)} %collective-permute-done.4.refs_2_), channel_id=1, source_target_pairs={{0,14},{2,0},{4,2},{6,4},{8,6},{10,8},{12,10},{14,12},{1,15},{3,1}... | collective-permute-start | bytes 712712 | tf_op jit(solution)/shard_map/ppermute | solution.py:48
  63.9 2.1 %collective-permute-done.5.refs_3_ = bf16[32,3712]{1,0:T(8,128)(2,1)S(1)} collective-permute-done((bf16[32,3712]{1,0:T(8,128)(2,1)S(1)}, bf16[32,3712]{1,0:T(8,128)(2,1)S(1)}, u32[]{:S(2)}, u32[]{:S(2)}) %collective-permute-start.5) | collective-permute-done | bytes 237600 | tf_op jit(solution)/shard_map/ppermute | solution.py:47
  66.1 1.9 %collective-permute-start.7 = (bf16[32,3712]{1,0:T(8,128)(2,1)S(1)}, bf16[32,3712]{1,0:T(8,128)(2,1)S(1)}, u32[]{:S(2)}, u32[]{:S(2)}) collective-permute-start(bf16[32,3712]{1,0:T(8,128)(2,1)S(1)} %collective-permute-done.5.refs_3_), channel_id=1, source_target_pairs={{0,2},{2,4},{4,6},{6,8},{8,10},{10,12},{12,14},{14,0},{1,3},{3,5},... | collective-permute-start | bytes 712712 | tf_op jit(solution)/shard_map/ppermute | solution.py:47
  68.0 0.0 collective-permute-done.6.refs_4_
  68.0 5.1 %collective-permute-start.8 = (bf16[32,3712]{1,0:T(8,128)(2,1)S(1)}, bf16[32,3712]{1,0:T(8,128)(2,1)S(1)}, u32[]{:S(2)}, u32[]{:S(2)}) collective-permute-start(bf16[32,3712]{1,0:T(8,128)(2,1)S(1)} %collective-permute-done.6.refs_4_), channel_id=1, source_target_pairs={{0,14},{2,0},{4,2},{6,4},{8,6},{10,8},{12,10},{14,12},{1,15},{3,1}... | collective-permute-start | bytes 712712 | tf_op jit(solution)/shard_map/ppermute | solution.py:48
  73.1 2.4 %collective-permute-done.7.refs_5_ = bf16[32,3712]{1,0:T(8,128)(2,1)S(1)} collective-permute-done((bf16[32,3712]{1,0:T(8,128)(2,1)S(1)}, bf16[32,3712]{1,0:T(8,128)(2,1)S(1)}, u32[]{:S(2)}, u32[]{:S(2)}) %collective-permute-start.7) | collective-permute-done | bytes 237600 | tf_op jit(solution)/shard_map/ppermute | solution.py:47
  75.6 1.9 %collective-permute-start.9 = (bf16[32,3712]{1,0:T(8,128)(2,1)S(1)}, bf16[32,3712]{1,0:T(8,128)(2,1)S(1)}, u32[]{:S(2)}, u32[]{:S(2)}) collective-permute-start(bf16[32,3712]{1,0:T(8,128)(2,1)S(1)} %collective-permute-done.7.refs_5_), channel_id=1, source_target_pairs={{0,2},{2,4},{4,6},{6,8},{8,10},{10,12},{12,14},{14,0},{1,3},{3,5},... | collective-permute-start | bytes 712712 | tf_op jit(solution)/shard_map/ppermute | solution.py:50
  77.5 0.1 pad_add_fusion.at_ref
  77.6 0.0 copy-start
  77.6 0.0 collective-permute-done.8.refs_6_
  77.6 7.2 %collective-permute-done.9.refs_7_ = bf16[32,3712]{1,0:T(8,128)(2,1)S(1)} collective-permute-done((bf16[32,3712]{1,0:T(8,128)(2,1)S(1)}, bf16[32,3712]{1,0:T(8,128)(2,1)S(1)}, u32[]{:S(2)}, u32[]{:S(2)}) %collective-permute-start.9) | collective-permute-done | bytes 237600 | tf_op jit(solution)/shard_map/ppermute | solution.py:50
  84.8 0.0 collective-permute-done.1.other_ref
  84.8 5.2 %hidden.1 = bf16[8,128,256]{2,1,0:T(8,128)(2,1)} custom-call(s32[3]{0:T(128)S(1)} %pad_add_fusion.at_ref, bf16[3584,256]{1,0:T(8,128)(2,1)} %bitcast.13, bf16[3584,256]{1,0:T(8,128)(2,1)} %collective-permute-done.1.other_ref, bf16[32,3712]{1,0:T(8,128)(2,1)S(1)} %get-tuple-element.18.refs_0_, bf16[32,3712]{1,0:T(8,128)(2,1)S(1)} %collective-permute-done.3.refs_1_, ...), custom_call_target="tpu_custom_call" | custom-call | tf_op jit(solution)/shard_map/hidden/pallas_call | solution.py:217
  90.0 5.8 %all-to-all-start.1 = ((bf16[8,128,256]{2,1,0:T(8,128)(2,1)}), bf16[8,128,256]{2,1,0:T(8,128)(2,1)S(1)}, u32[]{:S(2)}, u32[]{:S(2)}) async-start(bf16[8,128,256]{2,1,0:T(8,128)(2,1)} %hidden.1), calls=%async_computation.1 | async-start | bytes 1048576 | tf_op jit(solution)/shard_map/all_to_all | solution.py:227
  95.8 1.9 %collective-permute-start.10 = (bf16[224,2048]{1,0:T(8,128)(2,1)}, bf16[224,2048]{1,0:T(8,128)(2,1)S(1)}, u32[]{:S(2)}, u32[]{:S(2)}) collective-permute-start(bf16[224,2048]{1,0:T(8,128)(2,1)} %copy-done.2), channel_id=1, source_target_pairs={{0,1},{1,0},{2,3},{3,2},{4,5},{5,4},{6,7},{7,6},{8,9},{9,8},{10,11... | collective-permute-start | bytes 2752520 | tf_op jit(solution)/shard_map/ppermute | solution.py:226
  97.7 11.4 %all-to-all-done.1.h_ref = bf16[8,128,256]{2,1,0:T(8,128)(2,1)S(1)} async-done(((bf16[8,128,256]{2,1,0:T(8,128)(2,1)}), bf16[8,128,256]{2,1,0:T(8,128)(2,1)S(1)}, u32[]{:S(2)}, u32[]{:S(2)}) %all-to-all-start.1) | async-done | bytes 524320 | tf_op jit(solution)/shard_map/all_to_all | solution.py:227
  109.1 0.0 collective-permute-done.10.both_ref
  109.1 0.0 copy-start.3
  109.1 0.9 copy-done.3
  110.0 0.0 copy-done
  110.0 3.2 %down.1 = bf16[8,16,896]{2,1,0:T(8,128)(2,1)S(1)} custom-call(s32[3]{0:T(128)S(1)} %pad_add_fusion.at_ref, bf16[8,128,256]{2,1,0:T(8,128)(2,1)S(1)} %all-to-all-done.1.h_ref, bf16[224,2048]{1,0:T(8,128)(2,1)S(1)} %bitcast.11, bf16[224,2048]{1,0:T(8,128)(2,1)} %collective-permute-done.2.other_ref, bf16[224,2048]{1,0:T(8,128)(2,1)} %copy-done.2, ...), custom_call_target="tpu_custom_call" | custom-call | tf_op jit(solution)/shard_map/down/pallas_call | solution.py:228
  113.3 0.0 copy-start.1
  113.3 12.5 %all_to_all.20.back_ref = bf16[8,16,896]{2,1,0:T(8,128)(2,1)S(1)} all-to-all(bf16[8,16,896]{2,1,0:T(8,128)(2,1)S(1)} %down.1), channel_id=1, replica_groups=mesh['y'=8,'z'=8,'x'=8,'core'=2] {'x'}, dimensions={0} | all-to-all | bytes 458752 | tf_op jit(solution)/shard_map/all_to_all | solution.py:235
  125.8 0.3 spread.1
  126.1 19.9 %all_to_all.21.in_ref = bf16[64,2,1792]{2,1,0:T(2,128)(2,1)S(1)} all-to-all(bf16[64,2,1792]{2,1,0:T(2,128)(2,1)S(1)} %spread.1), channel_id=1, replica_groups=mesh['y'=8,'z'=8,'x'=8,'core'=2] {'y','z'}, dimensions={0} | all-to-all | bytes 917504 | tf_op jit(solution)/shard_map/all_to_all | solution.py:239
  146.1 0.0 copy-done.1
  146.1 0.9 mix.1
Async XLA Ops:
  0.0 30.5 %collective-permute-start = (bf16[224,2048]{1,0:T(8,128)(2,1)}, bf16[224,2048]{1,0:T(8,128)(2,1)S(1)}, u32[]{:S(2)}, u32[]{:S(2)}) collective-permute-start(bf16[224,2048]{1,0:T(8,128)(2,1)} %bitcast.9), channel_id=1, source_target_pairs={{0,2},{2,0},{4,6},{6,4},{8,10},{10,8},{12,14},{14,12},{1,3},{3,1},... | collective-permute-start | bytes 2752520 | tf_op jit(solution)/shard_map/ppermute | solution.py:203
  5.4 41.6 %all-to-all-start = ((bf16[64,2,1920]{2,1,0:T(2,128)(2,1)}), bf16[64,2,1920]{2,1,0:T(2,128)(2,1)S(1)}, u32[]{:S(2)}, u32[]{:S(2)}) async-start(bf16[64,2,1920]{2,1,0:T(2,128)(2,1)} %get-tuple-element.16), calls=%async_computation | async-start | bytes 983040 | tf_op jit(solution)/shard_map/all_to_all | solution.py:207
  28.6 4.7 %collective-permute-start.2 = (bf16[224,2048]{1,0:T(8,128)(2,1)}, bf16[224,2048]{1,0:T(8,128)(2,1)}, u32[]{:S(2)}, u32[]{:S(2)}) collective-permute-start(bf16[224,2048]{1,0:T(8,128)(2,1)} %bitcast.10), channel_id=1, source_target_pairs={{0,1},{1,0},{2,3},{3,2},{4,5},{5,4},{6,7},{7,6},{8,9},{9,8},{10,11... | collective-permute-start | bytes 2752520 | tf_op jit(solution)/shard_map/ppermute | solution.py:206
  30.5 24.2 %copy-start.2 = (bf16[224,2048]{1,0:T(8,128)(2,1)}, bf16[224,2048]{1,0:T(8,128)(2,1)S(1)}, u32[]{:S(2)}) copy-start(bf16[224,2048]{1,0:T(8,128)(2,1)S(1)} %collective-permute-done.pair_ref) | copy-start | bytes 2752516
  30.5 54.2 %collective-permute-start.1 = (bf16[3584,256]{1,0:T(8,128)(2,1)}, bf16[3584,256]{1,0:T(8,128)(2,1)}, u32[]{:S(2)}, u32[]{:S(2)}) collective-permute-start(bf16[3584,256]{1,0:T(8,128)(2,1)} %bitcast.12), channel_id=1, source_target_pairs={{0,1},{1,0},{2,3},{3,2},{4,5},{5,4},{6,7},{7,6},{8,9},{9,8},{10,11... | collective-permute-start | bytes 5505032 | tf_op jit(solution)/shard_map/ppermute | solution.py:205
  47.6 9.2 %collective-permute-start.3 = (bf16[32,3712]{1,0:T(8,128)(2,1)S(1)}, bf16[32,3712]{1,0:T(8,128)(2,1)S(1)}, u32[]{:S(2)}, u32[]{:S(2)}) collective-permute-start(bf16[32,3712]{1,0:T(8,128)(2,1)S(1)} %get-tuple-element.18.refs_0_), channel_id=1, source_target_pairs={{0,2},{2,4},{4,6},{6,8},{8,10},{10,12},{12,14},{14,0},{1,3},{3,5},... | collective-permute-start | bytes 712712 | tf_op jit(solution)/shard_map/ppermute | solution.py:47
  50.0 8.7 %collective-permute-start.4 = (bf16[32,3712]{1,0:T(8,128)(2,1)S(1)}, bf16[32,3712]{1,0:T(8,128)(2,1)S(1)}, u32[]{:S(2)}, u32[]{:S(2)}) collective-permute-start(bf16[32,3712]{1,0:T(8,128)(2,1)S(1)} %get-tuple-element.18.refs_0_), channel_id=1, source_target_pairs={{0,14},{2,0},{4,2},{6,4},{8,6},{10,8},{12,10},{14,12},{1,15},{3,1}... | collective-permute-start | bytes 712712 | tf_op jit(solution)/shard_map/ppermute | solution.py:48
  56.9 9.2 %collective-permute-start.5 = (bf16[32,3712]{1,0:T(8,128)(2,1)S(1)}, bf16[32,3712]{1,0:T(8,128)(2,1)S(1)}, u32[]{:S(2)}, u32[]{:S(2)}) collective-permute-start(bf16[32,3712]{1,0:T(8,128)(2,1)S(1)} %collective-permute-done.3.refs_1_), channel_id=1, source_target_pairs={{0,2},{2,4},{4,6},{6,8},{8,10},{10,12},{12,14},{14,0},{1,3},{3,5},... | collective-permute-start | bytes 712712 | tf_op jit(solution)/shard_map/ppermute | solution.py:47
  58.8 9.2 %collective-permute-start.6 = (bf16[32,3712]{1,0:T(8,128)(2,1)S(1)}, bf16[32,3712]{1,0:T(8,128)(2,1)S(1)}, u32[]{:S(2)}, u32[]{:S(2)}) collective-permute-start(bf16[32,3712]{1,0:T(8,128)(2,1)S(1)} %collective-permute-done.4.refs_2_), channel_id=1, source_target_pairs={{0,14},{2,0},{4,2},{6,4},{8,6},{10,8},{12,10},{14,12},{1,15},{3,1}... | collective-permute-start | bytes 712712 | tf_op jit(solution)/shard_map/ppermute | solution.py:48
  66.1 9.5 %collective-permute-start.7 = (bf16[32,3712]{1,0:T(8,128)(2,1)S(1)}, bf16[32,3712]{1,0:T(8,128)(2,1)S(1)}, u32[]{:S(2)}, u32[]{:S(2)}) collective-permute-start(bf16[32,3712]{1,0:T(8,128)(2,1)S(1)} %collective-permute-done.5.refs_3_), channel_id=1, source_target_pairs={{0,2},{2,4},{4,6},{6,8},{8,10},{10,12},{12,14},{14,0},{1,3},{3,5},... | collective-permute-start | bytes 712712 | tf_op jit(solution)/shard_map/ppermute | solution.py:47
  68.0 9.6 %collective-permute-start.8 = (bf16[32,3712]{1,0:T(8,128)(2,1)S(1)}, bf16[32,3712]{1,0:T(8,128)(2,1)S(1)}, u32[]{:S(2)}, u32[]{:S(2)}) collective-permute-start(bf16[32,3712]{1,0:T(8,128)(2,1)S(1)} %collective-permute-done.6.refs_4_), channel_id=1, source_target_pairs={{0,14},{2,0},{4,2},{6,4},{8,6},{10,8},{12,10},{14,12},{1,15},{3,1}... | collective-permute-start | bytes 712712 | tf_op jit(solution)/shard_map/ppermute | solution.py:48
  75.6 9.2 %collective-permute-start.9 = (bf16[32,3712]{1,0:T(8,128)(2,1)S(1)}, bf16[32,3712]{1,0:T(8,128)(2,1)S(1)}, u32[]{:S(2)}, u32[]{:S(2)}) collective-permute-start(bf16[32,3712]{1,0:T(8,128)(2,1)S(1)} %collective-permute-done.7.refs_5_), channel_id=1, source_target_pairs={{0,2},{2,4},{4,6},{6,8},{8,10},{10,12},{12,14},{14,0},{1,3},{3,5},... | collective-permute-start | bytes 712712 | tf_op jit(solution)/shard_map/ppermute | solution.py:50
  77.6 32.5 %copy-start = (bf16[1,2048,224]{1,2,0:T(8,128)(2,1)S(1)}, bf16[1,2048,224]{1,2,0:T(8,128)(2,1)}, u32[]{:S(2)}) copy-start(bf16[1,2048,224]{1,2,0:T(8,128)(2,1)} %param.9) | copy-start | bytes 2752516
  90.0 19.1 %all-to-all-start.1 = ((bf16[8,128,256]{2,1,0:T(8,128)(2,1)}), bf16[8,128,256]{2,1,0:T(8,128)(2,1)S(1)}, u32[]{:S(2)}, u32[]{:S(2)}) async-start(bf16[8,128,256]{2,1,0:T(8,128)(2,1)} %hidden.1), calls=%async_computation.1 | async-start | bytes 1048576 | tf_op jit(solution)/shard_map/all_to_all | solution.py:227
  95.8 13.3 %collective-permute-start.10 = (bf16[224,2048]{1,0:T(8,128)(2,1)}, bf16[224,2048]{1,0:T(8,128)(2,1)S(1)}, u32[]{:S(2)}, u32[]{:S(2)}) collective-permute-start(bf16[224,2048]{1,0:T(8,128)(2,1)} %copy-done.2), channel_id=1, source_target_pairs={{0,1},{1,0},{2,3},{3,2},{4,5},{5,4},{6,7},{7,6},{8,9},{9,8},{10,11... | collective-permute-start | bytes 2752520 | tf_op jit(solution)/shard_map/ppermute | solution.py:226
  109.1 0.9 copy-start.3
  113.3 32.8 %copy-start.1 = (bf16[64,8]{1,0:T(8,128)(2,1)S(1)}, bf16[64,8]{1,0:T(8,128)(2,1)}, u32[]{:S(2)}) copy-start(bf16[64,8]{1,0:T(8,128)(2,1)} %get-tuple-element.24.place_ref) | copy-start | bytes 3076

commit v7 on v6

--- a/solution.py
+++ b/solution.py
@@ -9,6 +9,7 @@
 from jax.sharding import PartitionSpec as P
 
 LANES = 128
+EXPERTS = 2
 bf16, f32, i32 = jnp.bfloat16, jnp.float32, jnp.int32
 VMEM = pl.BlockSpec(memory_space=pltpu.VMEM)
 SMEM = pl.BlockSpec(memory_space=pltpu.SMEM)
@@ -81,7 +82,7 @@
     )
 
 
-def compact_kernel(in_ref, rows_ref, select_ref):
+def compact_kernel(in_ref, rows_ref):
     groups, _, wide = in_ref.shape
     half = wide - LANES
     count = rows_ref.shape[0]
@@ -93,15 +94,19 @@
     alive = live[:, :1].astype(f32) > 0
     position = lax.broadcasted_iota(i32, (groups, count), 1).astype(f32) + 1.0
     spread = jnp.where(alive & (upto == position), 1.0, 0.0)
-    select_ref[...] = spread.astype(bf16)
     both = dot_dims(by_half(spread), in_ref[...].reshape(2 * groups, wide), 0, 0).astype(bf16)
     rows_ref[:, :half] = both[:count, :half]
     rows_ref[:, half : 2 * half] = both[count:, :half]
-    rows_ref[:, 2 * half :] = both[:count, half:]
+    slot = lax.broadcasted_iota(i32, (groups, count), 0).astype(f32)
+    came = jnp.sum(spread * slot, axis=0, keepdims=True)
+    came = jnp.broadcast_to(came, (LANES, count)).T
+    lane = lax.broadcasted_iota(i32, (count, LANES), 1)
+    ends = jnp.where(lane == EXPERTS, came, both[:count, half:].astype(f32))
+    rows_ref[:, 2 * half :] = ends.astype(bf16)
 
 
 def hidden_kernel(steps, at_ref, gu_ref, other_ref, *refs):
-    blocks, (out_ref, buf, sems) = refs[:-3], refs[-3:]
+    blocks, (out_ref, from_ref, buf, sems) = refs[:-4], refs[-4:]
     depth = gu_ref.shape[0] // CHUNKS
     copies = []
     for i, w in enumerate((gu_ref, other_ref)):
@@ -139,45 +144,49 @@
         for dest in range(n):
             lo = j * r + (dest % 2) * hr
             out_ref[dest, at, :] = h[lo : lo + hr]
-
-
-def down_kernel(at_ref, h_ref, own_ref, other_ref, pair_ref, both_ref, out_ref):
+        ends = [tail[j * r + b * hr : j * r + (b + 1) * hr] for b in range(2)]
+        from_ref[at, :] = jnp.where(lax.rem(x, 2) == 0, ends[0], ends[1])
+
+
+def down_kernel(at_ref, h_ref, own_ref, other_ref, pair_ref, both_ref, ends_ref, out_ref, whole):
     n, rows, units = h_ref.shape
     b, c = lax.rem(at_ref[0], 2), at_ref[1]
     h = jnp.concatenate([h_ref[k] for k in range(n)], axis=1)
     parts = [
         dot_dims(h, w[...], 1, 1).astype(bf16) for w in (own_ref, other_ref, pair_ref, both_ref)
     ]
-    hr = out_ref.shape[1]
     for bb in range(2):
         for cc in range(2):
 
             @pl.when((b == bb) & (c == cc))
             def _():
                 order = [parts[2 * (p // 2 != bb) + (p % 2 != cc)] for p in range(4)]
-                whole = jnp.concatenate(order, axis=1)
-                for k in range(out_ref.shape[0]):
-                    out_ref[k] = whole[k * hr : (k + 1) * hr]
-
-
-def spread_kernel(back_ref, select_ref, out_ref):
-    n, hr, feats = back_ref.shape
-    rows = [
-        jnp.concatenate([back_ref[2 * a], back_ref[2 * a + 1]], axis=0) for a in range(n // 2)
-    ]
-    whole = jnp.concatenate(rows, axis=1)
-    half = out_ref.shape[2]
-    for h in range(2):
-        out_ref[:, h, :] = dot(select_ref[...], whole[:, h * half : (h + 1) * half]).astype(bf16)
+                whole[...] = jnp.concatenate(order, axis=1)
+
+    slots, half = out_ref.shape[0], whole.shape[1] // 2
+    group = ends_ref[...].T[EXPERTS : EXPERTS + 1, :].astype(i32)
+    owner = lax.broadcasted_iota(i32, (1, rows), 1) // (rows // n)
+    slot = lax.broadcasted_iota(i32, (slots, rows), 0)
+    place = (slot == group * n + owner).astype(f32).astype(bf16)
+    for k in range(2):
+        out_ref[:, k, :half] = dot(place, whole[:, k * half : (k + 1) * half]).astype(bf16)
 
 
 def mix_kernel(in_ref, place_ref, out_ref):
-    slots, _, half = in_ref.shape
-    toks = out_ref.shape[0]
-    lhs = by_half(place_ref[...].astype(f32))
-    both = dot_dims(lhs, in_ref[...].reshape(2 * slots, half), 0, 0).astype(bf16)
-    out_ref[:, :half] = both[:toks]
-    out_ref[:, half:] = both[toks:]
+    slots = in_ref.shape[0]
+    groups, toks = place_ref.shape
+    n = slots // groups
+    half = out_ref.shape[1] // n
+    spread = jnp.broadcast_to(place_ref[...].astype(f32)[:, None, :], (groups, 2 * n, toks))
+    spread = spread.reshape(2 * slots, toks)
+    row = lax.broadcasted_iota(i32, (2 * slots, toks), 0)
+    which = (row % (2 * n)) // 4 * 2 + row % 2
+    lhs = jnp.concatenate([jnp.where(which == q, spread, 0.0) for q in range(n)], axis=1)
+    flat = in_ref[...].reshape(2 * slots, in_ref.shape[2])
+    both = dot_dims(lhs.astype(bf16), flat, 0, 0).astype(bf16)
+    out_ref[...] = jnp.concatenate(
+        [both[q * toks : (q + 1) * toks, :half] for q in range(n)], axis=1
+    )
 
 
 def shards(tokens, node_picks, gates, gate_up, down_weight):
@@ -206,17 +215,17 @@
     dn_other = lax.ppermute(dn, "core", swap)
     arrived = lax.all_to_all(send, group, split_axis=0, concat_axis=0, tiled=True)
     arrived, dn_other = lax.optimization_barrier((arrived, dn_other))
-    rows, select = call(
+    (rows,) = call(
         compact_kernel,
-        [((r, width + LANES), bf16), ((groups, r), bf16)],
+        [((r, width + LANES), bf16)],
         [VMEM],
         "compact",
     )(arrived)
     got = ring(rows, n)
     steps = tuple(k for k, _ in got)
-    (hid,) = call(
+    hid, ends = call(
         functools.partial(hidden_kernel, steps),
-        [((n, n * r // 2, units), bf16)],
+        [((n, n * r // 2, units), bf16), ((n * r // 2, LANES), f32)],
         [SMEM, HBM, HBM] + [VMEM] * n,
         "hidden",
         [pltpu.VMEM((2,) + gu.shape, bf16), pltpu.SemaphoreType.DMA((2, CHUNKS))],
@@ -225,18 +234,16 @@
     hid, dn_pair = lax.optimization_barrier((hid, dn_pair))
     dn_both = lax.ppermute(dn_pair, "core", swap)
     hid = lax.all_to_all(hid, "x", split_axis=0, concat_axis=0, tiled=True)
+    lanes = -(-2 * feats // LANES) * LANES
     (out,) = call(
         down_kernel,
-        [((n, r // 2, 4 * feats), bf16)],
-        [SMEM] + [VMEM] * 5,
+        [((groups * n, 2, lanes), bf16)],
+        [SMEM] + [VMEM] * 6,
         "down",
-        room=DOWN,
-    )(at, hid, dn, dn_other, dn_pair, dn_both)
-    back = lax.all_to_all(out, "x", split_axis=0, concat_axis=0, tiled=True)
-    (padded,) = call(spread_kernel, [((groups, 2, half), bf16)], [VMEM] * 2, "spread")(
-        back, select
-    )
-    returned = lax.all_to_all(padded, group, split_axis=0, concat_axis=0, tiled=True)
+        [pltpu.VMEM((n * r // 2, 4 * feats), bf16)],
+        DOWN,
+    )(at, hid, dn, dn_other, dn_pair, dn_both, ends)
+    returned = lax.all_to_all(out, group + ("x",), split_axis=0, concat_axis=0, tiled=True)
     (mixed,) = call(mix_kernel, [((toks, width), bf16)], [VMEM] * 2, "mix")(returned, place)
     return mixed
 

time: 148 us -> 160 us (1.081)
  the two profiles are of different devices: /device:TPU:32 before, /device:TPU:2 now
where the time goes in v7:
time: 160 us; the launch traced here: 159 us
  starting transfers between devices  65 us (41%)
  blocking collectives  41.8 us (26%)
  waiting for transfers between devices  36.3 us (23%)
  Pallas kernels  14.6 us (9%)
    all_to_all x1, blocking collectives, shards(): lax.all_to_all(out, group + ('x',), split_axis=0, concat_axis=0, tiled=True)  41.8 us
    ppermute x1, starting transfers between devices, shards(): dn_pair = lax.ppermute(dn, 'x', pair)  15.1 us
    all_to_all x1, waiting for transfers between devices, shards(): lax.all_to_all(send, group, split_axis=0, concat_axis=0, tiled=True)  13.7 us
    ppermute x3, starting transfers between devices, ring(): fwd = lax.ppermute(fwd, 'x', up)  13.2 us
    all_to_all x1, starting transfers between devices, shards(): lax.all_to_all(send, group, split_axis=0, concat_axis=0, tiled=True)  10.8 us
    all_to_all x1, waiting for transfers between devices, shards(): hid = lax.all_to_all(hid, 'x', split_axis=0, concat_axis=0, tiled=True)  9.92 us
    all_to_all x1, starting transfers between devices, shards(): hid = lax.all_to_all(hid, 'x', split_axis=0, concat_axis=0, tiled=True)  9.04 us
    ppermute x3, waiting for transfers between devices, ring(): fwd = lax.ppermute(fwd, 'x', up)  7.2 us
  transfers between devices with their start and end apart: 13, of which 7 were waited for; matrix products, arithmetic and copies ran while one was open for 0% of the time, Pallas kernels for 2%

profile of v7, /device:TPU:2, one launch (start us, length us, event | category | flops | bytes accessed | tf_op | source)
XLA Modules:
  0.0 158.9 jit_solution(1908743045315287327)
XLA Ops:
  0.0 15.1 %collective-permute-start = (bf16[224,2048]{1,0:T(8,128)(2,1)}, bf16[224,2048]{1,0:T(8,128)(2,1)S(1)}, u32[]{:S(2)}, u32[]{:S(2)}) collective-permute-start(bf16[224,2048]{1,0:T(8,128)(2,1)} %bitcast.9), channel_id=1, source_target_pairs={{0,2},{2,0},{4,6},{6,4},{8,10},{10,8},{12,14},{14,12},{1,3},{3,1},... | collective-permute-start | bytes 2752520 | tf_op jit(solution)/shard_map/ppermute | solution.py:212
  15.1 2.0 %pack.1 = (bf16[64,2,1920]{2,1,0:T(2,128)(2,1)}, bf16[64,8]{1,0:T(8,128)(2,1)}) custom-call(s32[4,8]{1,0:T(4,128)} %bitcast.14, bf16[4,2,8]{2,1,0:T(2,128)(2,1)} %bitcast.15, bf16[8,3584]{1,0:T(8,128)(2,1)} %tok_ref.1), custom_call_target="tpu_custom_call" | custom-call | tf_op jit(solution)/shard_map/pack/pallas_call | solution.py:205
  17.1 10.8 %all-to-all-start = ((bf16[64,2,1920]{2,1,0:T(2,128)(2,1)}), bf16[64,2,1920]{2,1,0:T(2,128)(2,1)S(1)}, u32[]{:S(2)}, u32[]{:S(2)}) async-start(bf16[64,2,1920]{2,1,0:T(2,128)(2,1)} %get-tuple-element.16), calls=%async_computation | async-start | bytes 983040 | tf_op jit(solution)/shard_map/all_to_all | solution.py:216
  27.9 1.9 %collective-permute-start.2 = (bf16[224,2048]{1,0:T(8,128)(2,1)}, bf16[224,2048]{1,0:T(8,128)(2,1)}, u32[]{:S(2)}, u32[]{:S(2)}) collective-permute-start(bf16[224,2048]{1,0:T(8,128)(2,1)} %bitcast.10), channel_id=1, source_target_pairs={{0,1},{1,0},{2,3},{3,2},{4,5},{5,4},{6,7},{7,6},{8,9},{9,8},{10,11... | collective-permute-start | bytes 2752520 | tf_op jit(solution)/shard_map/ppermute | solution.py:215
  29.8 0.0 collective-permute-done.pair_ref
  29.8 0.0 copy-start.2
  29.9 2.4 %collective-permute-start.1 = (bf16[3584,256]{1,0:T(8,128)(2,1)}, bf16[3584,256]{1,0:T(8,128)(2,1)}, u32[]{:S(2)}, u32[]{:S(2)}) collective-permute-start(bf16[3584,256]{1,0:T(8,128)(2,1)} %bitcast.12), channel_id=1, source_target_pairs={{0,1},{1,0},{2,3},{3,2},{4,5},{5,4},{6,7},{7,6},{8,9},{9,8},{10,11... | collective-permute-start | bytes 5505032 | tf_op jit(solution)/shard_map/ppermute | solution.py:214
  32.3 0.3 collective-permute-done.2.other_ref
  32.6 13.7 %all-to-all-done.in_ref = bf16[64,2,1920]{2,1,0:T(2,128)(2,1)S(1)} async-done(((bf16[64,2,1920]{2,1,0:T(2,128)(2,1)}), bf16[64,2,1920]{2,1,0:T(2,128)(2,1)S(1)}, u32[]{:S(2)}, u32[]{:S(2)}) %all-to-all-start) | async-done | bytes 491552 | tf_op jit(solution)/shard_map/all_to_all | solution.py:216
  46.3 0.6 compact.1.refs_0_
  47.0 4.4 %collective-permute-start.3 = (bf16[32,3712]{1,0:T(8,128)(2,1)S(1)}, bf16[32,3712]{1,0:T(8,128)(2,1)S(1)}, u32[]{:S(2)}, u32[]{:S(2)}) collective-permute-start(bf16[32,3712]{1,0:T(8,128)(2,1)S(1)} %compact.1.refs_0_), channel_id=1, source_target_pairs={{0,2},{2,4},{4,6},{6,8},{8,10},{10,12},{12,14},{14,0},{1,3},{3,5},... | collective-permute-start | bytes 712712 | tf_op jit(solution)/shard_map/ppermute | solution.py:48
  51.4 1.9 %collective-permute-start.4 = (bf16[32,3712]{1,0:T(8,128)(2,1)S(1)}, bf16[32,3712]{1,0:T(8,128)(2,1)S(1)}, u32[]{:S(2)}, u32[]{:S(2)}) collective-permute-start(bf16[32,3712]{1,0:T(8,128)(2,1)S(1)} %compact.1.refs_0_), channel_id=1, source_target_pairs={{0,14},{2,0},{4,2},{6,4},{8,6},{10,8},{12,10},{14,12},{1,15},{3,1}... | collective-permute-start | bytes 712712 | tf_op jit(solution)/shard_map/ppermute | solution.py:49
  53.3 0.0 copy-done.2
  53.3 1.8 %collective-permute-done.3.refs_1_ = bf16[32,3712]{1,0:T(8,128)(2,1)S(1)} collective-permute-done((bf16[32,3712]{1,0:T(8,128)(2,1)S(1)}, bf16[32,3712]{1,0:T(8,128)(2,1)S(1)}, u32[]{:S(2)}, u32[]{:S(2)}) %collective-permute-start.3) | collective-permute-done | bytes 237600 | tf_op jit(solution)/shard_map/ppermute | solution.py:48
  55.1 4.4 %collective-permute-start.5 = (bf16[32,3712]{1,0:T(8,128)(2,1)S(1)}, bf16[32,3712]{1,0:T(8,128)(2,1)S(1)}, u32[]{:S(2)}, u32[]{:S(2)}) collective-permute-start(bf16[32,3712]{1,0:T(8,128)(2,1)S(1)} %collective-permute-done.3.refs_1_), channel_id=1, source_target_pairs={{0,2},{2,4},{4,6},{6,8},{8,10},{10,12},{12,14},{14,0},{1,3},{3,5},... | collective-permute-start | bytes 712712 | tf_op jit(solution)/shard_map/ppermute | solution.py:48
  59.5 0.0 collective-permute-done.4.refs_2_
  59.5 2.1 %collective-permute-start.6 = (bf16[32,3712]{1,0:T(8,128)(2,1)S(1)}, bf16[32,3712]{1,0:T(8,128)(2,1)S(1)}, u32[]{:S(2)}, u32[]{:S(2)}) collective-permute-start(bf16[32,3712]{1,0:T(8,128)(2,1)S(1)} %collective-permute-done.4.refs_2_), channel_id=1, source_target_pairs={{0,14},{2,0},{4,2},{6,4},{8,6},{10,8},{12,10},{14,12},{1,15},{3,1}... | collective-permute-start | bytes 712712 | tf_op jit(solution)/shard_map/ppermute | solution.py:49
  61.6 2.4 %collective-permute-done.5.refs_3_ = bf16[32,3712]{1,0:T(8,128)(2,1)S(1)} collective-permute-done((bf16[32,3712]{1,0:T(8,128)(2,1)S(1)}, bf16[32,3712]{1,0:T(8,128)(2,1)S(1)}, u32[]{:S(2)}, u32[]{:S(2)}) %collective-permute-start.5) | collective-permute-done | bytes 237600 | tf_op jit(solution)/shard_map/ppermute | solution.py:48
  64.0 4.4 %collective-permute-start.7 = (bf16[32,3712]{1,0:T(8,128)(2,1)S(1)}, bf16[32,3712]{1,0:T(8,128)(2,1)S(1)}, u32[]{:S(2)}, u32[]{:S(2)}) collective-permute-start(bf16[32,3712]{1,0:T(8,128)(2,1)S(1)} %collective-permute-done.5.refs_3_), channel_id=1, source_target_pairs={{0,2},{2,4},{4,6},{6,8},{8,10},{10,12},{12,14},{14,0},{1,3},{3,5},... | collective-permute-start | bytes 712712 | tf_op jit(solution)/shard_map/ppermute | solution.py:48
  68.4 0.0 collective-permute-done.6.refs_4_
  68.4 2.4 %collective-permute-start.8 = (bf16[32,3712]{1,0:T(8,128)(2,1)S(1)}, bf16[32,3712]{1,0:T(8,128)(2,1)S(1)}, u32[]{:S(2)}, u32[]{:S(2)}) collective-permute-start(bf16[32,3712]{1,0:T(8,128)(2,1)S(1)} %collective-permute-done.6.refs_4_), channel_id=1, source_target_pairs={{0,14},{2,0},{4,2},{6,4},{8,6},{10,8},{12,10},{14,12},{1,15},{3,1}... | collective-permute-start | bytes 712712 | tf_op jit(solution)/shard_map/ppermute | solution.py:49
  70.8 3.0 %collective-permute-done.7.refs_5_ = bf16[32,3712]{1,0:T(8,128)(2,1)S(1)} collective-permute-done((bf16[32,3712]{1,0:T(8,128)(2,1)S(1)}, bf16[32,3712]{1,0:T(8,128)(2,1)S(1)}, u32[]{:S(2)}, u32[]{:S(2)}) %collective-permute-start.7) | collective-permute-done | bytes 237600 | tf_op jit(solution)/shard_map/ppermute | solution.py:48
  73.8 4.3 %collective-permute-start.9 = (bf16[32,3712]{1,0:T(8,128)(2,1)S(1)}, bf16[32,3712]{1,0:T(8,128)(2,1)S(1)}, u32[]{:S(2)}, u32[]{:S(2)}) collective-permute-start(bf16[32,3712]{1,0:T(8,128)(2,1)S(1)} %collective-permute-done.7.refs_5_), channel_id=1, source_target_pairs={{0,2},{2,4},{4,6},{6,8},{8,10},{10,12},{12,14},{14,0},{1,3},{3,5},... | collective-permute-start | bytes 712712 | tf_op jit(solution)/shard_map/ppermute | solution.py:51
  78.2 0.1 pad_add_fusion.at_ref
  78.2 0.0 copy-start
  78.3 0.0 collective-permute-done.8.refs_6_
  78.3 5.1 %collective-permute-done.9.refs_7_ = bf16[32,3712]{1,0:T(8,128)(2,1)S(1)} collective-permute-done((bf16[32,3712]{1,0:T(8,128)(2,1)S(1)}, bf16[32,3712]{1,0:T(8,128)(2,1)S(1)}, u32[]{:S(2)}, u32[]{:S(2)}) %collective-permute-start.9) | collective-permute-done | bytes 237600 | tf_op jit(solution)/shard_map/ppermute | solution.py:51
  83.3 0.0 collective-permute-done.1.other_ref
  83.3 5.2 %hidden.1 = (bf16[8,128,256]{2,1,0:T(8,128)(2,1)}, f32[128,128]{1,0:T(8,128)S(1)}) custom-call(s32[3]{0:T(128)S(1)} %pad_add_fusion.at_ref, bf16[3584,256]{1,0:T(8,128)(2,1)} %bitcast.13, bf16[3584,256]{1,0:T(8,128)(2,1)} %collective-permute-done.1.other_ref, bf16[32,3712]{1,0:T(8,128)(2,1)S(1)} %compact.1.refs_0_, ...), custom_call_target="tpu_custom_call" | custom-call | tf_op jit(solution)/shard_map/hidden/pallas_call | solution.py:226
  88.5 9.0 %all-to-all-start.1 = ((bf16[8,128,256]{2,1,0:T(8,128)(2,1)}), bf16[8,128,256]{2,1,0:T(8,128)(2,1)S(1)}, u32[]{:S(2)}, u32[]{:S(2)}) async-start(bf16[8,128,256]{2,1,0:T(8,128)(2,1)} %get-tuple-element.20), calls=%async_computation.1 | async-start | bytes 1048576 | tf_op jit(solution)/shard_map/all_to_all | solution.py:236
  97.6 1.9 %collective-permute-start.10 = (bf16[224,2048]{1,0:T(8,128)(2,1)}, bf16[224,2048]{1,0:T(8,128)(2,1)S(1)}, u32[]{:S(2)}, u32[]{:S(2)}) collective-permute-start(bf16[224,2048]{1,0:T(8,128)(2,1)} %copy-done.2), channel_id=1, source_target_pairs={{0,1},{1,0},{2,3},{3,2},{4,5},{5,4},{6,7},{7,6},{8,9},{9,8},{10,11... | collective-permute-start | bytes 2752520 | tf_op jit(solution)/shard_map/ppermute | solution.py:235
  99.5 9.9 %all-to-all-done.1.h_ref = bf16[8,128,256]{2,1,0:T(8,128)(2,1)S(1)} async-done(((bf16[8,128,256]{2,1,0:T(8,128)(2,1)}), bf16[8,128,256]{2,1,0:T(8,128)(2,1)S(1)}, u32[]{:S(2)}, u32[]{:S(2)}) %all-to-all-start.1) | async-done | bytes 524320 | tf_op jit(solution)/shard_map/all_to_all | solution.py:236
  109.4 0.0 collective-permute-done.10.both_ref
  109.4 0.0 copy-start.3
  109.4 0.9 copy-done.3
  110.4 0.0 copy-done
  110.4 5.0 %down.1 = bf16[512,2,512]{2,1,0:T(2,128)(2,1)} custom-call(s32[3]{0:T(128)S(1)} %pad_add_fusion.at_ref, bf16[8,128,256]{2,1,0:T(8,128)(2,1)S(1)} %all-to-all-done.1.h_ref, bf16[224,2048]{1,0:T(8,128)(2,1)S(1)} %bitcast.11, bf16[224,2048]{1,0:T(8,128)(2,1)} %collective-permute-done.2.other_ref, bf16[224,2048]{1,0:T(8,128)(2,1)} %copy-done.2, ...), custom_call_target="tpu_custom_call" | custom-call | tf_op jit(solution)/shard_map/down/pallas_call | solution.py:238
  115.4 0.0 copy-start.1
  115.4 41.8 %all_to_all.15.in_ref = bf16[512,2,512]{2,1,0:T(2,128)(2,1)S(1)} all-to-all(bf16[512,2,512]{2,1,0:T(2,128)(2,1)} %down.1), channel_id=1, replica_groups=mesh['y'=8,'z'=8,'x'=8,'core'=2] {'y','z','x'}, dimensions={0} | all-to-all | bytes 2097152 | tf_op jit(solution)/shard_map/all_to_all | solution.py:246
  157.1 0.0 copy-done.1
  157.1 1.7 %mix.1 = bf16[8,3584]{1,0:T(8,128)(2,1)} custom-call(bf16[512,2,512]{2,1,0:T(2,128)(2,1)S(1)} %all_to_all.15.in_ref, bf16[64,8]{1,0:T(8,128)(2,1)S(1)} %copy-done.1), custom_call_target="tpu_custom_call" | custom-call | tf_op jit(solution)/shard_map/mix/pallas_call | solution.py:247
Async XLA Ops:
  0.0 29.8 %collective-permute-start = (bf16[224,2048]{1,0:T(8,128)(2,1)}, bf16[224,2048]{1,0:T(8,128)(2,1)S(1)}, u32[]{:S(2)}, u32[]{:S(2)}) collective-permute-start(bf16[224,2048]{1,0:T(8,128)(2,1)} %bitcast.9), channel_id=1, source_target_pairs={{0,2},{2,0},{4,6},{6,4},{8,10},{10,8},{12,14},{14,12},{1,3},{3,1},... | collective-permute-start | bytes 2752520 | tf_op jit(solution)/shard_map/ppermute | solution.py:212
  17.1 29.2 %all-to-all-start = ((bf16[64,2,1920]{2,1,0:T(2,128)(2,1)}), bf16[64,2,1920]{2,1,0:T(2,128)(2,1)S(1)}, u32[]{:S(2)}, u32[]{:S(2)}) async-start(bf16[64,2,1920]{2,1,0:T(2,128)(2,1)} %get-tuple-element.16), calls=%async_computation | async-start | bytes 983040 | tf_op jit(solution)/shard_map/all_to_all | solution.py:216
  27.9 4.7 %collective-permute-start.2 = (bf16[224,2048]{1,0:T(8,128)(2,1)}, bf16[224,2048]{1,0:T(8,128)(2,1)}, u32[]{:S(2)}, u32[]{:S(2)}) collective-permute-start(bf16[224,2048]{1,0:T(8,128)(2,1)} %bitcast.10), channel_id=1, source_target_pairs={{0,1},{1,0},{2,3},{3,2},{4,5},{5,4},{6,7},{7,6},{8,9},{9,8},{10,11... | collective-permute-start | bytes 2752520 | tf_op jit(solution)/shard_map/ppermute | solution.py:215
  29.8 23.5 %copy-start.2 = (bf16[224,2048]{1,0:T(8,128)(2,1)}, bf16[224,2048]{1,0:T(8,128)(2,1)S(1)}, u32[]{:S(2)}) copy-start(bf16[224,2048]{1,0:T(8,128)(2,1)S(1)} %collective-permute-done.pair_ref) | copy-start | bytes 2752516
  29.9 53.5 %collective-permute-start.1 = (bf16[3584,256]{1,0:T(8,128)(2,1)}, bf16[3584,256]{1,0:T(8,128)(2,1)}, u32[]{:S(2)}, u32[]{:S(2)}) collective-permute-start(bf16[3584,256]{1,0:T(8,128)(2,1)} %bitcast.12), channel_id=1, source_target_pairs={{0,1},{1,0},{2,3},{3,2},{4,5},{5,4},{6,7},{7,6},{8,9},{9,8},{10,11... | collective-permute-start | bytes 5505032 | tf_op jit(solution)/shard_map/ppermute | solution.py:214
  47.0 8.1 %collective-permute-start.3 = (bf16[32,3712]{1,0:T(8,128)(2,1)S(1)}, bf16[32,3712]{1,0:T(8,128)(2,1)S(1)}, u32[]{:S(2)}, u32[]{:S(2)}) collective-permute-start(bf16[32,3712]{1,0:T(8,128)(2,1)S(1)} %compact.1.refs_0_), channel_id=1, source_target_pairs={{0,2},{2,4},{4,6},{6,8},{8,10},{10,12},{12,14},{14,0},{1,3},{3,5},... | collective-permute-start | bytes 712712 | tf_op jit(solution)/shard_map/ppermute | solution.py:48
  51.4 8.1 %collective-permute-start.4 = (bf16[32,3712]{1,0:T(8,128)(2,1)S(1)}, bf16[32,3712]{1,0:T(8,128)(2,1)S(1)}, u32[]{:S(2)}, u32[]{:S(2)}) collective-permute-start(bf16[32,3712]{1,0:T(8,128)(2,1)S(1)} %compact.1.refs_0_), channel_id=1, source_target_pairs={{0,14},{2,0},{4,2},{6,4},{8,6},{10,8},{12,10},{14,12},{1,15},{3,1}... | collective-permute-start | bytes 712712 | tf_op jit(solution)/shard_map/ppermute | solution.py:49
  55.1 8.9 %collective-permute-start.5 = (bf16[32,3712]{1,0:T(8,128)(2,1)S(1)}, bf16[32,3712]{1,0:T(8,128)(2,1)S(1)}, u32[]{:S(2)}, u32[]{:S(2)}) collective-permute-start(bf16[32,3712]{1,0:T(8,128)(2,1)S(1)} %collective-permute-done.3.refs_1_), channel_id=1, source_target_pairs={{0,2},{2,4},{4,6},{6,8},{8,10},{10,12},{12,14},{14,0},{1,3},{3,5},... | collective-permute-start | bytes 712712 | tf_op jit(solution)/shard_map/ppermute | solution.py:48
  59.5 8.9 %collective-permute-start.6 = (bf16[32,3712]{1,0:T(8,128)(2,1)S(1)}, bf16[32,3712]{1,0:T(8,128)(2,1)S(1)}, u32[]{:S(2)}, u32[]{:S(2)}) collective-permute-start(bf16[32,3712]{1,0:T(8,128)(2,1)S(1)} %collective-permute-done.4.refs_2_), channel_id=1, source_target_pairs={{0,14},{2,0},{4,2},{6,4},{8,6},{10,8},{12,10},{14,12},{1,15},{3,1}... | collective-permute-start | bytes 712712 | tf_op jit(solution)/shard_map/ppermute | solution.py:49
  64.0 9.8 %collective-permute-start.7 = (bf16[32,3712]{1,0:T(8,128)(2,1)S(1)}, bf16[32,3712]{1,0:T(8,128)(2,1)S(1)}, u32[]{:S(2)}, u32[]{:S(2)}) collective-permute-start(bf16[32,3712]{1,0:T(8,128)(2,1)S(1)} %collective-permute-done.5.refs_3_), channel_id=1, source_target_pairs={{0,2},{2,4},{4,6},{6,8},{8,10},{10,12},{12,14},{14,0},{1,3},{3,5},... | collective-permute-start | bytes 712712 | tf_op jit(solution)/shard_map/ppermute | solution.py:48
  68.4 9.9 %collective-permute-start.8 = (bf16[32,3712]{1,0:T(8,128)(2,1)S(1)}, bf16[32,3712]{1,0:T(8,128)(2,1)S(1)}, u32[]{:S(2)}, u32[]{:S(2)}) collective-permute-start(bf16[32,3712]{1,0:T(8,128)(2,1)S(1)} %collective-permute-done.6.refs_4_), channel_id=1, source_target_pairs={{0,14},{2,0},{4,2},{6,4},{8,6},{10,8},{12,10},{14,12},{1,15},{3,1}... | collective-permute-start | bytes 712712 | tf_op jit(solution)/shard_map/ppermute | solution.py:49
  73.8 9.5 %collective-permute-start.9 = (bf16[32,3712]{1,0:T(8,128)(2,1)S(1)}, bf16[32,3712]{1,0:T(8,128)(2,1)S(1)}, u32[]{:S(2)}, u32[]{:S(2)}) collective-permute-start(bf16[32,3712]{1,0:T(8,128)(2,1)S(1)} %collective-permute-done.7.refs_5_), channel_id=1, source_target_pairs={{0,2},{2,4},{4,6},{6,8},{8,10},{10,12},{12,14},{14,0},{1,3},{3,5},... | collective-permute-start | bytes 712712 | tf_op jit(solution)/shard_map/ppermute | solution.py:51
  78.2 32.1 %copy-start = (bf16[1,2048,224]{1,2,0:T(8,128)(2,1)S(1)}, bf16[1,2048,224]{1,2,0:T(8,128)(2,1)}, u32[]{:S(2)}) copy-start(bf16[1,2048,224]{1,2,0:T(8,128)(2,1)} %param.9) | copy-start | bytes 2752516
  88.5 20.9 %all-to-all-start.1 = ((bf16[8,128,256]{2,1,0:T(8,128)(2,1)}), bf16[8,128,256]{2,1,0:T(8,128)(2,1)S(1)}, u32[]{:S(2)}, u32[]{:S(2)}) async-start(bf16[8,128,256]{2,1,0:T(8,128)(2,1)} %get-tuple-element.20), calls=%async_computation.1 | async-start | bytes 1048576 | tf_op jit(solution)/shard_map/all_to_all | solution.py:236
  97.6 11.8 %collective-permute-start.10 = (bf16[224,2048]{1,0:T(8,128)(2,1)}, bf16[224,2048]{1,0:T(8,128)(2,1)S(1)}, u32[]{:S(2)}, u32[]{:S(2)}) collective-permute-start(bf16[224,2048]{1,0:T(8,128)(2,1)} %copy-done.2), channel_id=1, source_target_pairs={{0,1},{1,0},{2,3},{3,2},{4,5},{5,4},{6,7},{7,6},{8,9},{9,8},{10,11... | collective-permute-start | bytes 2752520 | tf_op jit(solution)/shard_map/ppermute | solution.py:235
  109.4 0.9 copy-start.3
  115.4 41.8 %copy-start.1 = (bf16[64,8]{1,0:T(8,128)(2,1)S(1)}, bf16[64,8]{1,0:T(8,128)(2,1)}, u32[]{:S(2)}) copy-start(bf16[64,8]{1,0:T(8,128)(2,1)} %get-tuple-element.24.place_ref) | copy-start | bytes 3076

commit v8 on v6

--- a/solution.py
+++ b/solution.py
@@ -51,7 +51,14 @@
     return got
 
 
-def pack_kernel(picks_ref, gates_ref, tok_ref, send_ref, place_ref):
+def pack_kernel(*refs):
+    sources, (send_ref, place_ref), held, sems = refs[:3], refs[3:5], refs[5:8], refs[8]
+    copies = [pltpu.make_async_copy(sources[i], held[i], sems.at[i]) for i in range(3)]
+    for copy in copies:
+        copy.start()
+    picks_ref, gates_ref, tok_ref = held
+    copies[0].wait()
+    copies[1].wait()
     visits, toks = picks_ref.shape
     groups, _, wide = send_ref.shape
     half = wide - LANES
@@ -67,6 +74,7 @@
             tail += jnp.where(lane == e, gate, 0.0)
     place = place.astype(bf16)
     place_ref[...] = place
+    copies[2].wait()
     for h in range(2):
         send_ref[:, h, :half] = dot(place, tok_ref[:, h * half : (h + 1) * half]).astype(bf16)
         send_ref[:, h, half:] = tail.astype(bf16)
@@ -101,7 +109,10 @@
 
 
 def hidden_kernel(steps, at_ref, gu_ref, other_ref, *refs):
-    blocks, (out_ref, buf, sems) = refs[:-3], refs[-3:]
+    blocks, (out_ref, buf, sems, late, late_sem) = refs[:-5], refs[-5:]
+    last = pltpu.make_async_copy(blocks[-1], late, late_sem)
+    last.start()
+    blocks = blocks[:-1] + (late,)
     depth = gu_ref.shape[0] // CHUNKS
     copies = []
     for i, w in enumerate((gu_ref, other_ref)):
@@ -117,6 +128,7 @@
     width = gu_ref.shape[0]
     units = gu_ref.shape[1] // 2
     hr = r // 2
+    last.wait()
     rows = jnp.concatenate([b[:, :width] for b in blocks], axis=0)
     tail = jnp.concatenate([b[:, width:] for b in blocks], axis=0).astype(f32)
     gate = jnp.where(at_ref[2] == 0, tail[:, 0:1], tail[:, 1:2])
@@ -193,13 +205,15 @@
     feats, units = dn.shape[0], dn.shape[1] // n
     swap = [(0, 1), (1, 0)]
     pair = [(i, i ^ 1) for i in range(n)]
+    asked = (node_picks.T, gates.transpose(1, 2, 0), tokens)
     send, place = call(
         pack_kernel,
         [((groups, 2, half + LANES), bf16), ((groups, toks), bf16)],
-        [VMEM] * 3,
+        [HBM] * 3,
         "pack",
-        room=60,
-    )(node_picks.T, gates.transpose(1, 2, 0), tokens)
+        [pltpu.VMEM(a.shape, a.dtype) for a in asked] + [pltpu.SemaphoreType.DMA((3,))],
+        60,
+    )(*asked)
     dn_pair = lax.ppermute(dn, "x", pair)
     dn_pair, mine = lax.optimization_barrier((dn_pair, gu))
     gu_other = lax.ppermute(mine, "core", swap)
@@ -217,12 +231,12 @@
     (hid,) = call(
         functools.partial(hidden_kernel, steps),
         [((n, n * r // 2, units), bf16)],
-        [SMEM, HBM, HBM] + [VMEM] * n,
+        [SMEM, HBM, HBM] + [VMEM] * (n - 1) + [HBM],
         "hidden",
-        [pltpu.VMEM((2,) + gu.shape, bf16), pltpu.SemaphoreType.DMA((2, CHUNKS))],
+        [pltpu.VMEM((2,) + gu.shape, bf16), pltpu.SemaphoreType.DMA((2, CHUNKS))]
+        + [pltpu.VMEM(rows.shape, bf16), pltpu.SemaphoreType.DMA],
         HID,
     )(at, gu, gu_other, *[b for _, b in got])
-    hid, dn_pair = lax.optimization_barrier((hid, dn_pair))
     dn_both = lax.ppermute(dn_pair, "core", swap)
     hid = lax.all_to_all(hid, "x", split_axis=0, concat_axis=0, tiled=True)
     (out,) = call(

time: 148 us -> 148 us (level)
    all_to_all x1, waiting for transfers between devices: 11.4 us -> 13.6 us  [shards(): hid = lax.all_to_all(hid, 'x', split_axis=0, concat_axis=0, tiled=True)]
    ppermute x1, waiting for transfers between devices: 7.19 us -> 5.13 us  [ring(): got.append((n // 2, lax.ppermute(fwd, 'x', up)))]
  transfers between devices with their start and end apart: 13 -> 13, of which waited for: 7 -> 7; matrix products, arithmetic and copies ran while one was open for 0% -> 0% of each run, Pallas kernels for 2% -> 6%
where the time goes in v8:
time: 148 us; the launch traced here: 147 us
  starting transfers between devices  61.8 us (42%)
  waiting for transfers between devices  39.5 us (27%)
  blocking collectives  32.4 us (22%)
  Pallas kernels  12.7 us (9%)
    all_to_all x1, starting transfers between devices, shards(): lax.all_to_all(send, group, split_axis=0, concat_axis=0, tiled=True)  23.2 us
    all_to_all x1, blocking collectives, shards(): lax.all_to_all(padded, group, split_axis=0, concat_axis=0, tiled=True)  19.9 us
    ppermute x3, starting transfers between devices, ring(): back = lax.ppermute(back, 'x', down)  14.9 us
    all_to_all x1, waiting for transfers between devices, shards(): lax.all_to_all(send, group, split_axis=0, concat_axis=0, tiled=True)  13.7 us
    all_to_all x1, waiting for transfers between devices, shards(): hid = lax.all_to_all(hid, 'x', split_axis=0, concat_axis=0, tiled=True)  13.6 us
    all_to_all x1, blocking collectives, shards(): back = lax.all_to_all(out, 'x', split_axis=0, concat_axis=0, tiled=True)  12.5 us
    ppermute x3, waiting for transfers between devices, ring(): fwd = lax.ppermute(fwd, 'x', up)  6.71 us
    ppermute x3, starting transfers between devices, ring(): fwd = lax.ppermute(fwd, 'x', up)  6.2 us
  transfers between devices with their start and end apart: 13, of which 7 were waited for; matrix products, arithmetic and copies ran while one was open for 0% of the time, Pallas kernels for 6%

profile of v8, /device:TPU:32, one launch (start us, length us, event | category | flops | bytes accessed | tf_op | source)
XLA Modules:
  0.0 146.7 jit_solution(8376814544566463982)
XLA Ops:
  0.0 3.4 %collective-permute-start = (bf16[224,2048]{1,0:T(8,128)(2,1)}, bf16[224,2048]{1,0:T(8,128)(2,1)S(1)}, u32[]{:S(2)}, u32[]{:S(2)}) collective-permute-start(bf16[224,2048]{1,0:T(8,128)(2,1)} %bitcast.9), channel_id=1, source_target_pairs={{0,2},{2,0},{4,6},{6,4},{8,10},{10,8},{12,14},{14,12},{1,3},{3,1},... | collective-permute-start | bytes 2752520 | tf_op jit(solution)/shard_map/ppermute | solution.py:217
  3.4 2.1 %pack.1 = (bf16[64,2,1920]{2,1,0:T(2,128)(2,1)}, bf16[64,8]{1,0:T(8,128)(2,1)}) custom-call(s32[4,8]{1,0:T(4,128)} %bitcast.14, bf16[4,2,8]{2,1,0:T(2,128)(2,1)} %bitcast.15, bf16[8,3584]{1,0:T(8,128)(2,1)} %refs_2_.1), custom_call_target="tpu_custom_call" | custom-call | tf_op jit(solution)/shard_map/pack/pallas_call | solution.py:209
  5.5 23.2 %all-to-all-start = ((bf16[64,2,1920]{2,1,0:T(2,128)(2,1)}), bf16[64,2,1920]{2,1,0:T(2,128)(2,1)S(1)}, u32[]{:S(2)}, u32[]{:S(2)}) async-start(bf16[64,2,1920]{2,1,0:T(2,128)(2,1)} %get-tuple-element.14), calls=%async_computation | async-start | bytes 983040 | tf_op jit(solution)/shard_map/all_to_all | solution.py:221
  28.6 1.9 %collective-permute-start.2 = (bf16[224,2048]{1,0:T(8,128)(2,1)}, bf16[224,2048]{1,0:T(8,128)(2,1)}, u32[]{:S(2)}, u32[]{:S(2)}) collective-permute-start(bf16[224,2048]{1,0:T(8,128)(2,1)} %bitcast.10), channel_id=1, source_target_pairs={{0,1},{1,0},{2,3},{3,2},{4,5},{5,4},{6,7},{7,6},{8,9},{9,8},{10,11... | collective-permute-start | bytes 2752520 | tf_op jit(solution)/shard_map/ppermute | solution.py:220
  30.6 0.0 collective-permute-done.pair_ref
  30.6 0.0 copy-start.2
  30.6 2.4 %collective-permute-start.1 = (bf16[3584,256]{1,0:T(8,128)(2,1)}, bf16[3584,256]{1,0:T(8,128)(2,1)}, u32[]{:S(2)}, u32[]{:S(2)}) collective-permute-start(bf16[3584,256]{1,0:T(8,128)(2,1)} %bitcast.12), channel_id=1, source_target_pairs={{0,1},{1,0},{2,3},{3,2},{4,5},{5,4},{6,7},{7,6},{8,9},{9,8},{10,11... | collective-permute-start | bytes 5505032 | tf_op jit(solution)/shard_map/ppermute | solution.py:219
  33.0 0.3 collective-permute-done.2.other_ref
  33.3 13.7 %all-to-all-done.in_ref = bf16[64,2,1920]{2,1,0:T(2,128)(2,1)S(1)} async-done(((bf16[64,2,1920]{2,1,0:T(2,128)(2,1)}), bf16[64,2,1920]{2,1,0:T(2,128)(2,1)S(1)}, u32[]{:S(2)}, u32[]{:S(2)}) %all-to-all-start) | async-done | bytes 491552 | tf_op jit(solution)/shard_map/all_to_all | solution.py:221
  47.1 0.6 compact.1
  47.7 2.4 %collective-permute-start.3 = (bf16[32,3712]{1,0:T(8,128)(2,1)S(1)}, bf16[32,3712]{1,0:T(8,128)(2,1)S(1)}, u32[]{:S(2)}, u32[]{:S(2)}) collective-permute-start(bf16[32,3712]{1,0:T(8,128)(2,1)S(1)} %get-tuple-element.16.refs_0_), channel_id=1, source_target_pairs={{0,2},{2,4},{4,6},{6,8},{8,10},{10,12},{12,14},{14,0},{1,3},{3,5},... | collective-permute-start | bytes 712712 | tf_op jit(solution)/shard_map/ppermute | solution.py:47
  50.1 4.7 %collective-permute-start.4 = (bf16[32,3712]{1,0:T(8,128)(2,1)S(1)}, bf16[32,3712]{1,0:T(8,128)(2,1)S(1)}, u32[]{:S(2)}, u32[]{:S(2)}) collective-permute-start(bf16[32,3712]{1,0:T(8,128)(2,1)S(1)} %get-tuple-element.16.refs_0_), channel_id=1, source_target_pairs={{0,14},{2,0},{4,2},{6,4},{8,6},{10,8},{12,10},{14,12},{1,15},{3,1}... | collective-permute-start | bytes 712712 | tf_op jit(solution)/shard_map/ppermute | solution.py:48
  54.7 0.0 copy-done.2
  54.8 2.1 %collective-permute-done.3.refs_1_ = bf16[32,3712]{1,0:T(8,128)(2,1)S(1)} collective-permute-done((bf16[32,3712]{1,0:T(8,128)(2,1)S(1)}, bf16[32,3712]{1,0:T(8,128)(2,1)S(1)}, u32[]{:S(2)}, u32[]{:S(2)}) %collective-permute-start.3) | collective-permute-done | bytes 237600 | tf_op jit(solution)/shard_map/ppermute | solution.py:47
  56.9 1.9 %collective-permute-start.5 = (bf16[32,3712]{1,0:T(8,128)(2,1)S(1)}, bf16[32,3712]{1,0:T(8,128)(2,1)S(1)}, u32[]{:S(2)}, u32[]{:S(2)}) collective-permute-start(bf16[32,3712]{1,0:T(8,128)(2,1)S(1)} %collective-permute-done.3.refs_1_), channel_id=1, source_target_pairs={{0,2},{2,4},{4,6},{6,8},{8,10},{10,12},{12,14},{14,0},{1,3},{3,5},... | collective-permute-start | bytes 712712 | tf_op jit(solution)/shard_map/ppermute | solution.py:47
  58.8 0.0 collective-permute-done.4.refs_2_
  58.8 5.1 %collective-permute-start.6 = (bf16[32,3712]{1,0:T(8,128)(2,1)S(1)}, bf16[32,3712]{1,0:T(8,128)(2,1)S(1)}, u32[]{:S(2)}, u32[]{:S(2)}) collective-permute-start(bf16[32,3712]{1,0:T(8,128)(2,1)S(1)} %collective-permute-done.4.refs_2_), channel_id=1, source_target_pairs={{0,14},{2,0},{4,2},{6,4},{8,6},{10,8},{12,10},{14,12},{1,15},{3,1}... | collective-permute-start | bytes 712712 | tf_op jit(solution)/shard_map/ppermute | solution.py:48
  64.0 2.1 %collective-permute-done.5.refs_3_ = bf16[32,3712]{1,0:T(8,128)(2,1)S(1)} collective-permute-done((bf16[32,3712]{1,0:T(8,128)(2,1)S(1)}, bf16[32,3712]{1,0:T(8,128)(2,1)S(1)}, u32[]{:S(2)}, u32[]{:S(2)}) %collective-permute-start.5) | collective-permute-done | bytes 237600 | tf_op jit(solution)/shard_map/ppermute | solution.py:47
  66.1 1.9 %collective-permute-start.7 = (bf16[32,3712]{1,0:T(8,128)(2,1)S(1)}, bf16[32,3712]{1,0:T(8,128)(2,1)S(1)}, u32[]{:S(2)}, u32[]{:S(2)}) collective-permute-start(bf16[32,3712]{1,0:T(8,128)(2,1)S(1)} %collective-permute-done.5.refs_3_), channel_id=1, source_target_pairs={{0,2},{2,4},{4,6},{6,8},{8,10},{10,12},{12,14},{14,0},{1,3},{3,5},... | collective-permute-start | bytes 712712 | tf_op jit(solution)/shard_map/ppermute | solution.py:47
  68.0 0.0 collective-permute-done.6.refs_4_
  68.0 5.1 %collective-permute-start.8 = (bf16[32,3712]{1,0:T(8,128)(2,1)S(1)}, bf16[32,3712]{1,0:T(8,128)(2,1)S(1)}, u32[]{:S(2)}, u32[]{:S(2)}) collective-permute-start(bf16[32,3712]{1,0:T(8,128)(2,1)S(1)} %collective-permute-done.6.refs_4_), channel_id=1, source_target_pairs={{0,14},{2,0},{4,2},{6,4},{8,6},{10,8},{12,10},{14,12},{1,15},{3,1}... | collective-permute-start | bytes 712712 | tf_op jit(solution)/shard_map/ppermute | solution.py:48
  73.2 2.4 %collective-permute-done.7.refs_5_ = bf16[32,3712]{1,0:T(8,128)(2,1)S(1)} collective-permute-done((bf16[32,3712]{1,0:T(8,128)(2,1)S(1)}, bf16[32,3712]{1,0:T(8,128)(2,1)S(1)}, u32[]{:S(2)}, u32[]{:S(2)}) %collective-permute-start.7) | collective-permute-done | bytes 237600 | tf_op jit(solution)/shard_map/ppermute | solution.py:47
  75.6 1.9 %collective-permute-start.9 = (bf16[32,3712]{1,0:T(8,128)(2,1)S(1)}, bf16[32,3712]{1,0:T(8,128)(2,1)S(1)}, u32[]{:S(2)}, u32[]{:S(2)}) collective-permute-start(bf16[32,3712]{1,0:T(8,128)(2,1)S(1)} %collective-permute-done.7.refs_5_), channel_id=1, source_target_pairs={{0,2},{2,4},{4,6},{6,8},{8,10},{10,12},{12,14},{14,0},{1,3},{3,5},... | collective-permute-start | bytes 712712 | tf_op jit(solution)/shard_map/ppermute | solution.py:50
  77.5 0.1 pad_add_fusion.at_ref
  77.6 0.0 copy-start
  77.6 2.0 %collective-permute-start.10 = (bf16[224,2048]{1,0:T(8,128)(2,1)}, bf16[224,2048]{1,0:T(8,128)(2,1)}, u32[]{:S(2)}, u32[]{:S(2)}) collective-permute-start(bf16[224,2048]{1,0:T(8,128)(2,1)} %copy-done.2), channel_id=1, source_target_pairs={{0,1},{1,0},{2,3},{3,2},{4,5},{5,4},{6,7},{7,6},{8,9},{9,8},{10,11... | collective-permute-start | bytes 2752520 | tf_op jit(solution)/shard_map/ppermute | solution.py:240
  79.7 0.0 collective-permute-done.8.refs_6_
  79.7 5.1 %collective-permute-done.9.refs_7_ = bf16[32,3712]{1,0:T(8,128)(2,1)S(1)} collective-permute-done((bf16[32,3712]{1,0:T(8,128)(2,1)S(1)}, bf16[32,3712]{1,0:T(8,128)(2,1)S(1)}, u32[]{:S(2)}, u32[]{:S(2)}) %collective-permute-start.9) | collective-permute-done | bytes 237600 | tf_op jit(solution)/shard_map/ppermute | solution.py:50
  84.8 0.0 collective-permute-done.1.other_ref
  84.8 5.5 %hidden.1 = bf16[8,128,256]{2,1,0:T(8,128)(2,1)} custom-call(s32[3]{0:T(128)S(1)} %pad_add_fusion.at_ref, bf16[3584,256]{1,0:T(8,128)(2,1)} %bitcast.13, bf16[3584,256]{1,0:T(8,128)(2,1)} %collective-permute-done.1.other_ref, bf16[32,3712]{1,0:T(8,128)(2,1)S(1)} %get-tuple-element.16.refs_0_, bf16[32,3712]{1,0:T(8,128)(2,1)S(1)} %collective-permute-done.3.refs_1_, ...), custom_call_target="tpu_custom_call" | custom-call | tf_op jit(solution)/shard_map/hidden/pallas_call | solution.py:231
  90.4 5.8 %all-to-all-start.1 = ((bf16[8,128,256]{2,1,0:T(8,128)(2,1)}), bf16[8,128,256]{2,1,0:T(8,128)(2,1)S(1)}, u32[]{:S(2)}, u32[]{:S(2)}) async-start(bf16[8,128,256]{2,1,0:T(8,128)(2,1)} %hidden.1), calls=%async_computation.1 | async-start | bytes 1048576 | tf_op jit(solution)/shard_map/all_to_all | solution.py:241
  96.2 0.0 collective-permute-done.10.both_ref
  96.2 13.6 %all-to-all-done.1.h_ref = bf16[8,128,256]{2,1,0:T(8,128)(2,1)S(1)} async-done(((bf16[8,128,256]{2,1,0:T(8,128)(2,1)}), bf16[8,128,256]{2,1,0:T(8,128)(2,1)S(1)}, u32[]{:S(2)}, u32[]{:S(2)}) %all-to-all-start.1) | async-done | bytes 524320 | tf_op jit(solution)/shard_map/all_to_all | solution.py:241
  109.8 0.0 copy-done
  109.8 3.2 %down.1 = bf16[8,16,896]{2,1,0:T(8,128)(2,1)S(1)} custom-call(s32[3]{0:T(128)S(1)} %pad_add_fusion.at_ref, bf16[8,128,256]{2,1,0:T(8,128)(2,1)S(1)} %all-to-all-done.1.h_ref, bf16[224,2048]{1,0:T(8,128)(2,1)S(1)} %bitcast.11, bf16[224,2048]{1,0:T(8,128)(2,1)} %collective-permute-done.2.other_ref, bf16[224,2048]{1,0:T(8,128)(2,1)} %copy-done.2, ...), custom_call_target="tpu_custom_call" | custom-call | tf_op jit(solution)/shard_map/down/pallas_call | solution.py:242
  113.0 0.0 copy-start.1
  113.0 12.5 %all_to_all.20.back_ref = bf16[8,16,896]{2,1,0:T(8,128)(2,1)S(1)} all-to-all(bf16[8,16,896]{2,1,0:T(8,128)(2,1)S(1)} %down.1), channel_id=1, replica_groups=mesh['y'=8,'z'=8,'x'=8,'core'=2] {'x'}, dimensions={0} | all-to-all | bytes 458752 | tf_op jit(solution)/shard_map/all_to_all | solution.py:249
  125.5 0.3 spread.1
  125.9 19.9 %all_to_all.21.in_ref = bf16[64,2,1792]{2,1,0:T(2,128)(2,1)S(1)} all-to-all(bf16[64,2,1792]{2,1,0:T(2,128)(2,1)S(1)} %spread.1), channel_id=1, replica_groups=mesh['y'=8,'z'=8,'x'=8,'core'=2] {'y','z'}, dimensions={0} | all-to-all | bytes 917504 | tf_op jit(solution)/shard_map/all_to_all | solution.py:253
  145.8 0.0 copy-done.1
  145.8 0.9 mix.1
Async XLA Ops:
  0.0 30.6 %collective-permute-start = (bf16[224,2048]{1,0:T(8,128)(2,1)}, bf16[224,2048]{1,0:T(8,128)(2,1)S(1)}, u32[]{:S(2)}, u32[]{:S(2)}) collective-permute-start(bf16[224,2048]{1,0:T(8,128)(2,1)} %bitcast.9), channel_id=1, source_target_pairs={{0,2},{2,0},{4,6},{6,4},{8,10},{10,8},{12,14},{14,12},{1,3},{3,1},... | collective-permute-start | bytes 2752520 | tf_op jit(solution)/shard_map/ppermute | solution.py:217
  5.5 41.6 %all-to-all-start = ((bf16[64,2,1920]{2,1,0:T(2,128)(2,1)}), bf16[64,2,1920]{2,1,0:T(2,128)(2,1)S(1)}, u32[]{:S(2)}, u32[]{:S(2)}) async-start(bf16[64,2,1920]{2,1,0:T(2,128)(2,1)} %get-tuple-element.14), calls=%async_computation | async-start | bytes 983040 | tf_op jit(solution)/shard_map/all_to_all | solution.py:221
  28.6 4.7 %collective-permute-start.2 = (bf16[224,2048]{1,0:T(8,128)(2,1)}, bf16[224,2048]{1,0:T(8,128)(2,1)}, u32[]{:S(2)}, u32[]{:S(2)}) collective-permute-start(bf16[224,2048]{1,0:T(8,128)(2,1)} %bitcast.10), channel_id=1, source_target_pairs={{0,1},{1,0},{2,3},{3,2},{4,5},{5,4},{6,7},{7,6},{8,9},{9,8},{10,11... | collective-permute-start | bytes 2752520 | tf_op jit(solution)/shard_map/ppermute | solution.py:220
  30.6 24.2 %copy-start.2 = (bf16[224,2048]{1,0:T(8,128)(2,1)}, bf16[224,2048]{1,0:T(8,128)(2,1)S(1)}, u32[]{:S(2)}) copy-start(bf16[224,2048]{1,0:T(8,128)(2,1)S(1)} %collective-permute-done.pair_ref) | copy-start | bytes 2752516
  30.6 54.2 %collective-permute-start.1 = (bf16[3584,256]{1,0:T(8,128)(2,1)}, bf16[3584,256]{1,0:T(8,128)(2,1)}, u32[]{:S(2)}, u32[]{:S(2)}) collective-permute-start(bf16[3584,256]{1,0:T(8,128)(2,1)} %bitcast.12), channel_id=1, source_target_pairs={{0,1},{1,0},{2,3},{3,2},{4,5},{5,4},{6,7},{7,6},{8,9},{9,8},{10,11... | collective-permute-start | bytes 5505032 | tf_op jit(solution)/shard_map/ppermute | solution.py:219
  47.7 9.2 %collective-permute-start.3 = (bf16[32,3712]{1,0:T(8,128)(2,1)S(1)}, bf16[32,3712]{1,0:T(8,128)(2,1)S(1)}, u32[]{:S(2)}, u32[]{:S(2)}) collective-permute-start(bf16[32,3712]{1,0:T(8,128)(2,1)S(1)} %get-tuple-element.16.refs_0_), channel_id=1, source_target_pairs={{0,2},{2,4},{4,6},{6,8},{8,10},{10,12},{12,14},{14,0},{1,3},{3,5},... | collective-permute-start | bytes 712712 | tf_op jit(solution)/shard_map/ppermute | solution.py:47
  50.1 8.7 %collective-permute-start.4 = (bf16[32,3712]{1,0:T(8,128)(2,1)S(1)}, bf16[32,3712]{1,0:T(8,128)(2,1)S(1)}, u32[]{:S(2)}, u32[]{:S(2)}) collective-permute-start(bf16[32,3712]{1,0:T(8,128)(2,1)S(1)} %get-tuple-element.16.refs_0_), channel_id=1, source_target_pairs={{0,14},{2,0},{4,2},{6,4},{8,6},{10,8},{12,10},{14,12},{1,15},{3,1}... | collective-permute-start | bytes 712712 | tf_op jit(solution)/shard_map/ppermute | solution.py:48
  56.9 9.2 %collective-permute-start.5 = (bf16[32,3712]{1,0:T(8,128)(2,1)S(1)}, bf16[32,3712]{1,0:T(8,128)(2,1)S(1)}, u32[]{:S(2)}, u32[]{:S(2)}) collective-permute-start(bf16[32,3712]{1,0:T(8,128)(2,1)S(1)} %collective-permute-done.3.refs_1_), channel_id=1, source_target_pairs={{0,2},{2,4},{4,6},{6,8},{8,10},{10,12},{12,14},{14,0},{1,3},{3,5},... | collective-permute-start | bytes 712712 | tf_op jit(solution)/shard_map/ppermute | solution.py:47
  58.8 9.2 %collective-permute-start.6 = (bf16[32,3712]{1,0:T(8,128)(2,1)S(1)}, bf16[32,3712]{1,0:T(8,128)(2,1)S(1)}, u32[]{:S(2)}, u32[]{:S(2)}) collective-permute-start(bf16[32,3712]{1,0:T(8,128)(2,1)S(1)} %collective-permute-done.4.refs_2_), channel_id=1, source_target_pairs={{0,14},{2,0},{4,2},{6,4},{8,6},{10,8},{12,10},{14,12},{1,15},{3,1}... | collective-permute-start | bytes 712712 | tf_op jit(solution)/shard_map/ppermute | solution.py:48
  66.1 9.5 %collective-permute-start.7 = (bf16[32,3712]{1,0:T(8,128)(2,1)S(1)}, bf16[32,3712]{1,0:T(8,128)(2,1)S(1)}, u32[]{:S(2)}, u32[]{:S(2)}) collective-permute-start(bf16[32,3712]{1,0:T(8,128)(2,1)S(1)} %collective-permute-done.5.refs_3_), channel_id=1, source_target_pairs={{0,2},{2,4},{4,6},{6,8},{8,10},{10,12},{12,14},{14,0},{1,3},{3,5},... | collective-permute-start | bytes 712712 | tf_op jit(solution)/shard_map/ppermute | solution.py:47
  68.0 11.6 %collective-permute-start.8 = (bf16[32,3712]{1,0:T(8,128)(2,1)S(1)}, bf16[32,3712]{1,0:T(8,128)(2,1)S(1)}, u32[]{:S(2)}, u32[]{:S(2)}) collective-permute-start(bf16[32,3712]{1,0:T(8,128)(2,1)S(1)} %collective-permute-done.6.refs_4_), channel_id=1, source_target_pairs={{0,14},{2,0},{4,2},{6,4},{8,6},{10,8},{12,10},{14,12},{1,15},{3,1}... | collective-permute-start | bytes 712712 | tf_op jit(solution)/shard_map/ppermute | solution.py:48
  75.6 9.2 %collective-permute-start.9 = (bf16[32,3712]{1,0:T(8,128)(2,1)S(1)}, bf16[32,3712]{1,0:T(8,128)(2,1)S(1)}, u32[]{:S(2)}, u32[]{:S(2)}) collective-permute-start(bf16[32,3712]{1,0:T(8,128)(2,1)S(1)} %collective-permute-done.7.refs_5_), channel_id=1, source_target_pairs={{0,2},{2,4},{4,6},{6,8},{8,10},{10,12},{12,14},{14,0},{1,3},{3,5},... | collective-permute-start | bytes 712712 | tf_op jit(solution)/shard_map/ppermute | solution.py:50
  77.6 32.2 %copy-start = (bf16[1,2048,224]{1,2,0:T(8,128)(2,1)S(1)}, bf16[1,2048,224]{1,2,0:T(8,128)(2,1)}, u32[]{:S(2)}) copy-start(bf16[1,2048,224]{1,2,0:T(8,128)(2,1)} %param.9) | copy-start | bytes 2752516
  77.6 18.6 %collective-permute-start.10 = (bf16[224,2048]{1,0:T(8,128)(2,1)}, bf16[224,2048]{1,0:T(8,128)(2,1)}, u32[]{:S(2)}, u32[]{:S(2)}) collective-permute-start(bf16[224,2048]{1,0:T(8,128)(2,1)} %copy-done.2), channel_id=1, source_target_pairs={{0,1},{1,0},{2,3},{3,2},{4,5},{5,4},{6,7},{7,6},{8,9},{9,8},{10,11... | collective-permute-start | bytes 2752520 | tf_op jit(solution)/shard_map/ppermute | solution.py:240
  90.4 19.4 %all-to-all-start.1 = ((bf16[8,128,256]{2,1,0:T(8,128)(2,1)}), bf16[8,128,256]{2,1,0:T(8,128)(2,1)S(1)}, u32[]{:S(2)}, u32[]{:S(2)}) async-start(bf16[8,128,256]{2,1,0:T(8,128)(2,1)} %hidden.1), calls=%async_computation.1 | async-start | bytes 1048576 | tf_op jit(solution)/shard_map/all_to_all | solution.py:241
  113.0 32.8 %copy-start.1 = (bf16[64,8]{1,0:T(8,128)(2,1)S(1)}, bf16[64,8]{1,0:T(8,128)(2,1)}, u32[]{:S(2)}) copy-start(bf16[64,8]{1,0:T(8,128)(2,1)} %get-tuple-element.20.place_ref) | copy-start | bytes 3076

commit v9 on v8

--- a/solution.py
+++ b/solution.py
@@ -18,6 +18,9 @@
 CHUNKS = 4
 
 
+COSTS = {"compact": pl.CostEstimate(flops=10**10, bytes_accessed=2**24, transcendentals=0)}
+
+
 def dot(a, b):
     return jnp.dot(a, b, preferred_element_type=f32)
 
@@ -33,6 +36,7 @@
         in_specs=specs,
         out_specs=[VMEM] * len(outs),
         scratch_shapes=list(scratch),
+        cost_estimate=COSTS.get(name),
         compiler_params=pltpu.CompilerParams(vmem_limit_bytes=room * 2**20),
         name=name,
     )
@@ -42,12 +46,14 @@
     up = [(i, (i + 1) % n) for i in range(n)]
     down = [(i, (i - 1) % n) for i in range(n)]
     got = [(0, block)]
-    fwd = back = block
+    fwd = back = near = block
     for k in range(1, n // 2):
+        near = back
         fwd = lax.ppermute(fwd, "x", up)
         back = lax.ppermute(back, "x", down)
         got += [(k, fwd), (n - k, back)]
-    got.append((n // 2, lax.ppermute(fwd, "x", up)))
+    twice = [(i, (i - 2) % n) for i in range(n)]
+    got.append((n // 2, lax.ppermute(near, "x", twice)))
     return got
 
 
@@ -109,10 +115,7 @@
 
 
 def hidden_kernel(steps, at_ref, gu_ref, other_ref, *refs):
-    blocks, (out_ref, buf, sems, late, late_sem) = refs[:-5], refs[-5:]
-    last = pltpu.make_async_copy(blocks[-1], late, late_sem)
-    last.start()
-    blocks = blocks[:-1] + (late,)
+    blocks, (out_ref, buf, sems) = refs[:-3], refs[-3:]
     depth = gu_ref.shape[0] // CHUNKS
     copies = []
     for i, w in enumerate((gu_ref, other_ref)):
@@ -128,7 +131,6 @@
     width = gu_ref.shape[0]
     units = gu_ref.shape[1] // 2
     hr = r // 2
-    last.wait()
     rows = jnp.concatenate([b[:, :width] for b in blocks], axis=0)
     tail = jnp.concatenate([b[:, width:] for b in blocks], axis=0).astype(f32)
     gate = jnp.where(at_ref[2] == 0, tail[:, 0:1], tail[:, 1:2])
@@ -231,10 +233,9 @@
     (hid,) = call(
         functools.partial(hidden_kernel, steps),
         [((n, n * r // 2, units), bf16)],
-        [SMEM, HBM, HBM] + [VMEM] * (n - 1) + [HBM],
+        [SMEM, HBM, HBM] + [VMEM] * n,
         "hidden",
-        [pltpu.VMEM((2,) + gu.shape, bf16), pltpu.SemaphoreType.DMA((2, CHUNKS))]
-        + [pltpu.VMEM(rows.shape, bf16), pltpu.SemaphoreType.DMA],
+        [pltpu.VMEM((2,) + gu.shape, bf16), pltpu.SemaphoreType.DMA((2, CHUNKS))],
         HID,
     )(at, gu, gu_other, *[b for _, b in got])
     dn_both = lax.ppermute(dn_pair, "core", swap)

time: 148 us -> 147 us (level)
  waiting for transfers between devices: 39.5 us -> 35.4 us
  blocking collectives: 32.4 us -> 36.1 us
    ppermute x3, waiting for transfers between devices: 6.71 us -> 0.46 us  [ring(): fwd = lax.ppermute(fwd, 'x', up)]
    all_to_all x1, blocking collectives: 19.9 us -> 23.6 us  [shards(): lax.all_to_all(padded, group, split_axis=0, concat_axis=0, tiled=True)]
    ppermute x3, waiting for transfers between devices: 0.01 us -> 3.35 us  [ring(): back = lax.ppermute(back, 'x', down)]
    ppermute x1, waiting for transfers between devices: 5.13 us -> 3.51 us  [ring(): got.append((n // 2, lax.ppermute(near, 'x', twice)))]
    all_to_all x1, starting transfers between devices: 5.81 us -> 4.31 us  [shards(): hid = lax.all_to_all(hid, 'x', split_axis=0, concat_axis=0, tiled=True)]
  transfers between devices with their start and end apart: 13 -> 13, of which waited for: 7 -> 7; matrix products, arithmetic and copies ran while one was open for 0% -> 0% of each run, Pallas kernels for 6% -> 5%
where the time goes in v9:
time: 147 us; the launch traced here: 146 us
  starting transfers between devices  62.2 us (42%)
  blocking collectives  36.1 us (25%)
  waiting for transfers between devices  35.4 us (24%)
  Pallas kernels  12.3 us (8%)
    all_to_all x1, blocking collectives, shards(): lax.all_to_all(padded, group, split_axis=0, concat_axis=0, tiled=True)  23.6 us
    all_to_all x1, starting transfers between devices, shards(): lax.all_to_all(send, group, split_axis=0, concat_axis=0, tiled=True)  23.2 us
    ppermute x3, starting transfers between devices, ring(): back = lax.ppermute(back, 'x', down)  15.8 us
    all_to_all x1, waiting for transfers between devices, shards(): hid = lax.all_to_all(hid, 'x', split_axis=0, concat_axis=0, tiled=True)  14 us
    all_to_all x1, waiting for transfers between devices, shards(): lax.all_to_all(send, group, split_axis=0, concat_axis=0, tiled=True)  13.7 us
    all_to_all x1, blocking collectives, shards(): back = lax.all_to_all(out, 'x', split_axis=0, concat_axis=0, tiled=True)  12.5 us
    ppermute x3, starting transfers between devices, ring(): fwd = lax.ppermute(fwd, 'x', up)  6.93 us
    pallas_call x1, Pallas kernels, shards(): call(functools.partial(hidden_kernel, steps), [((n, n * r // 2, units), b...  5.23 us
  transfers between devices with their start and end apart: 13, of which 7 were waited for; matrix products, arithmetic and copies ran while one was open for 0% of the time, Pallas kernels for 5%

profile of v9, /device:TPU:32, one launch (start us, length us, event | category | flops | bytes accessed | tf_op | source)
XLA Modules:
  0.0 146.4 jit_solution(3296078109107598414)
XLA Ops:
  0.0 3.4 %collective-permute-start = (bf16[224,2048]{1,0:T(8,128)(2,1)}, bf16[224,2048]{1,0:T(8,128)(2,1)S(1)}, u32[]{:S(2)}, u32[]{:S(2)}) collective-permute-start(bf16[224,2048]{1,0:T(8,128)(2,1)} %bitcast.9), channel_id=1, source_target_pairs={{0,2},{2,0},{4,6},{6,4},{8,10},{10,8},{12,14},{14,12},{1,3},{3,1},... | collective-permute-start | bytes 2752520 | tf_op jit(solution)/shard_map/ppermute | solution.py:219
  3.4 2.1 %pack.1 = (bf16[64,2,1920]{2,1,0:T(2,128)(2,1)}, bf16[64,8]{1,0:T(8,128)(2,1)}) custom-call(s32[4,8]{1,0:T(4,128)} %bitcast.14, bf16[4,2,8]{2,1,0:T(2,128)(2,1)} %bitcast.15, bf16[8,3584]{1,0:T(8,128)(2,1)} %refs_2_.1), custom_call_target="tpu_custom_call" | custom-call | tf_op jit(solution)/shard_map/pack/pallas_call | solution.py:211
  5.5 23.2 %all-to-all-start = ((bf16[64,2,1920]{2,1,0:T(2,128)(2,1)}), bf16[64,2,1920]{2,1,0:T(2,128)(2,1)S(1)}, u32[]{:S(2)}, u32[]{:S(2)}) async-start(bf16[64,2,1920]{2,1,0:T(2,128)(2,1)} %get-tuple-element.14), calls=%async_computation | async-start | bytes 983040 | tf_op jit(solution)/shard_map/all_to_all | solution.py:223
  28.6 1.9 %collective-permute-start.2 = (bf16[224,2048]{1,0:T(8,128)(2,1)}, bf16[224,2048]{1,0:T(8,128)(2,1)}, u32[]{:S(2)}, u32[]{:S(2)}) collective-permute-start(bf16[224,2048]{1,0:T(8,128)(2,1)} %bitcast.10), channel_id=1, source_target_pairs={{0,1},{1,0},{2,3},{3,2},{4,5},{5,4},{6,7},{7,6},{8,9},{9,8},{10,11... | collective-permute-start | bytes 2752520 | tf_op jit(solution)/shard_map/ppermute | solution.py:222
  30.6 0.0 collective-permute-done.pair_ref
  30.6 0.0 copy-start.2
  30.6 2.4 %collective-permute-start.1 = (bf16[3584,256]{1,0:T(8,128)(2,1)}, bf16[3584,256]{1,0:T(8,128)(2,1)}, u32[]{:S(2)}, u32[]{:S(2)}) collective-permute-start(bf16[3584,256]{1,0:T(8,128)(2,1)} %bitcast.12), channel_id=1, source_target_pairs={{0,1},{1,0},{2,3},{3,2},{4,5},{5,4},{6,7},{7,6},{8,9},{9,8},{10,11... | collective-permute-start | bytes 5505032 | tf_op jit(solution)/shard_map/ppermute | solution.py:221
  33.0 0.3 collective-permute-done.2.other_ref
  33.3 13.7 %all-to-all-done.in_ref = bf16[64,2,1920]{2,1,0:T(2,128)(2,1)S(1)} async-done(((bf16[64,2,1920]{2,1,0:T(2,128)(2,1)}), bf16[64,2,1920]{2,1,0:T(2,128)(2,1)S(1)}, u32[]{:S(2)}, u32[]{:S(2)}) %all-to-all-start) | async-done | bytes 491552 | tf_op jit(solution)/shard_map/all_to_all | solution.py:223
  47.1 0.6 compact.1
  47.7 0.0 copy-done.2
  47.7 4.7 %collective-permute-start.4 = (bf16[32,3712]{1,0:T(8,128)(2,1)S(1)}, bf16[32,3712]{1,0:T(8,128)(2,1)S(1)}, u32[]{:S(2)}, u32[]{:S(2)}) collective-permute-start(bf16[32,3712]{1,0:T(8,128)(2,1)S(1)} %get-tuple-element.16.refs_0_), channel_id=1, source_target_pairs={{0,14},{2,0},{4,2},{6,4},{8,6},{10,8},{12,10},{14,12},{1,15},{3,1}... | collective-permute-start | bytes 712712 | tf_op jit(solution)/shard_map/ppermute | solution.py:53
  52.4 1.9 %collective-permute-start.3 = (bf16[32,3712]{1,0:T(8,128)(2,1)S(1)}, bf16[32,3712]{1,0:T(8,128)(2,1)S(1)}, u32[]{:S(2)}, u32[]{:S(2)}) collective-permute-start(bf16[32,3712]{1,0:T(8,128)(2,1)S(1)} %get-tuple-element.16.refs_0_), channel_id=1, source_target_pairs={{0,2},{2,4},{4,6},{6,8},{8,10},{10,12},{12,14},{14,0},{1,3},{3,5},... | collective-permute-start | bytes 712712 | tf_op jit(solution)/shard_map/ppermute | solution.py:52
  54.3 1.7 %collective-permute-done.4.refs_2_ = bf16[32,3712]{1,0:T(8,128)(2,1)S(1)} collective-permute-done((bf16[32,3712]{1,0:T(8,128)(2,1)S(1)}, bf16[32,3712]{1,0:T(8,128)(2,1)S(1)}, u32[]{:S(2)}, u32[]{:S(2)}) %collective-permute-start.4) | collective-permute-done | bytes 237600 | tf_op jit(solution)/shard_map/ppermute | solution.py:53
  56.0 5.6 %collective-permute-start.6 = (bf16[32,3712]{1,0:T(8,128)(2,1)S(1)}, bf16[32,3712]{1,0:T(8,128)(2,1)S(1)}, u32[]{:S(2)}, u32[]{:S(2)}) collective-permute-start(bf16[32,3712]{1,0:T(8,128)(2,1)S(1)} %collective-permute-done.4.refs_2_), channel_id=1, source_target_pairs={{0,14},{2,0},{4,2},{6,4},{8,6},{10,8},{12,10},{14,12},{1,15},{3,1}... | collective-permute-start | bytes 712712 | tf_op jit(solution)/shard_map/ppermute | solution.py:53
  61.6 0.0 collective-permute-done.3.refs_1_
  61.6 1.9 %collective-permute-start.5 = (bf16[32,3712]{1,0:T(8,128)(2,1)S(1)}, bf16[32,3712]{1,0:T(8,128)(2,1)S(1)}, u32[]{:S(2)}, u32[]{:S(2)}) collective-permute-start(bf16[32,3712]{1,0:T(8,128)(2,1)S(1)} %collective-permute-done.3.refs_1_), channel_id=1, source_target_pairs={{0,2},{2,4},{4,6},{6,8},{8,10},{10,12},{12,14},{14,0},{1,3},{3,5},... | collective-permute-start | bytes 712712 | tf_op jit(solution)/shard_map/ppermute | solution.py:52
  63.5 1.7 %collective-permute-done.6.refs_4_ = bf16[32,3712]{1,0:T(8,128)(2,1)S(1)} collective-permute-done((bf16[32,3712]{1,0:T(8,128)(2,1)S(1)}, bf16[32,3712]{1,0:T(8,128)(2,1)S(1)}, u32[]{:S(2)}, u32[]{:S(2)}) %collective-permute-start.6) | collective-permute-done | bytes 237600 | tf_op jit(solution)/shard_map/ppermute | solution.py:53
  65.2 5.6 %collective-permute-start.8 = (bf16[32,3712]{1,0:T(8,128)(2,1)S(1)}, bf16[32,3712]{1,0:T(8,128)(2,1)S(1)}, u32[]{:S(2)}, u32[]{:S(2)}) collective-permute-start(bf16[32,3712]{1,0:T(8,128)(2,1)S(1)} %collective-permute-done.6.refs_4_), channel_id=1, source_target_pairs={{0,14},{2,0},{4,2},{6,4},{8,6},{10,8},{12,10},{14,12},{1,15},{3,1}... | collective-permute-start | bytes 712712 | tf_op jit(solution)/shard_map/ppermute | solution.py:53
  70.8 2.2 %collective-permute-start.9 = (bf16[32,3712]{1,0:T(8,128)(2,1)S(1)}, bf16[32,3712]{1,0:T(8,128)(2,1)S(1)}, u32[]{:S(2)}, u32[]{:S(2)}) collective-permute-start(bf16[32,3712]{1,0:T(8,128)(2,1)S(1)} %collective-permute-done.6.refs_4_), channel_id=1, source_target_pairs={{0,12},{2,14},{4,0},{6,2},{8,4},{10,6},{12,8},{14,10},{1,13},{3,15... | collective-permute-start | bytes 712712 | tf_op jit(solution)/shard_map/ppermute | solution.py:56
  73.0 0.0 collective-permute-done.5.refs_3_
  73.0 3.1 %collective-permute-start.7 = (bf16[32,3712]{1,0:T(8,128)(2,1)S(1)}, bf16[32,3712]{1,0:T(8,128)(2,1)S(1)}, u32[]{:S(2)}, u32[]{:S(2)}) collective-permute-start(bf16[32,3712]{1,0:T(8,128)(2,1)S(1)} %collective-permute-done.5.refs_3_), channel_id=1, source_target_pairs={{0,2},{2,4},{4,6},{6,8},{8,10},{10,12},{12,14},{14,0},{1,3},{3,5},... | collective-permute-start | bytes 712712 | tf_op jit(solution)/shard_map/ppermute | solution.py:52
  76.1 0.1 pad_add_fusion.at_ref
  76.2 0.0 copy-start
  76.2 2.0 %collective-permute-start.10 = (bf16[224,2048]{1,0:T(8,128)(2,1)}, bf16[224,2048]{1,0:T(8,128)(2,1)}, u32[]{:S(2)}, u32[]{:S(2)}) collective-permute-start(bf16[224,2048]{1,0:T(8,128)(2,1)} %copy-done.2), channel_id=1, source_target_pairs={{0,1},{1,0},{2,3},{3,2},{4,5},{5,4},{6,7},{7,6},{8,9},{9,8},{10,11... | collective-permute-start | bytes 2752520 | tf_op jit(solution)/shard_map/ppermute | solution.py:241
  78.2 0.0 collective-permute-done.8.refs_6_
  78.2 3.5 %collective-permute-done.9.refs_7_ = bf16[32,3712]{1,0:T(8,128)(2,1)S(1)} collective-permute-done((bf16[32,3712]{1,0:T(8,128)(2,1)S(1)}, bf16[32,3712]{1,0:T(8,128)(2,1)S(1)}, u32[]{:S(2)}, u32[]{:S(2)}) %collective-permute-start.9) | collective-permute-done | bytes 237600 | tf_op jit(solution)/shard_map/ppermute | solution.py:56
  81.8 0.4 collective-permute-done.7.refs_5_
  82.2 0.0 collective-permute-done.1.other_ref
  82.2 5.2 %hidden.1 = bf16[8,128,256]{2,1,0:T(8,128)(2,1)} custom-call(s32[3]{0:T(128)S(1)} %pad_add_fusion.at_ref, bf16[3584,256]{1,0:T(8,128)(2,1)} %bitcast.13, bf16[3584,256]{1,0:T(8,128)(2,1)} %collective-permute-done.1.other_ref, bf16[32,3712]{1,0:T(8,128)(2,1)S(1)} %get-tuple-element.16.refs_0_, bf16[32,3712]{1,0:T(8,128)(2,1)S(1)} %collective-permute-done.3.refs_1_, ...), custom_call_target="tpu_custom_call" | custom-call | tf_op jit(solution)/shard_map/hidden/pallas_call | solution.py:233
  87.4 4.3 %all-to-all-start.1 = ((bf16[8,128,256]{2,1,0:T(8,128)(2,1)}), bf16[8,128,256]{2,1,0:T(8,128)(2,1)S(1)}, u32[]{:S(2)}, u32[]{:S(2)}) async-start(bf16[8,128,256]{2,1,0:T(8,128)(2,1)} %hidden.1), calls=%async_computation.1 | async-start | bytes 1048576 | tf_op jit(solution)/shard_map/all_to_all | solution.py:242
  91.8 0.0 collective-permute-done.10.both_ref
  91.8 14.0 %all-to-all-done.1.h_ref = bf16[8,128,256]{2,1,0:T(8,128)(2,1)S(1)} async-done(((bf16[8,128,256]{2,1,0:T(8,128)(2,1)}), bf16[8,128,256]{2,1,0:T(8,128)(2,1)S(1)}, u32[]{:S(2)}, u32[]{:S(2)}) %all-to-all-start.1) | async-done | bytes 524320 | tf_op jit(solution)/shard_map/all_to_all | solution.py:242
  105.8 0.0 copy-done
  105.8 3.2 %down.1 = bf16[8,16,896]{2,1,0:T(8,128)(2,1)S(1)} custom-call(s32[3]{0:T(128)S(1)} %pad_add_fusion.at_ref, bf16[8,128,256]{2,1,0:T(8,128)(2,1)S(1)} %all-to-all-done.1.h_ref, bf16[224,2048]{1,0:T(8,128)(2,1)S(1)} %bitcast.11, bf16[224,2048]{1,0:T(8,128)(2,1)} %collective-permute-done.2.other_ref, bf16[224,2048]{1,0:T(8,128)(2,1)} %copy-done.2, ...), custom_call_target="tpu_custom_call" | custom-call | tf_op jit(solution)/shard_map/down/pallas_call | solution.py:243
  109.0 0.0 copy-start.1
  109.0 12.5 %all_to_all.20.back_ref = bf16[8,16,896]{2,1,0:T(8,128)(2,1)S(1)} all-to-all(bf16[8,16,896]{2,1,0:T(8,128)(2,1)S(1)} %down.1), channel_id=1, replica_groups=mesh['y'=8,'z'=8,'x'=8,'core'=2] {'x'}, dimensions={0} | all-to-all | bytes 458752 | tf_op jit(solution)/shard_map/all_to_all | solution.py:250
  121.5 0.3 spread.1
  121.8 23.6 %all_to_all.21.in_ref = bf16[64,2,1792]{2,1,0:T(2,128)(2,1)S(1)} all-to-all(bf16[64,2,1792]{2,1,0:T(2,128)(2,1)S(1)} %spread.1), channel_id=1, replica_groups=mesh['y'=8,'z'=8,'x'=8,'core'=2] {'y','z'}, dimensions={0} | all-to-all | bytes 917504 | tf_op jit(solution)/shard_map/all_to_all | solution.py:254
  145.5 0.0 copy-done.1
  145.5 0.9 mix.1
Async XLA Ops:
  0.0 30.6 %collective-permute-start = (bf16[224,2048]{1,0:T(8,128)(2,1)}, bf16[224,2048]{1,0:T(8,128)(2,1)S(1)}, u32[]{:S(2)}, u32[]{:S(2)}) collective-permute-start(bf16[224,2048]{1,0:T(8,128)(2,1)} %bitcast.9), channel_id=1, source_target_pairs={{0,2},{2,0},{4,6},{6,4},{8,10},{10,8},{12,14},{14,12},{1,3},{3,1},... | collective-permute-start | bytes 2752520 | tf_op jit(solution)/shard_map/ppermute | solution.py:219
  5.5 41.6 %all-to-all-start = ((bf16[64,2,1920]{2,1,0:T(2,128)(2,1)}), bf16[64,2,1920]{2,1,0:T(2,128)(2,1)S(1)}, u32[]{:S(2)}, u32[]{:S(2)}) async-start(bf16[64,2,1920]{2,1,0:T(2,128)(2,1)} %get-tuple-element.14), calls=%async_computation | async-start | bytes 983040 | tf_op jit(solution)/shard_map/all_to_all | solution.py:223
  28.6 4.7 %collective-permute-start.2 = (bf16[224,2048]{1,0:T(8,128)(2,1)}, bf16[224,2048]{1,0:T(8,128)(2,1)}, u32[]{:S(2)}, u32[]{:S(2)}) collective-permute-start(bf16[224,2048]{1,0:T(8,128)(2,1)} %bitcast.10), channel_id=1, source_target_pairs={{0,1},{1,0},{2,3},{3,2},{4,5},{5,4},{6,7},{7,6},{8,9},{9,8},{10,11... | collective-permute-start | bytes 2752520 | tf_op jit(solution)/shard_map/ppermute | solution.py:222
  30.6 17.1 %copy-start.2 = (bf16[224,2048]{1,0:T(8,128)(2,1)}, bf16[224,2048]{1,0:T(8,128)(2,1)S(1)}, u32[]{:S(2)}) copy-start(bf16[224,2048]{1,0:T(8,128)(2,1)S(1)} %collective-permute-done.pair_ref) | copy-start | bytes 2752516
  30.6 51.6 %collective-permute-start.1 = (bf16[3584,256]{1,0:T(8,128)(2,1)}, bf16[3584,256]{1,0:T(8,128)(2,1)}, u32[]{:S(2)}, u32[]{:S(2)}) collective-permute-start(bf16[3584,256]{1,0:T(8,128)(2,1)} %bitcast.12), channel_id=1, source_target_pairs={{0,1},{1,0},{2,3},{3,2},{4,5},{5,4},{6,7},{7,6},{8,9},{9,8},{10,11... | collective-permute-start | bytes 5505032 | tf_op jit(solution)/shard_map/ppermute | solution.py:221
  47.7 8.3 %collective-permute-start.4 = (bf16[32,3712]{1,0:T(8,128)(2,1)S(1)}, bf16[32,3712]{1,0:T(8,128)(2,1)S(1)}, u32[]{:S(2)}, u32[]{:S(2)}) collective-permute-start(bf16[32,3712]{1,0:T(8,128)(2,1)S(1)} %get-tuple-element.16.refs_0_), channel_id=1, source_target_pairs={{0,14},{2,0},{4,2},{6,4},{8,6},{10,8},{12,10},{14,12},{1,15},{3,1}... | collective-permute-start | bytes 712712 | tf_op jit(solution)/shard_map/ppermute | solution.py:53
  52.4 9.2 %collective-permute-start.3 = (bf16[32,3712]{1,0:T(8,128)(2,1)S(1)}, bf16[32,3712]{1,0:T(8,128)(2,1)S(1)}, u32[]{:S(2)}, u32[]{:S(2)}) collective-permute-start(bf16[32,3712]{1,0:T(8,128)(2,1)S(1)} %get-tuple-element.16.refs_0_), channel_id=1, source_target_pairs={{0,2},{2,4},{4,6},{6,8},{8,10},{10,12},{12,14},{14,0},{1,3},{3,5},... | collective-permute-start | bytes 712712 | tf_op jit(solution)/shard_map/ppermute | solution.py:52
  56.0 9.2 %collective-permute-start.6 = (bf16[32,3712]{1,0:T(8,128)(2,1)S(1)}, bf16[32,3712]{1,0:T(8,128)(2,1)S(1)}, u32[]{:S(2)}, u32[]{:S(2)}) collective-permute-start(bf16[32,3712]{1,0:T(8,128)(2,1)S(1)} %collective-permute-done.4.refs_2_), channel_id=1, source_target_pairs={{0,14},{2,0},{4,2},{6,4},{8,6},{10,8},{12,10},{14,12},{1,15},{3,1}... | collective-permute-start | bytes 712712 | tf_op jit(solution)/shard_map/ppermute | solution.py:53
  61.6 11.4 %collective-permute-start.5 = (bf16[32,3712]{1,0:T(8,128)(2,1)S(1)}, bf16[32,3712]{1,0:T(8,128)(2,1)S(1)}, u32[]{:S(2)}, u32[]{:S(2)}) collective-permute-start(bf16[32,3712]{1,0:T(8,128)(2,1)S(1)} %collective-permute-done.3.refs_1_), channel_id=1, source_target_pairs={{0,2},{2,4},{4,6},{6,8},{8,10},{10,12},{12,14},{14,0},{1,3},{3,5},... | collective-permute-start | bytes 712712 | tf_op jit(solution)/shard_map/ppermute | solution.py:52
  65.2 13.1 %collective-permute-start.8 = (bf16[32,3712]{1,0:T(8,128)(2,1)S(1)}, bf16[32,3712]{1,0:T(8,128)(2,1)S(1)}, u32[]{:S(2)}, u32[]{:S(2)}) collective-permute-start(bf16[32,3712]{1,0:T(8,128)(2,1)S(1)} %collective-permute-done.6.refs_4_), channel_id=1, source_target_pairs={{0,14},{2,0},{4,2},{6,4},{8,6},{10,8},{12,10},{14,12},{1,15},{3,1}... | collective-permute-start | bytes 712712 | tf_op jit(solution)/shard_map/ppermute | solution.py:53
  70.8 11.0 %collective-permute-start.9 = (bf16[32,3712]{1,0:T(8,128)(2,1)S(1)}, bf16[32,3712]{1,0:T(8,128)(2,1)S(1)}, u32[]{:S(2)}, u32[]{:S(2)}) collective-permute-start(bf16[32,3712]{1,0:T(8,128)(2,1)S(1)} %collective-permute-done.6.refs_4_), channel_id=1, source_target_pairs={{0,12},{2,14},{4,0},{6,2},{8,4},{10,6},{12,8},{14,10},{1,13},{3,15... | collective-permute-start | bytes 712712 | tf_op jit(solution)/shard_map/ppermute | solution.py:56
  73.0 9.2 %collective-permute-start.7 = (bf16[32,3712]{1,0:T(8,128)(2,1)S(1)}, bf16[32,3712]{1,0:T(8,128)(2,1)S(1)}, u32[]{:S(2)}, u32[]{:S(2)}) collective-permute-start(bf16[32,3712]{1,0:T(8,128)(2,1)S(1)} %collective-permute-done.5.refs_3_), channel_id=1, source_target_pairs={{0,2},{2,4},{4,6},{6,8},{8,10},{10,12},{12,14},{14,0},{1,3},{3,5},... | collective-permute-start | bytes 712712 | tf_op jit(solution)/shard_map/ppermute | solution.py:52
  76.2 29.6 %copy-start = (bf16[1,2048,224]{1,2,0:T(8,128)(2,1)S(1)}, bf16[1,2048,224]{1,2,0:T(8,128)(2,1)}, u32[]{:S(2)}) copy-start(bf16[1,2048,224]{1,2,0:T(8,128)(2,1)} %param.9) | copy-start | bytes 2752516
  76.2 15.6 %collective-permute-start.10 = (bf16[224,2048]{1,0:T(8,128)(2,1)}, bf16[224,2048]{1,0:T(8,128)(2,1)}, u32[]{:S(2)}, u32[]{:S(2)}) collective-permute-start(bf16[224,2048]{1,0:T(8,128)(2,1)} %copy-done.2), channel_id=1, source_target_pairs={{0,1},{1,0},{2,3},{3,2},{4,5},{5,4},{6,7},{7,6},{8,9},{9,8},{10,11... | collective-permute-start | bytes 2752520 | tf_op jit(solution)/shard_map/ppermute | solution.py:241
  87.4 18.4 %all-to-all-start.1 = ((bf16[8,128,256]{2,1,0:T(8,128)(2,1)}), bf16[8,128,256]{2,1,0:T(8,128)(2,1)S(1)}, u32[]{:S(2)}, u32[]{:S(2)}) async-start(bf16[8,128,256]{2,1,0:T(8,128)(2,1)} %hidden.1), calls=%async_computation.1 | async-start | bytes 1048576 | tf_op jit(solution)/shard_map/all_to_all | solution.py:242
  109.0 36.5 %copy-start.1 = (bf16[64,8]{1,0:T(8,128)(2,1)S(1)}, bf16[64,8]{1,0:T(8,128)(2,1)}, u32[]{:S(2)}) copy-start(bf16[64,8]{1,0:T(8,128)(2,1)} %get-tuple-element.20.place_ref) | copy-start | bytes 3076

commit v10 on v9

--- a/solution.py
+++ b/solution.py
@@ -217,17 +217,17 @@
         60,
     )(*asked)
     dn_pair = lax.ppermute(dn, "x", pair)
-    dn_pair, mine = lax.optimization_barrier((dn_pair, gu))
-    gu_other = lax.ppermute(mine, "core", swap)
-    dn_other = lax.ppermute(dn, "core", swap)
     arrived = lax.all_to_all(send, group, split_axis=0, concat_axis=0, tiled=True)
-    arrived, dn_other = lax.optimization_barrier((arrived, dn_other))
     rows, select = call(
         compact_kernel,
         [((r, width + LANES), bf16), ((groups, r), bf16)],
         [VMEM],
         "compact",
     )(arrived)
+    rows, dn_pair, mine, own = lax.optimization_barrier((rows, dn_pair, gu, dn))
+    gu_other = lax.ppermute(mine, "core", swap)
+    dn_other = lax.ppermute(own, "core", swap)
+    dn_both = lax.ppermute(dn_pair, "core", swap)
     got = ring(rows, n)
     steps = tuple(k for k, _ in got)
     (hid,) = call(
@@ -238,7 +238,6 @@
         [pltpu.VMEM((2,) + gu.shape, bf16), pltpu.SemaphoreType.DMA((2, CHUNKS))],
         HID,
     )(at, gu, gu_other, *[b for _, b in got])
-    dn_both = lax.ppermute(dn_pair, "core", swap)
     hid = lax.all_to_all(hid, "x", split_axis=0, concat_axis=0, tiled=True)
     (out,) = call(
         down_kernel,

time: 147 us -> 165 us (1.12)
  waiting for transfers between devices: 35.4 us -> 48 us
  blocking collectives: 36.1 us -> 40.2 us
    ppermute x3, waiting for transfers between devices: 3.35 us -> 10.7 us  [ring(): back = lax.ppermute(back, 'x', down)]
    ppermute x1, waiting for transfers between devices: 0.01 us -> 4.45 us  [shards(): dn_pair = lax.ppermute(dn, 'x', pair)]
    all_to_all x1, blocking collectives: 23.6 us -> 27.7 us  [shards(): lax.all_to_all(padded, group, split_axis=0, concat_axis=0, tiled=True)]
    all_to_all x1, waiting for transfers between devices: 14 us -> 16.8 us  [shards(): hid = lax.all_to_all(hid, 'x', split_axis=0, concat_axis=0, tiled=True)]
    ppermute x1, waiting for transfers between devices: 3.51 us -> 0.96 us  [ring(): got.append((n // 2, lax.ppermute(near, 'x', twice)))]
  transfers between devices with their start and end apart: 13 -> 13, of which waited for: 7 -> 7; matrix products, arithmetic and copies ran while one was open for 0% -> 0% of each run, Pallas kernels for 5% -> 4%
where the time goes in v10:
time: 165 us; the launch traced here: 164 us
  starting transfers between devices  63.3 us (38%)
  waiting for transfers between devices  48 us (29%)
  blocking collectives  40.2 us (24%)
  Pallas kernels  12.4 us (8%)
    all_to_all x1, blocking collectives, shards(): lax.all_to_all(padded, group, split_axis=0, concat_axis=0, tiled=True)  27.7 us
    all_to_all x1, starting transfers between devices, shards(): lax.all_to_all(send, group, split_axis=0, concat_axis=0, tiled=True)  23.1 us
    all_to_all x1, waiting for transfers between devices, shards(): hid = lax.all_to_all(hid, 'x', split_axis=0, concat_axis=0, tiled=True)  16.8 us
    ppermute x3, starting transfers between devices, ring(): back = lax.ppermute(back, 'x', down)  16 us
    all_to_all x1, waiting for transfers between devices, shards(): lax.all_to_all(send, group, split_axis=0, concat_axis=0, tiled=True)  15.2 us
    all_to_all x1, blocking collectives, shards(): back = lax.all_to_all(out, 'x', split_axis=0, concat_axis=0, tiled=True)  12.5 us
    ppermute x3, waiting for transfers between devices, ring(): back = lax.ppermute(back, 'x', down)  10.7 us
    ppermute x3, starting transfers between devices, ring(): fwd = lax.ppermute(fwd, 'x', up)  7.21 us
  transfers between devices with their start and end apart: 13, of which 7 were waited for; matrix products, arithmetic and copies ran while one was open for 0% of the time, Pallas kernels for 4%

profile of v10, /device:TPU:32, one launch (start us, length us, event | category | flops | bytes accessed | tf_op | source)
XLA Modules:
  0.0 164.3 jit_solution(9306054927928370264)
XLA Ops:
  0.0 2.0 %pack.1 = (bf16[64,2,1920]{2,1,0:T(2,128)(2,1)}, bf16[64,8]{1,0:T(8,128)(2,1)}) custom-call(s32[4,8]{1,0:T(4,128)} %bitcast.14, bf16[4,2,8]{2,1,0:T(2,128)(2,1)} %bitcast.15, bf16[8,3584]{1,0:T(8,128)(2,1)} %refs_2_.1), custom_call_target="tpu_custom_call" | custom-call | tf_op jit(solution)/shard_map/pack/pallas_call | solution.py:211
  2.1 23.1 %all-to-all-start = ((bf16[64,2,1920]{2,1,0:T(2,128)(2,1)}), bf16[64,2,1920]{2,1,0:T(2,128)(2,1)S(1)}, u32[]{:S(2)}, u32[]{:S(2)}) async-start(bf16[64,2,1920]{2,1,0:T(2,128)(2,1)} %get-tuple-element.13), calls=%async_computation | async-start | bytes 983040 | tf_op jit(solution)/shard_map/all_to_all | solution.py:220
  25.1 0.0 copy-start
  25.2 3.5 %collective-permute-start = (bf16[224,2048]{1,0:T(8,128)(2,1)}, bf16[224,2048]{1,0:T(8,128)(2,1)S(1)}, u32[]{:S(2)}, u32[]{:S(2)}) collective-permute-start(bf16[224,2048]{1,0:T(8,128)(2,1)} %bitcast.9), channel_id=1, source_target_pairs={{0,2},{2,0},{4,6},{6,4},{8,10},{10,8},{12,14},{14,12},{1,3},{3,1},... | collective-permute-start | bytes 2752520 | tf_op jit(solution)/shard_map/ppermute | solution.py:219
  28.7 15.2 %all-to-all-done.in_ref = bf16[64,2,1920]{2,1,0:T(2,128)(2,1)S(1)} async-done(((bf16[64,2,1920]{2,1,0:T(2,128)(2,1)}), bf16[64,2,1920]{2,1,0:T(2,128)(2,1)S(1)}, u32[]{:S(2)}, u32[]{:S(2)}) %all-to-all-start) | async-done | bytes 491552 | tf_op jit(solution)/shard_map/all_to_all | solution.py:220
  43.9 0.6 compact.1
  44.5 4.4 %collective-permute-done.pair_ref = bf16[224,2048]{1,0:T(8,128)(2,1)S(1)} collective-permute-done((bf16[224,2048]{1,0:T(8,128)(2,1)}, bf16[224,2048]{1,0:T(8,128)(2,1)S(1)}, u32[]{:S(2)}, u32[]{:S(2)}) %collective-permute-start) | collective-permute-done | bytes 917536 | tf_op jit(solution)/shard_map/ppermute | solution.py:219
  48.9 0.0 copy-start.2
  48.9 1.9 %collective-permute-start.1 = (bf16[3584,256]{1,0:T(8,128)(2,1)}, bf16[3584,256]{1,0:T(8,128)(2,1)}, u32[]{:S(2)}, u32[]{:S(2)}) collective-permute-start(bf16[3584,256]{1,0:T(8,128)(2,1)} %bitcast.12), channel_id=1, source_target_pairs={{0,1},{1,0},{2,3},{3,2},{4,5},{5,4},{6,7},{7,6},{8,9},{9,8},{10,11... | collective-permute-start | bytes 5505032 | tf_op jit(solution)/shard_map/ppermute | solution.py:228
  50.8 4.8 %collective-permute-start.3 = (bf16[32,3712]{1,0:T(8,128)(2,1)S(1)}, bf16[32,3712]{1,0:T(8,128)(2,1)S(1)}, u32[]{:S(2)}, u32[]{:S(2)}) collective-permute-start(bf16[32,3712]{1,0:T(8,128)(2,1)S(1)} %get-tuple-element.16.refs_0_), channel_id=1, source_target_pairs={{0,14},{2,0},{4,2},{6,4},{8,6},{10,8},{12,10},{14,12},{1,15},{3,1}... | collective-permute-start | bytes 712712 | tf_op jit(solution)/shard_map/ppermute | solution.py:53
  55.6 1.9 %collective-permute-start.2 = (bf16[32,3712]{1,0:T(8,128)(2,1)S(1)}, bf16[32,3712]{1,0:T(8,128)(2,1)S(1)}, u32[]{:S(2)}, u32[]{:S(2)}) collective-permute-start(bf16[32,3712]{1,0:T(8,128)(2,1)S(1)} %get-tuple-element.16.refs_0_), channel_id=1, source_target_pairs={{0,2},{2,4},{4,6},{6,8},{8,10},{10,12},{12,14},{14,0},{1,3},{3,5},... | collective-permute-start | bytes 712712 | tf_op jit(solution)/shard_map/ppermute | solution.py:52
  57.6 3.8 %collective-permute-done.3.refs_2_ = bf16[32,3712]{1,0:T(8,128)(2,1)S(1)} collective-permute-done((bf16[32,3712]{1,0:T(8,128)(2,1)S(1)}, bf16[32,3712]{1,0:T(8,128)(2,1)S(1)}, u32[]{:S(2)}, u32[]{:S(2)}) %collective-permute-start.3) | collective-permute-done | bytes 237600 | tf_op jit(solution)/shard_map/ppermute | solution.py:53
  61.3 5.6 %collective-permute-start.5 = (bf16[32,3712]{1,0:T(8,128)(2,1)S(1)}, bf16[32,3712]{1,0:T(8,128)(2,1)S(1)}, u32[]{:S(2)}, u32[]{:S(2)}) collective-permute-start(bf16[32,3712]{1,0:T(8,128)(2,1)S(1)} %collective-permute-done.3.refs_2_), channel_id=1, source_target_pairs={{0,14},{2,0},{4,2},{6,4},{8,6},{10,8},{12,10},{14,12},{1,15},{3,1}... | collective-permute-start | bytes 712712 | tf_op jit(solution)/shard_map/ppermute | solution.py:53
  66.9 0.0 copy-done.2
  66.9 0.0 collective-permute-done.2.refs_1_
  66.9 1.9 %collective-permute-start.4 = (bf16[32,3712]{1,0:T(8,128)(2,1)S(1)}, bf16[32,3712]{1,0:T(8,128)(2,1)S(1)}, u32[]{:S(2)}, u32[]{:S(2)}) collective-permute-start(bf16[32,3712]{1,0:T(8,128)(2,1)S(1)} %collective-permute-done.2.refs_1_), channel_id=1, source_target_pairs={{0,2},{2,4},{4,6},{6,8},{8,10},{10,12},{12,14},{14,0},{1,3},{3,5},... | collective-permute-start | bytes 712712 | tf_op jit(solution)/shard_map/ppermute | solution.py:52
  68.9 2.9 %collective-permute-done.5.refs_4_ = bf16[32,3712]{1,0:T(8,128)(2,1)S(1)} collective-permute-done((bf16[32,3712]{1,0:T(8,128)(2,1)S(1)}, bf16[32,3712]{1,0:T(8,128)(2,1)S(1)}, u32[]{:S(2)}, u32[]{:S(2)}) %collective-permute-start.5) | collective-permute-done | bytes 237600 | tf_op jit(solution)/shard_map/ppermute | solution.py:53
  71.8 5.6 %collective-permute-start.7 = (bf16[32,3712]{1,0:T(8,128)(2,1)S(1)}, bf16[32,3712]{1,0:T(8,128)(2,1)S(1)}, u32[]{:S(2)}, u32[]{:S(2)}) collective-permute-start(bf16[32,3712]{1,0:T(8,128)(2,1)S(1)} %collective-permute-done.5.refs_4_), channel_id=1, source_target_pairs={{0,14},{2,0},{4,2},{6,4},{8,6},{10,8},{12,10},{14,12},{1,15},{3,1}... | collective-permute-start | bytes 712712 | tf_op jit(solution)/shard_map/ppermute | solution.py:53
  77.4 1.9 %collective-permute-start.8 = (bf16[32,3712]{1,0:T(8,128)(2,1)S(1)}, bf16[32,3712]{1,0:T(8,128)(2,1)S(1)}, u32[]{:S(2)}, u32[]{:S(2)}) collective-permute-start(bf16[32,3712]{1,0:T(8,128)(2,1)S(1)} %collective-permute-done.5.refs_4_), channel_id=1, source_target_pairs={{0,12},{2,14},{4,0},{6,2},{8,4},{10,6},{12,8},{14,10},{1,13},{3,15... | collective-permute-start | bytes 712712 | tf_op jit(solution)/shard_map/ppermute | solution.py:56
  79.3 0.0 collective-permute-done.4.refs_3_
  79.3 3.4 %collective-permute-start.6 = (bf16[32,3712]{1,0:T(8,128)(2,1)S(1)}, bf16[32,3712]{1,0:T(8,128)(2,1)S(1)}, u32[]{:S(2)}, u32[]{:S(2)}) collective-permute-start(bf16[32,3712]{1,0:T(8,128)(2,1)S(1)} %collective-permute-done.4.refs_3_), channel_id=1, source_target_pairs={{0,2},{2,4},{4,6},{6,8},{8,10},{10,12},{12,14},{14,0},{1,3},{3,5},... | collective-permute-start | bytes 712712 | tf_op jit(solution)/shard_map/ppermute | solution.py:52
  82.7 0.1 pad_add_fusion.at_ref
  82.8 1.9 %collective-permute-start.10 = (bf16[224,2048]{1,0:T(8,128)(2,1)}, bf16[224,2048]{1,0:T(8,128)(2,1)}, u32[]{:S(2)}, u32[]{:S(2)}) collective-permute-start(bf16[224,2048]{1,0:T(8,128)(2,1)} %copy-done.2), channel_id=1, source_target_pairs={{0,1},{1,0},{2,3},{3,2},{4,5},{5,4},{6,7},{7,6},{8,9},{9,8},{10,11... | collective-permute-start | bytes 2752520 | tf_op jit(solution)/shard_map/ppermute | solution.py:230
  84.7 4.0 %collective-permute-done.7.refs_6_ = bf16[32,3712]{1,0:T(8,128)(2,1)S(1)} collective-permute-done((bf16[32,3712]{1,0:T(8,128)(2,1)S(1)}, bf16[32,3712]{1,0:T(8,128)(2,1)S(1)}, u32[]{:S(2)}, u32[]{:S(2)}) %collective-permute-start.7) | collective-permute-done | bytes 237600 | tf_op jit(solution)/shard_map/ppermute | solution.py:53
  88.7 0.0 copy-done
  88.7 1.9 %collective-permute-start.9 = (bf16[224,2048]{1,0:T(8,128)(2,1)S(1)}, bf16[224,2048]{1,0:T(8,128)(2,1)}, u32[]{:S(2)}, u32[]{:S(2)}) collective-permute-start(bf16[224,2048]{1,0:T(8,128)(2,1)S(1)} %bitcast.10), channel_id=1, source_target_pairs={{0,1},{1,0},{2,3},{3,2},{4,5},{5,4},{6,7},{7,6},{8,9},{9,8},{10,11... | collective-permute-start | bytes 2752520 | tf_op jit(solution)/shard_map/ppermute | solution.py:229
  90.6 1.0 collective-permute-done.8.refs_7_
  91.6 0.0 collective-permute-done.6.refs_5_
  91.6 0.0 collective-permute-done.1.other_ref
  91.6 5.2 %hidden.1 = bf16[8,128,256]{2,1,0:T(8,128)(2,1)} custom-call(s32[3]{0:T(128)S(1)} %pad_add_fusion.at_ref, bf16[3584,256]{1,0:T(8,128)(2,1)} %bitcast.13, bf16[3584,256]{1,0:T(8,128)(2,1)} %collective-permute-done.1.other_ref, bf16[32,3712]{1,0:T(8,128)(2,1)S(1)} %get-tuple-element.16.refs_0_, bf16[32,3712]{1,0:T(8,128)(2,1)S(1)} %collective-permute-done.2.refs_1_, ...), custom_call_target="tpu_custom_call" | custom-call | tf_op jit(solution)/shard_map/hidden/pallas_call | solution.py:233
  96.8 5.9 %all-to-all-start.1 = ((bf16[8,128,256]{2,1,0:T(8,128)(2,1)}), bf16[8,128,256]{2,1,0:T(8,128)(2,1)S(1)}, u32[]{:S(2)}, u32[]{:S(2)}) async-start(bf16[8,128,256]{2,1,0:T(8,128)(2,1)} %hidden.1), calls=%async_computation.1 | async-start | bytes 1048576 | tf_op jit(solution)/shard_map/all_to_all | solution.py:241
  102.7 0.0 collective-permute-done.10.both_ref
  102.7 0.0 collective-permute-done.9.other_ref
  102.7 16.8 %all-to-all-done.1.h_ref = bf16[8,128,256]{2,1,0:T(8,128)(2,1)S(1)} async-done(((bf16[8,128,256]{2,1,0:T(8,128)(2,1)}), bf16[8,128,256]{2,1,0:T(8,128)(2,1)S(1)}, u32[]{:S(2)}, u32[]{:S(2)}) %all-to-all-start.1) | async-done | bytes 524320 | tf_op jit(solution)/shard_map/all_to_all | solution.py:241
  119.5 3.2 %down.1 = bf16[8,16,896]{2,1,0:T(8,128)(2,1)S(1)} custom-call(s32[3]{0:T(128)S(1)} %pad_add_fusion.at_ref, bf16[8,128,256]{2,1,0:T(8,128)(2,1)S(1)} %all-to-all-done.1.h_ref, bf16[224,2048]{1,0:T(8,128)(2,1)S(1)} %bitcast.11, bf16[224,2048]{1,0:T(8,128)(2,1)} %collective-permute-done.9.other_ref, bf16[224,2048]{1,0:T(8,128)(2,1)} %copy-done.2, ...), custom_call_target="tpu_custom_call" | custom-call | tf_op jit(solution)/shard_map/down/pallas_call | solution.py:242
  122.7 0.0 copy-start.1
  122.7 12.5 %all_to_all.20.back_ref = bf16[8,16,896]{2,1,0:T(8,128)(2,1)S(1)} all-to-all(bf16[8,16,896]{2,1,0:T(8,128)(2,1)S(1)} %down.1), channel_id=1, replica_groups=mesh['y'=8,'z'=8,'x'=8,'core'=2] {'x'}, dimensions={0} | all-to-all | bytes 458752 | tf_op jit(solution)/shard_map/all_to_all | solution.py:249
  135.3 0.3 spread.1
  135.6 27.7 %all_to_all.21.in_ref = bf16[64,2,1792]{2,1,0:T(2,128)(2,1)S(1)} all-to-all(bf16[64,2,1792]{2,1,0:T(2,128)(2,1)S(1)} %spread.1), channel_id=1, replica_groups=mesh['y'=8,'z'=8,'x'=8,'core'=2] {'y','z'}, dimensions={0} | all-to-all | bytes 917504 | tf_op jit(solution)/shard_map/all_to_all | solution.py:253
  163.3 0.0 copy-done.1
  163.3 0.9 mix.1
Async XLA Ops:
  2.1 41.8 %all-to-all-start = ((bf16[64,2,1920]{2,1,0:T(2,128)(2,1)}), bf16[64,2,1920]{2,1,0:T(2,128)(2,1)S(1)}, u32[]{:S(2)}, u32[]{:S(2)}) async-start(bf16[64,2,1920]{2,1,0:T(2,128)(2,1)} %get-tuple-element.13), calls=%async_computation | async-start | bytes 983040 | tf_op jit(solution)/shard_map/all_to_all | solution.py:220
  25.1 63.6 %copy-start = (bf16[1,2048,224]{1,2,0:T(8,128)(2,1)S(1)}, bf16[1,2048,224]{1,2,0:T(8,128)(2,1)}, u32[]{:S(2)}) copy-start(bf16[1,2048,224]{1,2,0:T(8,128)(2,1)} %param.9) | copy-start | bytes 2752516
  25.2 23.8 %collective-permute-start = (bf16[224,2048]{1,0:T(8,128)(2,1)}, bf16[224,2048]{1,0:T(8,128)(2,1)S(1)}, u32[]{:S(2)}, u32[]{:S(2)}) collective-permute-start(bf16[224,2048]{1,0:T(8,128)(2,1)} %bitcast.9), channel_id=1, source_target_pairs={{0,2},{2,0},{4,6},{6,4},{8,10},{10,8},{12,14},{14,12},{1,3},{3,1},... | collective-permute-start | bytes 2752520 | tf_op jit(solution)/shard_map/ppermute | solution.py:219
  48.9 18.0 %copy-start.2 = (bf16[224,2048]{1,0:T(8,128)(2,1)}, bf16[224,2048]{1,0:T(8,128)(2,1)S(1)}, u32[]{:S(2)}) copy-start(bf16[224,2048]{1,0:T(8,128)(2,1)S(1)} %collective-permute-done.pair_ref) | copy-start | bytes 2752516
  48.9 42.7 %collective-permute-start.1 = (bf16[3584,256]{1,0:T(8,128)(2,1)}, bf16[3584,256]{1,0:T(8,128)(2,1)}, u32[]{:S(2)}, u32[]{:S(2)}) collective-permute-start(bf16[3584,256]{1,0:T(8,128)(2,1)} %bitcast.12), channel_id=1, source_target_pairs={{0,1},{1,0},{2,3},{3,2},{4,5},{5,4},{6,7},{7,6},{8,9},{9,8},{10,11... | collective-permute-start | bytes 5505032 | tf_op jit(solution)/shard_map/ppermute | solution.py:228
  50.8 10.5 %collective-permute-start.3 = (bf16[32,3712]{1,0:T(8,128)(2,1)S(1)}, bf16[32,3712]{1,0:T(8,128)(2,1)S(1)}, u32[]{:S(2)}, u32[]{:S(2)}) collective-permute-start(bf16[32,3712]{1,0:T(8,128)(2,1)S(1)} %get-tuple-element.16.refs_0_), channel_id=1, source_target_pairs={{0,14},{2,0},{4,2},{6,4},{8,6},{10,8},{12,10},{14,12},{1,15},{3,1}... | collective-permute-start | bytes 712712 | tf_op jit(solution)/shard_map/ppermute | solution.py:53
  55.6 11.3 %collective-permute-start.2 = (bf16[32,3712]{1,0:T(8,128)(2,1)S(1)}, bf16[32,3712]{1,0:T(8,128)(2,1)S(1)}, u32[]{:S(2)}, u32[]{:S(2)}) collective-permute-start(bf16[32,3712]{1,0:T(8,128)(2,1)S(1)} %get-tuple-element.16.refs_0_), channel_id=1, source_target_pairs={{0,2},{2,4},{4,6},{6,8},{8,10},{10,12},{12,14},{14,0},{1,3},{3,5},... | collective-permute-start | bytes 712712 | tf_op jit(solution)/shard_map/ppermute | solution.py:52
  61.3 10.5 %collective-permute-start.5 = (bf16[32,3712]{1,0:T(8,128)(2,1)S(1)}, bf16[32,3712]{1,0:T(8,128)(2,1)S(1)}, u32[]{:S(2)}, u32[]{:S(2)}) collective-permute-start(bf16[32,3712]{1,0:T(8,128)(2,1)S(1)} %collective-permute-done.3.refs_2_), channel_id=1, source_target_pairs={{0,14},{2,0},{4,2},{6,4},{8,6},{10,8},{12,10},{14,12},{1,15},{3,1}... | collective-permute-start | bytes 712712 | tf_op jit(solution)/shard_map/ppermute | solution.py:53
  66.9 12.4 %collective-permute-start.4 = (bf16[32,3712]{1,0:T(8,128)(2,1)S(1)}, bf16[32,3712]{1,0:T(8,128)(2,1)S(1)}, u32[]{:S(2)}, u32[]{:S(2)}) collective-permute-start(bf16[32,3712]{1,0:T(8,128)(2,1)S(1)} %collective-permute-done.2.refs_1_), channel_id=1, source_target_pairs={{0,2},{2,4},{4,6},{6,8},{8,10},{10,12},{12,14},{14,0},{1,3},{3,5},... | collective-permute-start | bytes 712712 | tf_op jit(solution)/shard_map/ppermute | solution.py:52
  71.8 16.9 %collective-permute-start.7 = (bf16[32,3712]{1,0:T(8,128)(2,1)S(1)}, bf16[32,3712]{1,0:T(8,128)(2,1)S(1)}, u32[]{:S(2)}, u32[]{:S(2)}) collective-permute-start(bf16[32,3712]{1,0:T(8,128)(2,1)S(1)} %collective-permute-done.5.refs_4_), channel_id=1, source_target_pairs={{0,14},{2,0},{4,2},{6,4},{8,6},{10,8},{12,10},{14,12},{1,15},{3,1}... | collective-permute-start | bytes 712712 | tf_op jit(solution)/shard_map/ppermute | solution.py:53
  77.4 14.2 %collective-permute-start.8 = (bf16[32,3712]{1,0:T(8,128)(2,1)S(1)}, bf16[32,3712]{1,0:T(8,128)(2,1)S(1)}, u32[]{:S(2)}, u32[]{:S(2)}) collective-permute-start(bf16[32,3712]{1,0:T(8,128)(2,1)S(1)} %collective-permute-done.5.refs_4_), channel_id=1, source_target_pairs={{0,12},{2,14},{4,0},{6,2},{8,4},{10,6},{12,8},{14,10},{1,13},{3,15... | collective-permute-start | bytes 712712 | tf_op jit(solution)/shard_map/ppermute | solution.py:56
  79.3 12.3 %collective-permute-start.6 = (bf16[32,3712]{1,0:T(8,128)(2,1)S(1)}, bf16[32,3712]{1,0:T(8,128)(2,1)S(1)}, u32[]{:S(2)}, u32[]{:S(2)}) collective-permute-start(bf16[32,3712]{1,0:T(8,128)(2,1)S(1)} %collective-permute-done.4.refs_3_), channel_id=1, source_target_pairs={{0,2},{2,4},{4,6},{6,8},{8,10},{10,12},{12,14},{14,0},{1,3},{3,5},... | collective-permute-start | bytes 712712 | tf_op jit(solution)/shard_map/ppermute | solution.py:52
  82.8 19.9 %collective-permute-start.10 = (bf16[224,2048]{1,0:T(8,128)(2,1)}, bf16[224,2048]{1,0:T(8,128)(2,1)}, u32[]{:S(2)}, u32[]{:S(2)}) collective-permute-start(bf16[224,2048]{1,0:T(8,128)(2,1)} %copy-done.2), channel_id=1, source_target_pairs={{0,1},{1,0},{2,3},{3,2},{4,5},{5,4},{6,7},{7,6},{8,9},{9,8},{10,11... | collective-permute-start | bytes 2752520 | tf_op jit(solution)/shard_map/ppermute | solution.py:230
  88.7 14.0 %collective-permute-start.9 = (bf16[224,2048]{1,0:T(8,128)(2,1)S(1)}, bf16[224,2048]{1,0:T(8,128)(2,1)}, u32[]{:S(2)}, u32[]{:S(2)}) collective-permute-start(bf16[224,2048]{1,0:T(8,128)(2,1)S(1)} %bitcast.10), channel_id=1, source_target_pairs={{0,1},{1,0},{2,3},{3,2},{4,5},{5,4},{6,7},{7,6},{8,9},{9,8},{10,11... | collective-permute-start | bytes 2752520 | tf_op jit(solution)/shard_map/ppermute | solution.py:229
  96.8 22.7 %all-to-all-start.1 = ((bf16[8,128,256]{2,1,0:T(8,128)(2,1)}), bf16[8,128,256]{2,1,0:T(8,128)(2,1)S(1)}, u32[]{:S(2)}, u32[]{:S(2)}) async-start(bf16[8,128,256]{2,1,0:T(8,128)(2,1)} %hidden.1), calls=%async_computation.1 | async-start | bytes 1048576 | tf_op jit(solution)/shard_map/all_to_all | solution.py:241
  122.7 40.6 %copy-start.1 = (bf16[64,8]{1,0:T(8,128)(2,1)S(1)}, bf16[64,8]{1,0:T(8,128)(2,1)}, u32[]{:S(2)}) copy-start(bf16[64,8]{1,0:T(8,128)(2,1)} %get-tuple-element.20.place_ref) | copy-start | bytes 3076

commit v11 on v9

--- a/solution.py
+++ b/solution.py
@@ -15,7 +15,7 @@
 HBM = pl.BlockSpec(memory_space=pltpu.HBM)
 HID = 50
 DOWN = 52
-CHUNKS = 4
+CHUNKS = 2
 
 
 COSTS = {"compact": pl.CostEstimate(flops=10**10, bytes_accessed=2**24, transcendentals=0)}

time: 147 us -> 147 us (level)
  no operation moved by 1% of the time
where the time goes in v11:
time: 147 us; the launch traced here: 146 us
  starting transfers between devices  62.2 us (42%)
  blocking collectives  36.1 us (25%)
  waiting for transfers between devices  35.4 us (24%)
  Pallas kernels  12.2 us (8%)
    all_to_all x1, blocking collectives, shards(): lax.all_to_all(padded, group, split_axis=0, concat_axis=0, tiled=True)  23.6 us
    all_to_all x1, starting transfers between devices, shards(): lax.all_to_all(send, group, split_axis=0, concat_axis=0, tiled=True)  23.2 us
    ppermute x3, starting transfers between devices, ring(): back = lax.ppermute(back, 'x', down)  15.8 us
    all_to_all x1, waiting for transfers between devices, shards(): hid = lax.all_to_all(hid, 'x', split_axis=0, concat_axis=0, tiled=True)  14 us
    all_to_all x1, waiting for transfers between devices, shards(): lax.all_to_all(send, group, split_axis=0, concat_axis=0, tiled=True)  13.7 us
    all_to_all x1, blocking collectives, shards(): back = lax.all_to_all(out, 'x', split_axis=0, concat_axis=0, tiled=True)  12.5 us
    ppermute x3, starting transfers between devices, ring(): fwd = lax.ppermute(fwd, 'x', up)  6.93 us
    pallas_call x1, Pallas kernels, shards(): call(functools.partial(hidden_kernel, steps), [((n, n * r // 2, units), b...  5.11 us
  transfers between devices with their start and end apart: 13, of which 7 were waited for; matrix products, arithmetic and copies ran while one was open for 0% of the time, Pallas kernels for 5%

profile of v11, /device:TPU:32, one launch (start us, length us, event | category | flops | bytes accessed | tf_op | source)
XLA Modules:
  0.0 146.3 jit_solution(15917032116391550467)
XLA Ops:
  0.0 3.4 %collective-permute-start = (bf16[224,2048]{1,0:T(8,128)(2,1)}, bf16[224,2048]{1,0:T(8,128)(2,1)S(1)}, u32[]{:S(2)}, u32[]{:S(2)}) collective-permute-start(bf16[224,2048]{1,0:T(8,128)(2,1)} %bitcast.9), channel_id=1, source_target_pairs={{0,2},{2,0},{4,6},{6,4},{8,10},{10,8},{12,14},{14,12},{1,3},{3,1},... | collective-permute-start | bytes 2752520 | tf_op jit(solution)/shard_map/ppermute | solution.py:219
  3.4 2.1 %pack.1 = (bf16[64,2,1920]{2,1,0:T(2,128)(2,1)}, bf16[64,8]{1,0:T(8,128)(2,1)}) custom-call(s32[4,8]{1,0:T(4,128)} %bitcast.14, bf16[4,2,8]{2,1,0:T(2,128)(2,1)} %bitcast.15, bf16[8,3584]{1,0:T(8,128)(2,1)} %refs_2_.1), custom_call_target="tpu_custom_call" | custom-call | tf_op jit(solution)/shard_map/pack/pallas_call | solution.py:211
  5.5 23.2 %all-to-all-start = ((bf16[64,2,1920]{2,1,0:T(2,128)(2,1)}), bf16[64,2,1920]{2,1,0:T(2,128)(2,1)S(1)}, u32[]{:S(2)}, u32[]{:S(2)}) async-start(bf16[64,2,1920]{2,1,0:T(2,128)(2,1)} %get-tuple-element.14), calls=%async_computation | async-start | bytes 983040 | tf_op jit(solution)/shard_map/all_to_all | solution.py:223
  28.6 1.9 %collective-permute-start.2 = (bf16[224,2048]{1,0:T(8,128)(2,1)}, bf16[224,2048]{1,0:T(8,128)(2,1)}, u32[]{:S(2)}, u32[]{:S(2)}) collective-permute-start(bf16[224,2048]{1,0:T(8,128)(2,1)} %bitcast.10), channel_id=1, source_target_pairs={{0,1},{1,0},{2,3},{3,2},{4,5},{5,4},{6,7},{7,6},{8,9},{9,8},{10,11... | collective-permute-start | bytes 2752520 | tf_op jit(solution)/shard_map/ppermute | solution.py:222
  30.6 0.0 collective-permute-done.pair_ref
  30.6 0.0 copy-start.2
  30.6 2.4 %collective-permute-start.1 = (bf16[3584,256]{1,0:T(8,128)(2,1)}, bf16[3584,256]{1,0:T(8,128)(2,1)}, u32[]{:S(2)}, u32[]{:S(2)}) collective-permute-start(bf16[3584,256]{1,0:T(8,128)(2,1)} %bitcast.12), channel_id=1, source_target_pairs={{0,1},{1,0},{2,3},{3,2},{4,5},{5,4},{6,7},{7,6},{8,9},{9,8},{10,11... | collective-permute-start | bytes 5505032 | tf_op jit(solution)/shard_map/ppermute | solution.py:221
  33.0 0.3 collective-permute-done.2.other_ref
  33.3 13.7 %all-to-all-done.in_ref = bf16[64,2,1920]{2,1,0:T(2,128)(2,1)S(1)} async-done(((bf16[64,2,1920]{2,1,0:T(2,128)(2,1)}), bf16[64,2,1920]{2,1,0:T(2,128)(2,1)S(1)}, u32[]{:S(2)}, u32[]{:S(2)}) %all-to-all-start) | async-done | bytes 491552 | tf_op jit(solution)/shard_map/all_to_all | solution.py:223
  47.1 0.6 compact.1
  47.7 0.0 copy-done.2
  47.7 4.7 %collective-permute-start.4 = (bf16[32,3712]{1,0:T(8,128)(2,1)S(1)}, bf16[32,3712]{1,0:T(8,128)(2,1)S(1)}, u32[]{:S(2)}, u32[]{:S(2)}) collective-permute-start(bf16[32,3712]{1,0:T(8,128)(2,1)S(1)} %get-tuple-element.16.refs_0_), channel_id=1, source_target_pairs={{0,14},{2,0},{4,2},{6,4},{8,6},{10,8},{12,10},{14,12},{1,15},{3,1}... | collective-permute-start | bytes 712712 | tf_op jit(solution)/shard_map/ppermute | solution.py:53
  52.4 1.9 %collective-permute-start.3 = (bf16[32,3712]{1,0:T(8,128)(2,1)S(1)}, bf16[32,3712]{1,0:T(8,128)(2,1)S(1)}, u32[]{:S(2)}, u32[]{:S(2)}) collective-permute-start(bf16[32,3712]{1,0:T(8,128)(2,1)S(1)} %get-tuple-element.16.refs_0_), channel_id=1, source_target_pairs={{0,2},{2,4},{4,6},{6,8},{8,10},{10,12},{12,14},{14,0},{1,3},{3,5},... | collective-permute-start | bytes 712712 | tf_op jit(solution)/shard_map/ppermute | solution.py:52
  54.3 1.7 %collective-permute-done.4.refs_2_ = bf16[32,3712]{1,0:T(8,128)(2,1)S(1)} collective-permute-done((bf16[32,3712]{1,0:T(8,128)(2,1)S(1)}, bf16[32,3712]{1,0:T(8,128)(2,1)S(1)}, u32[]{:S(2)}, u32[]{:S(2)}) %collective-permute-start.4) | collective-permute-done | bytes 237600 | tf_op jit(solution)/shard_map/ppermute | solution.py:53
  56.0 5.6 %collective-permute-start.6 = (bf16[32,3712]{1,0:T(8,128)(2,1)S(1)}, bf16[32,3712]{1,0:T(8,128)(2,1)S(1)}, u32[]{:S(2)}, u32[]{:S(2)}) collective-permute-start(bf16[32,3712]{1,0:T(8,128)(2,1)S(1)} %collective-permute-done.4.refs_2_), channel_id=1, source_target_pairs={{0,14},{2,0},{4,2},{6,4},{8,6},{10,8},{12,10},{14,12},{1,15},{3,1}... | collective-permute-start | bytes 712712 | tf_op jit(solution)/shard_map/ppermute | solution.py:53
  61.6 0.0 collective-permute-done.3.refs_1_
  61.6 1.9 %collective-permute-start.5 = (bf16[32,3712]{1,0:T(8,128)(2,1)S(1)}, bf16[32,3712]{1,0:T(8,128)(2,1)S(1)}, u32[]{:S(2)}, u32[]{:S(2)}) collective-permute-start(bf16[32,3712]{1,0:T(8,128)(2,1)S(1)} %collective-permute-done.3.refs_1_), channel_id=1, source_target_pairs={{0,2},{2,4},{4,6},{6,8},{8,10},{10,12},{12,14},{14,0},{1,3},{3,5},... | collective-permute-start | bytes 712712 | tf_op jit(solution)/shard_map/ppermute | solution.py:52
  63.5 1.7 %collective-permute-done.6.refs_4_ = bf16[32,3712]{1,0:T(8,128)(2,1)S(1)} collective-permute-done((bf16[32,3712]{1,0:T(8,128)(2,1)S(1)}, bf16[32,3712]{1,0:T(8,128)(2,1)S(1)}, u32[]{:S(2)}, u32[]{:S(2)}) %collective-permute-start.6) | collective-permute-done | bytes 237600 | tf_op jit(solution)/shard_map/ppermute | solution.py:53
  65.2 5.6 %collective-permute-start.8 = (bf16[32,3712]{1,0:T(8,128)(2,1)S(1)}, bf16[32,3712]{1,0:T(8,128)(2,1)S(1)}, u32[]{:S(2)}, u32[]{:S(2)}) collective-permute-start(bf16[32,3712]{1,0:T(8,128)(2,1)S(1)} %collective-permute-done.6.refs_4_), channel_id=1, source_target_pairs={{0,14},{2,0},{4,2},{6,4},{8,6},{10,8},{12,10},{14,12},{1,15},{3,1}... | collective-permute-start | bytes 712712 | tf_op jit(solution)/shard_map/ppermute | solution.py:53
  70.8 2.2 %collective-permute-start.9 = (bf16[32,3712]{1,0:T(8,128)(2,1)S(1)}, bf16[32,3712]{1,0:T(8,128)(2,1)S(1)}, u32[]{:S(2)}, u32[]{:S(2)}) collective-permute-start(bf16[32,3712]{1,0:T(8,128)(2,1)S(1)} %collective-permute-done.6.refs_4_), channel_id=1, source_target_pairs={{0,12},{2,14},{4,0},{6,2},{8,4},{10,6},{12,8},{14,10},{1,13},{3,15... | collective-permute-start | bytes 712712 | tf_op jit(solution)/shard_map/ppermute | solution.py:56
  73.0 0.0 collective-permute-done.5.refs_3_
  73.0 3.1 %collective-permute-start.7 = (bf16[32,3712]{1,0:T(8,128)(2,1)S(1)}, bf16[32,3712]{1,0:T(8,128)(2,1)S(1)}, u32[]{:S(2)}, u32[]{:S(2)}) collective-permute-start(bf16[32,3712]{1,0:T(8,128)(2,1)S(1)} %collective-permute-done.5.refs_3_), channel_id=1, source_target_pairs={{0,2},{2,4},{4,6},{6,8},{8,10},{10,12},{12,14},{14,0},{1,3},{3,5},... | collective-permute-start | bytes 712712 | tf_op jit(solution)/shard_map/ppermute | solution.py:52
  76.1 0.1 pad_add_fusion.at_ref
  76.2 0.0 copy-start
  76.2 2.0 %collective-permute-start.10 = (bf16[224,2048]{1,0:T(8,128)(2,1)}, bf16[224,2048]{1,0:T(8,128)(2,1)}, u32[]{:S(2)}, u32[]{:S(2)}) collective-permute-start(bf16[224,2048]{1,0:T(8,128)(2,1)} %copy-done.2), channel_id=1, source_target_pairs={{0,1},{1,0},{2,3},{3,2},{4,5},{5,4},{6,7},{7,6},{8,9},{9,8},{10,11... | collective-permute-start | bytes 2752520 | tf_op jit(solution)/shard_map/ppermute | solution.py:241
  78.2 0.0 collective-permute-done.8.refs_6_
  78.2 3.5 %collective-permute-done.9.refs_7_ = bf16[32,3712]{1,0:T(8,128)(2,1)S(1)} collective-permute-done((bf16[32,3712]{1,0:T(8,128)(2,1)S(1)}, bf16[32,3712]{1,0:T(8,128)(2,1)S(1)}, u32[]{:S(2)}, u32[]{:S(2)}) %collective-permute-start.9) | collective-permute-done | bytes 237600 | tf_op jit(solution)/shard_map/ppermute | solution.py:56
  81.8 0.4 collective-permute-done.7.refs_5_
  82.2 0.0 collective-permute-done.1.other_ref
  82.2 5.1 %hidden.1 = bf16[8,128,256]{2,1,0:T(8,128)(2,1)} custom-call(s32[3]{0:T(128)S(1)} %pad_add_fusion.at_ref, bf16[3584,256]{1,0:T(8,128)(2,1)} %bitcast.13, bf16[3584,256]{1,0:T(8,128)(2,1)} %collective-permute-done.1.other_ref, bf16[32,3712]{1,0:T(8,128)(2,1)S(1)} %get-tuple-element.16.refs_0_, bf16[32,3712]{1,0:T(8,128)(2,1)S(1)} %collective-permute-done.3.refs_1_, ...), custom_call_target="tpu_custom_call" | custom-call | tf_op jit(solution)/shard_map/hidden/pallas_call | solution.py:233
  87.3 4.3 %all-to-all-start.1 = ((bf16[8,128,256]{2,1,0:T(8,128)(2,1)}), bf16[8,128,256]{2,1,0:T(8,128)(2,1)S(1)}, u32[]{:S(2)}, u32[]{:S(2)}) async-start(bf16[8,128,256]{2,1,0:T(8,128)(2,1)} %hidden.1), calls=%async_computation.1 | async-start | bytes 1048576 | tf_op jit(solution)/shard_map/all_to_all | solution.py:242
  91.6 0.0 collective-permute-done.10.both_ref
  91.6 14.0 %all-to-all-done.1.h_ref = bf16[8,128,256]{2,1,0:T(8,128)(2,1)S(1)} async-done(((bf16[8,128,256]{2,1,0:T(8,128)(2,1)}), bf16[8,128,256]{2,1,0:T(8,128)(2,1)S(1)}, u32[]{:S(2)}, u32[]{:S(2)}) %all-to-all-start.1) | async-done | bytes 524320 | tf_op jit(solution)/shard_map/all_to_all | solution.py:242
  105.7 0.0 copy-done
  105.7 3.2 %down.1 = bf16[8,16,896]{2,1,0:T(8,128)(2,1)S(1)} custom-call(s32[3]{0:T(128)S(1)} %pad_add_fusion.at_ref, bf16[8,128,256]{2,1,0:T(8,128)(2,1)S(1)} %all-to-all-done.1.h_ref, bf16[224,2048]{1,0:T(8,128)(2,1)S(1)} %bitcast.11, bf16[224,2048]{1,0:T(8,128)(2,1)} %collective-permute-done.2.other_ref, bf16[224,2048]{1,0:T(8,128)(2,1)} %copy-done.2, ...), custom_call_target="tpu_custom_call" | custom-call | tf_op jit(solution)/shard_map/down/pallas_call | solution.py:243
  108.9 0.0 copy-start.1
  108.9 12.5 %all_to_all.20.back_ref = bf16[8,16,896]{2,1,0:T(8,128)(2,1)S(1)} all-to-all(bf16[8,16,896]{2,1,0:T(8,128)(2,1)S(1)} %down.1), channel_id=1, replica_groups=mesh['y'=8,'z'=8,'x'=8,'core'=2] {'x'}, dimensions={0} | all-to-all | bytes 458752 | tf_op jit(solution)/shard_map/all_to_all | solution.py:250
  121.4 0.3 spread.1
  121.7 23.6 %all_to_all.21.in_ref = bf16[64,2,1792]{2,1,0:T(2,128)(2,1)S(1)} all-to-all(bf16[64,2,1792]{2,1,0:T(2,128)(2,1)S(1)} %spread.1), channel_id=1, replica_groups=mesh['y'=8,'z'=8,'x'=8,'core'=2] {'y','z'}, dimensions={0} | all-to-all | bytes 917504 | tf_op jit(solution)/shard_map/all_to_all | solution.py:254
  145.3 0.0 copy-done.1
  145.3 0.9 mix.1
Async XLA Ops:
  0.0 30.6 %collective-permute-start = (bf16[224,2048]{1,0:T(8,128)(2,1)}, bf16[224,2048]{1,0:T(8,128)(2,1)S(1)}, u32[]{:S(2)}, u32[]{:S(2)}) collective-permute-start(bf16[224,2048]{1,0:T(8,128)(2,1)} %bitcast.9), channel_id=1, source_target_pairs={{0,2},{2,0},{4,6},{6,4},{8,10},{10,8},{12,14},{14,12},{1,3},{3,1},... | collective-permute-start | bytes 2752520 | tf_op jit(solution)/shard_map/ppermute | solution.py:219
  5.5 41.6 %all-to-all-start = ((bf16[64,2,1920]{2,1,0:T(2,128)(2,1)}), bf16[64,2,1920]{2,1,0:T(2,128)(2,1)S(1)}, u32[]{:S(2)}, u32[]{:S(2)}) async-start(bf16[64,2,1920]{2,1,0:T(2,128)(2,1)} %get-tuple-element.14), calls=%async_computation | async-start | bytes 983040 | tf_op jit(solution)/shard_map/all_to_all | solution.py:223
  28.6 4.7 %collective-permute-start.2 = (bf16[224,2048]{1,0:T(8,128)(2,1)}, bf16[224,2048]{1,0:T(8,128)(2,1)}, u32[]{:S(2)}, u32[]{:S(2)}) collective-permute-start(bf16[224,2048]{1,0:T(8,128)(2,1)} %bitcast.10), channel_id=1, source_target_pairs={{0,1},{1,0},{2,3},{3,2},{4,5},{5,4},{6,7},{7,6},{8,9},{9,8},{10,11... | collective-permute-start | bytes 2752520 | tf_op jit(solution)/shard_map/ppermute | solution.py:222
  30.6 17.1 %copy-start.2 = (bf16[224,2048]{1,0:T(8,128)(2,1)}, bf16[224,2048]{1,0:T(8,128)(2,1)S(1)}, u32[]{:S(2)}) copy-start(bf16[224,2048]{1,0:T(8,128)(2,1)S(1)} %collective-permute-done.pair_ref) | copy-start | bytes 2752516
  30.6 51.6 %collective-permute-start.1 = (bf16[3584,256]{1,0:T(8,128)(2,1)}, bf16[3584,256]{1,0:T(8,128)(2,1)}, u32[]{:S(2)}, u32[]{:S(2)}) collective-permute-start(bf16[3584,256]{1,0:T(8,128)(2,1)} %bitcast.12), channel_id=1, source_target_pairs={{0,1},{1,0},{2,3},{3,2},{4,5},{5,4},{6,7},{7,6},{8,9},{9,8},{10,11... | collective-permute-start | bytes 5505032 | tf_op jit(solution)/shard_map/ppermute | solution.py:221
  47.7 8.3 %collective-permute-start.4 = (bf16[32,3712]{1,0:T(8,128)(2,1)S(1)}, bf16[32,3712]{1,0:T(8,128)(2,1)S(1)}, u32[]{:S(2)}, u32[]{:S(2)}) collective-permute-start(bf16[32,3712]{1,0:T(8,128)(2,1)S(1)} %get-tuple-element.16.refs_0_), channel_id=1, source_target_pairs={{0,14},{2,0},{4,2},{6,4},{8,6},{10,8},{12,10},{14,12},{1,15},{3,1}... | collective-permute-start | bytes 712712 | tf_op jit(solution)/shard_map/ppermute | solution.py:53
  52.4 9.2 %collective-permute-start.3 = (bf16[32,3712]{1,0:T(8,128)(2,1)S(1)}, bf16[32,3712]{1,0:T(8,128)(2,1)S(1)}, u32[]{:S(2)}, u32[]{:S(2)}) collective-permute-start(bf16[32,3712]{1,0:T(8,128)(2,1)S(1)} %get-tuple-element.16.refs_0_), channel_id=1, source_target_pairs={{0,2},{2,4},{4,6},{6,8},{8,10},{10,12},{12,14},{14,0},{1,3},{3,5},... | collective-permute-start | bytes 712712 | tf_op jit(solution)/shard_map/ppermute | solution.py:52
  56.0 9.2 %collective-permute-start.6 = (bf16[32,3712]{1,0:T(8,128)(2,1)S(1)}, bf16[32,3712]{1,0:T(8,128)(2,1)S(1)}, u32[]{:S(2)}, u32[]{:S(2)}) collective-permute-start(bf16[32,3712]{1,0:T(8,128)(2,1)S(1)} %collective-permute-done.4.refs_2_), channel_id=1, source_target_pairs={{0,14},{2,0},{4,2},{6,4},{8,6},{10,8},{12,10},{14,12},{1,15},{3,1}... | collective-permute-start | bytes 712712 | tf_op jit(solution)/shard_map/ppermute | solution.py:53
  61.6 11.4 %collective-permute-start.5 = (bf16[32,3712]{1,0:T(8,128)(2,1)S(1)}, bf16[32,3712]{1,0:T(8,128)(2,1)S(1)}, u32[]{:S(2)}, u32[]{:S(2)}) collective-permute-start(bf16[32,3712]{1,0:T(8,128)(2,1)S(1)} %collective-permute-done.3.refs_1_), channel_id=1, source_target_pairs={{0,2},{2,4},{4,6},{6,8},{8,10},{10,12},{12,14},{14,0},{1,3},{3,5},... | collective-permute-start | bytes 712712 | tf_op jit(solution)/shard_map/ppermute | solution.py:52
  65.2 13.1 %collective-permute-start.8 = (bf16[32,3712]{1,0:T(8,128)(2,1)S(1)}, bf16[32,3712]{1,0:T(8,128)(2,1)S(1)}, u32[]{:S(2)}, u32[]{:S(2)}) collective-permute-start(bf16[32,3712]{1,0:T(8,128)(2,1)S(1)} %collective-permute-done.6.refs_4_), channel_id=1, source_target_pairs={{0,14},{2,0},{4,2},{6,4},{8,6},{10,8},{12,10},{14,12},{1,15},{3,1}... | collective-permute-start | bytes 712712 | tf_op jit(solution)/shard_map/ppermute | solution.py:53
  70.8 11.0 %collective-permute-start.9 = (bf16[32,3712]{1,0:T(8,128)(2,1)S(1)}, bf16[32,3712]{1,0:T(8,128)(2,1)S(1)}, u32[]{:S(2)}, u32[]{:S(2)}) collective-permute-start(bf16[32,3712]{1,0:T(8,128)(2,1)S(1)} %collective-permute-done.6.refs_4_), channel_id=1, source_target_pairs={{0,12},{2,14},{4,0},{6,2},{8,4},{10,6},{12,8},{14,10},{1,13},{3,15... | collective-permute-start | bytes 712712 | tf_op jit(solution)/shard_map/ppermute | solution.py:56
  73.0 9.2 %collective-permute-start.7 = (bf16[32,3712]{1,0:T(8,128)(2,1)S(1)}, bf16[32,3712]{1,0:T(8,128)(2,1)S(1)}, u32[]{:S(2)}, u32[]{:S(2)}) collective-permute-start(bf16[32,3712]{1,0:T(8,128)(2,1)S(1)} %collective-permute-done.5.refs_3_), channel_id=1, source_target_pairs={{0,2},{2,4},{4,6},{6,8},{8,10},{10,12},{12,14},{14,0},{1,3},{3,5},... | collective-permute-start | bytes 712712 | tf_op jit(solution)/shard_map/ppermute | solution.py:52
  76.2 29.5 %copy-start = (bf16[1,2048,224]{1,2,0:T(8,128)(2,1)S(1)}, bf16[1,2048,224]{1,2,0:T(8,128)(2,1)}, u32[]{:S(2)}) copy-start(bf16[1,2048,224]{1,2,0:T(8,128)(2,1)} %param.9) | copy-start | bytes 2752516
  76.2 15.5 %collective-permute-start.10 = (bf16[224,2048]{1,0:T(8,128)(2,1)}, bf16[224,2048]{1,0:T(8,128)(2,1)}, u32[]{:S(2)}, u32[]{:S(2)}) collective-permute-start(bf16[224,2048]{1,0:T(8,128)(2,1)} %copy-done.2), channel_id=1, source_target_pairs={{0,1},{1,0},{2,3},{3,2},{4,5},{5,4},{6,7},{7,6},{8,9},{9,8},{10,11... | collective-permute-start | bytes 2752520 | tf_op jit(solution)/shard_map/ppermute | solution.py:241
  87.3 18.4 %all-to-all-start.1 = ((bf16[8,128,256]{2,1,0:T(8,128)(2,1)}), bf16[8,128,256]{2,1,0:T(8,128)(2,1)S(1)}, u32[]{:S(2)}, u32[]{:S(2)}) async-start(bf16[8,128,256]{2,1,0:T(8,128)(2,1)} %hidden.1), calls=%async_computation.1 | async-start | bytes 1048576 | tf_op jit(solution)/shard_map/all_to_all | solution.py:242
  108.9 36.5 %copy-start.1 = (bf16[64,8]{1,0:T(8,128)(2,1)S(1)}, bf16[64,8]{1,0:T(8,128)(2,1)}, u32[]{:S(2)}) copy-start(bf16[64,8]{1,0:T(8,128)(2,1)} %get-tuple-element.20.place_ref) | copy-start | bytes 3076
